TPU v7x, 256 devices: a whole 4x4x8 slice. The times are simulated.
256 devices in a mesh: tile: 32 (over x_lo, z, core), src: 8 (over y, x_hi).
Axes of the slice: x: 4 (x_hi: 2, x_lo: 2; x = x_hi * 2 + x_lo), y: 4, z: 8, core: 2. Of those that a mesh axis runs over, the one named last changes fastest.
Arguments:
- mask: float32 [32, 512, 512], P('tile'), may hold values from 0 to 1.2, as said below
- target: int32 [32, 512, 512], P('tile'), may hold values 0 or 1
- shifts: int32 [64, 2], P('src'), may hold values from -32 to 32
- source_weights: float32 [64], P('src'), may hold values from 0.5 to 4
- pupil: int32 [128, 128], replicated, may hold values from 0 to 1, as said below
Outputs:
- new_mask: float32 [32, 512, 512], P('tile')
- new_weights: float32 [64], P('src')
- resist: float32 [32, 512, 512], P('tile')
Inputs may be any that keep to these rules, and one draw needn't show every extreme that they name: `mask`: non-negative transmissions. `pupil`: row i (frequency f_i = i - 64) is 1 where f_i^2 + f_j^2 <= R_i^2 and 0 elsewhere, with a radius R_i of 48 to 64 for each row.
All inputs are finite; a program needn't handle non-finite values. No bound on the sum of `target` on one device may be relied on, other than what follows from the above.
Results may differ from a plain program's by a relative error of at most 0.017.
The roundings to bfloat16 on the way count: a program that leaves them out, or rounds other values in their place, can miss the bound.
Values may be sent and summed in bfloat16 or wider, within the bound.
No kernel may reach another device: no remote copies, remote signals or barrier semaphores. Data moves between devices by JAX's collectives and lax.ppermute only.
A program may use at most 128 MiB of HBM per device.

v0:
```python
import math

import jax
import jax.numpy as jnp
from jax import lax
from jax.sharding import PartitionSpec as P

HALO = 64
SHIFT_MAX = 32
GRID_ROWS = 4


steepness = 10.0
threshold = 0.25
mask_rate = 0.5
source_rate = 8.0


def passed_along(block, axis, distance):
    devices = range(lax.axis_size(axis))
    route = [(i - distance, i) for i in devices if i - distance in devices]
    return lax.ppermute(block, axis, route)


def make_tables(tile_size, band_width):
    extent = tile_size + 2 * HALO
    spectrum_span = band_width + 2 * SHIFT_MAX
    freq_index = jnp.arange(spectrum_span, dtype=jnp.int32) - spectrum_span // 2
    positions = jnp.arange(extent, dtype=jnp.int32)
    phases = jnp.mod(freq_index[:, None] * positions[None, :], extent).astype(jnp.float32) * (
        2.0 * math.pi / extent
    )
    freq_re = (jnp.cos(phases) / extent).astype(jnp.bfloat16)
    freq_im = (-jnp.sin(phases) / extent).astype(jnp.bfloat16)
    band_index = jnp.arange(band_width, dtype=jnp.int32) - band_width // 2
    pixel_ext = jnp.arange(tile_size, dtype=jnp.int32) + HALO
    back_phase = jnp.mod(pixel_ext[:, None] * band_index[None, :], extent).astype(jnp.float32) * (
        2.0 * math.pi / extent
    )
    back_re = jnp.cos(back_phase).astype(jnp.bfloat16)
    back_im = jnp.sin(back_phase).astype(jnp.bfloat16)
    return (freq_re, freq_im, back_re, back_im)


def dot_nn(left, right):
    return jnp.dot(left, right, preferred_element_type=jnp.float32)


def dot_nt(left, right):
    return lax.dot_general(
        left, right, (((1,), (1,)), ((), ())), preferred_element_type=jnp.float32
    )


def dot_tn(left, right):
    return lax.dot_general(
        left, right, (((0,), (0,)), ((), ())), preferred_element_type=jnp.float32
    )


def spectrum_rows(ext_bf, freq_re, freq_im, rows_re, rows_im):
    prod_re = dot_nn(rows_re, ext_bf).astype(jnp.bfloat16)
    prod_im = dot_nn(rows_im, ext_bf).astype(jnp.bfloat16)
    spec_re = dot_nt(prod_re, freq_re) - dot_nt(prod_im, freq_im)
    spec_im = dot_nt(prod_re, freq_im) + dot_nt(prod_im, freq_re)
    return (spec_re, spec_im)


def source_field(spec_re, spec_im, source_shift, pupil_gain, left_re, left_im, back_re, back_im):
    band_width = pupil_gain.shape[0]
    offsets = SHIFT_MAX - source_shift
    win_re = (
        lax.dynamic_slice(spec_re, (offsets[0], offsets[1]), (band_width, band_width)) * pupil_gain
    ).astype(jnp.bfloat16)
    win_im = (
        lax.dynamic_slice(spec_im, (offsets[0], offsets[1]), (band_width, band_width)) * pupil_gain
    ).astype(jnp.bfloat16)
    amp_re = (dot_nn(left_re, win_re) - dot_nn(left_im, win_im)).astype(jnp.bfloat16)
    amp_im = (dot_nn(left_re, win_im) + dot_nn(left_im, win_re)).astype(jnp.bfloat16)
    field_re = dot_nt(amp_re, back_re) - dot_nt(amp_im, back_im)
    field_im = dot_nt(amp_re, back_im) + dot_nt(amp_im, back_re)
    return (field_re, field_im)


def source_adjoint(
    grad_re,
    grad_im,
    source_shift,
    coef_map,
    field_re,
    field_im,
    pupil_gain,
    left_re,
    left_im,
    back_re,
    back_im,
):
    band_width = pupil_gain.shape[0]
    dfield_re = (coef_map * field_re).astype(jnp.bfloat16)
    dfield_im = (coef_map * field_im).astype(jnp.bfloat16)
    damp_re = (dot_nn(dfield_re, back_re) + dot_nn(dfield_im, back_im)).astype(jnp.bfloat16)
    damp_im = (dot_nn(dfield_im, back_re) - dot_nn(dfield_re, back_im)).astype(jnp.bfloat16)
    dwin_re = (dot_tn(left_re, damp_re) + dot_tn(left_im, damp_im)) * pupil_gain
    dwin_im = (dot_tn(left_re, damp_im) - dot_tn(left_im, damp_re)) * pupil_gain
    offsets = SHIFT_MAX - source_shift
    corner = (offsets[0], offsets[1])
    grad_re = lax.dynamic_update_slice(
        grad_re, lax.dynamic_slice(grad_re, corner, (band_width, band_width)) + dwin_re, corner
    )
    grad_im = lax.dynamic_update_slice(
        grad_im, lax.dynamic_slice(grad_im, corner, (band_width, band_width)) + dwin_im, corner
    )
    return (grad_re, grad_im)


def mask_adjoint(grad_re, grad_im, freq_re, freq_im):
    highest = lax.Precision.HIGHEST
    wide_re = freq_re.astype(jnp.float32)
    wide_im = freq_im.astype(jnp.float32)
    dprod_re = jnp.dot(grad_re, wide_re, precision=highest) + jnp.dot(
        grad_im, wide_im, precision=highest
    )
    dprod_im = jnp.dot(grad_im, wide_re, precision=highest) - jnp.dot(
        grad_re, wide_im, precision=highest
    )
    first_term = lax.dot_general(wide_re, dprod_re, (((0,), (0,)), ((), ())), precision=highest)
    second_term = lax.dot_general(wide_im, dprod_im, (((0,), (0,)), ((), ())), precision=highest)
    return first_term + second_term


def take_rim(values, side, axis_dim):
    length = values.shape[axis_dim]
    if side < 0:
        return lax.slice_in_dim(values, length - HALO, length, 1, axis_dim)
    if side > 0:
        return lax.slice_in_dim(values, 0, HALO, 1, axis_dim)
    return values


def ext_band(values, side, axis_dim, tile_size):
    if side < 0:
        return lax.slice_in_dim(values, 0, HALO, 1, axis_dim)
    if side > 0:
        return lax.slice_in_dim(values, HALO + tile_size, 2 * HALO + tile_size, 1, axis_dim)
    return lax.slice_in_dim(values, HALO, HALO + tile_size, 1, axis_dim)


def landing_range(side, tile_size):
    if side < 0:
        return (tile_size - HALO, tile_size)
    if side > 0:
        return (0, HALO)
    return (0, tile_size)


def rim_fetch(rim_piece, offset):
    return passed_along(rim_piece, "tile", offset)


def rim_return(rim_piece, offset):
    return passed_along(rim_piece.astype(jnp.bfloat16), "tile", offset).astype(rim_piece.dtype)


def extend_tile(tile_bf, columns, column):
    strips = []
    for vertical in (-1, 0, 1):
        pieces_row = []
        for lateral in (-1, 0, 1):
            if vertical == 0 and lateral == 0:
                pieces_row.append(tile_bf)
            else:
                rim_piece = take_rim(take_rim(tile_bf, vertical, 0), lateral, 1)
                arrived = rim_fetch(rim_piece, -(vertical * columns + lateral))
                inside = (column + lateral >= 0) & (column + lateral < columns)
                pieces_row.append(jnp.where(inside, arrived, jnp.zeros_like(arrived)))
        strips.append(jnp.concatenate(pieces_row, axis=1))
    return jnp.concatenate(strips, axis=0)


def return_rims(ext_grad, columns, column, tile_size):
    tile_grad = ext_grad[HALO : HALO + tile_size, HALO : HALO + tile_size]
    for vertical in (-1, 0, 1):
        for lateral in (-1, 0, 1):
            if vertical != 0 or lateral != 0:
                rim_piece = ext_band(
                    ext_band(ext_grad, vertical, 0, tile_size), lateral, 1, tile_size
                )
                arrived = rim_return(rim_piece, vertical * columns + lateral)
                inside = (column - lateral >= 0) & (column - lateral < columns)
                arrived = jnp.where(inside, arrived, jnp.zeros_like(arrived))
                row_low, row_high = landing_range(vertical, tile_size)
                col_low, col_high = landing_range(lateral, tile_size)
                tile_grad = tile_grad.at[row_low:row_high, col_low:col_high].add(arrived)
    return tile_grad


def per_device(mask, target, shifts, source_weights, pupil):
    tile_size = mask.shape[1]
    band_width = pupil.shape[0]
    spectrum_span = band_width + 2 * SHIFT_MAX
    columns = lax.axis_size("tile") // GRID_ROWS
    column = lax.axis_index("tile") % columns
    own_count = shifts.shape[0]
    sources = own_count * lax.axis_size("src")
    freq_re, freq_im, back_re, back_im = make_tables(tile_size, band_width)
    pupil_gain = pupil.astype(jnp.float32)
    ext_bf = extend_tile(mask[0].astype(jnp.bfloat16), columns, column)
    spec_re, spec_im = spectrum_rows(ext_bf, freq_re, freq_im, freq_re, freq_im)
    target_rows = target[0]

    def forward(totals, source_item):
        source_shift, source_weight = source_item
        field_re, field_im = source_field(
            spec_re, spec_im, source_shift, pupil_gain, back_re, back_im, back_re, back_im
        )
        intensity = field_re * field_re + field_im * field_im
        return (totals + source_weight * intensity, (field_re, field_im))

    zero_image = jnp.zeros((back_re.shape[0], tile_size), jnp.float32)
    partial_image, (fields_re, fields_im) = lax.scan(forward, zero_image, (shifts, source_weights))
    aerial = lax.psum(partial_image.astype(jnp.bfloat16), "src").astype(jnp.float32) / sources
    resist_tile = jax.nn.sigmoid(steepness * (aerial - threshold))
    grad_img = (
        2.0
        * (resist_tile - target_rows.astype(jnp.float32))
        * resist_tile
        * (1.0 - resist_tile)
        * steepness
    )

    def backward(totals, source_item):
        source_shift, source_weight, field_re, field_im = source_item
        coef_map = 2.0 * source_weight / sources * grad_img
        grad_re, grad_im = source_adjoint(
            totals[0],
            totals[1],
            source_shift,
            coef_map,
            field_re,
            field_im,
            pupil_gain,
            back_re,
            back_im,
            back_re,
            back_im,
        )
        weight_term = jnp.sum(grad_img * (field_re * field_re + field_im * field_im))
        return ((grad_re, grad_im), weight_term)

    zero_spec = jnp.zeros((spectrum_span, spectrum_span), jnp.float32)
    (grad_re, grad_im), weight_terms = lax.scan(
        backward, (zero_spec, zero_spec), (shifts, source_weights, fields_re, fields_im)
    )
    weight_total = lax.psum(weight_terms, "tile")
    grad_re, grad_im = (
        lax.psum(grad_re.astype(jnp.bfloat16), "src").astype(jnp.float32),
        lax.psum(grad_im.astype(jnp.bfloat16), "src").astype(jnp.float32),
    )
    ext_grad = mask_adjoint(grad_re, grad_im, freq_re, freq_im)
    tile_grad = return_rims(ext_grad, columns, column, tile_size)
    new_mask = mask - mask_rate * tile_grad[None]
    pixel_count = tile_size * tile_size * lax.axis_size("tile")
    new_weights = source_weights - source_rate * weight_total / pixel_count
    return (new_mask, new_weights, resist_tile[None])


def solution(mesh):
    in_specs = (P("tile", None, None), P("tile", None, None), P("src", None), P("src"), P())
    out_specs = (P("tile", None, None), P("src"), P("tile", None, None))
    return jax.shard_map(
        per_device, mesh=mesh, in_specs=in_specs, out_specs=out_specs, check_vma=False
    )
```

profile of v0, /device:TPU:32, one launch (start us, length us, event | category | flops | bytes accessed | tf_op | source)
XLA Modules:
  0.0 703.5 jit_solution(10869570832613525158)
XLA Ops:
  8.7 1.9 collective-permute-start.4
  10.6 2.4 collective-permute-start.3
  14.4 9.0 %collective-permute-start.2 = (bf16[64,64]{1,0:T(8,128)(2,1)S(1)}, bf16[64,64]{1,0:T(8,128)(2,1)S(1)}, u32[]{:S(2)}, u32[]{:S(2)}) collective-permute-start(bf16[64,64]{1,0:T(8,128)(2,1)S(1)} %get-tuple-element.683), channel_id=1, source_target_pairs={{0,56},{8,64},{16,72},{24,80},{32,88},{40,96},{48,104},{56,112},{6... | collective-permute-start | bytes 24584 | tf_op jit(solution)/shard_map/ppermute | solution.py:22
  25.0 9.1 %collective-permute-start = (bf16[64,64]{1,0:T(8,128)(2,1)S(1)}, bf16[64,64]{1,0:T(8,128)(2,1)S(1)}, u32[]{:S(2)}, u32[]{:S(2)}) collective-permute-start(bf16[64,64]{1,0:T(8,128)(2,1)S(1)} %get-tuple-element.680), channel_id=1, source_target_pairs={{0,72},{8,80},{16,88},{24,96},{32,104},{40,112},{48,120},{56,128},... | collective-permute-start | bytes 24584 | tf_op jit(solution)/shard_map/ppermute | solution.py:22
  35.5 8.5 %collective-permute-start.1 = (bf16[64,512]{1,0:T(8,128)(2,1)S(1)}, bf16[64,512]{1,0:T(8,128)(2,1)S(1)}, u32[]{:S(2)}, u32[]{:S(2)}) collective-permute-start(bf16[64,512]{1,0:T(8,128)(2,1)S(1)} %get-tuple-element.684), channel_id=1, source_target_pairs={{0,64},{8,72},{16,80},{24,88},{32,96},{40,104},{48,112},{56,120},{... | collective-permute-start | bytes 196616 | tf_op jit(solution)/shard_map/ppermute | solution.py:22
  46.6 2.4 convolution_convert_fusion.1
  49.0 2.4 convolution_convert_fusion
  51.4 2.1 fusion.103
  53.5 2.1 fusion.102
  55.6 2.1 convolution_add_fusion.6
  57.7 2.1 convolution_subtract_fusion.5
  59.9 156.3 %while.46 = (s32[]{:T(128)}, f32[512,512]{1,0:T(8,128)S(1)}, f32[8,512,512]{2,1,0:T(8,128)}, f32[8,512,512]{2,1,0:T(8,128)}, f32[8]{0:T(128)}, /*index=5*/s32[8,...) while((s32[]{:T(128)}, f32[512,512]{1,0:T(8,128)S(1)}, ...), condition=%wide.region_1.2_spmd.clone.clone.clone.clone, body=%wide.region_0.1_spmd.clone.clone.clone.clone.sunk | while | flops 343212032 | bytes 16012771 | solution.py:220
  71.8 2.3 bitcast_dynamic-update-slice_fusion.5
  76.3 2.4 select_add_fusion.2
  91.3 2.3 bitcast_dynamic-update-slice_fusion.5
  95.8 2.4 select_add_fusion.2
  110.7 2.3 bitcast_dynamic-update-slice_fusion.5
  115.3 2.4 select_add_fusion.2
  130.2 2.3 bitcast_dynamic-update-slice_fusion.5
  134.7 2.4 select_add_fusion.2
  149.6 2.4 bitcast_dynamic-update-slice_fusion.5
  154.2 2.4 select_add_fusion.2
  169.1 2.3 bitcast_dynamic-update-slice_fusion.5
  173.7 2.4 select_add_fusion.2
  188.6 2.3 bitcast_dynamic-update-slice_fusion.5
  193.1 2.4 select_add_fusion.2
  208.0 2.4 bitcast_dynamic-update-slice_fusion.5
  212.7 2.4 select_add_fusion.2
  219.3 95.2 %all-reduce.4.cloned.1.call-done = bf16[512,512]{1,0:T(8,128)(2,1)} async-done(((bf16[512,512]{1,0:T(8,128)(2,1)}), bf16[512,512]{1,0:T(8,128)(2,1)}) %all-reduce.4.cloned.1.call-update) | async-done | bytes 524304 | tf_op jit(solution)/shard_map/psum | solution.py:221
  314.4 2.5 fusion.98
  317.0 177.8 %while.45 = (s32[]{:T(128)}, f32[192,192]{0,1:T(8,128)S(1)}, f32[192,192]{0,1:T(8,128)S(1)}, f32[8]{0:T(128)S(1)}, s32[8,2]{0,1:T(2,128)S(1)}, /*index=5*/f32[8]...) while((s32[]{:T(128)}, f32[192,192]{0,1:T(8,128)S(1)}, ...), condition=%wide.region_5.6_spmd.clone.clone.clone, body=%wide.region_3.5_spmd.clone.clone.clone.sunk | while | flops 343769088 | bytes 9064773 | solution.py:251
  318.3 2.5 fusion.231
  332.7 1.7 dynamic_update_slice.51
  340.5 2.5 fusion.231
  362.3 2.5 fusion.231
  384.2 2.5 fusion.231
  398.7 1.7 dynamic_update_slice.51
  402.9 1.7 dynamic_update_slice.50
  406.5 2.5 fusion.231
  428.7 2.5 fusion.231
  443.2 1.8 dynamic_update_slice.51
  447.4 1.8 dynamic_update_slice.50
  451.1 2.5 fusion.231
  465.6 1.8 dynamic_update_slice.51
  469.9 1.8 dynamic_update_slice.50
  473.6 2.5 fusion.231
  488.1 1.8 dynamic_update_slice.51
  492.3 1.8 dynamic_update_slice.50
  496.1 49.3 %psum.31 = f32[8]{0:T(128)S(1)} all-reduce(f32[8]{0:T(128)S(1)} %get-tuple-element.350), channel_id=1, replica_groups=mesh['tile'=32,'src'=8] {'tile'}, use_global_device_ids=true, to_apply=%region_10.11 | all-reduce | flops 8 | bytes 64 | tf_op jit(solution)/shard_map/psum | solution.py:254
  546.0 86.8 %all-reduce.6.cloned.1.call-done = (bf16[192,192]{0,1:T(8,128)(2,1)}, bf16[192,192]{0,1:T(8,128)(2,1)}) async-done(((bf16[192,192]{0,1:T(8,128)(2,1)}, bf16[192,192]{0,1:T(8,128)(2,1)}), (bf16[192,192]{0,1:T(8,128)(2,1)}, bf16[192,192]{0,1:T(8,128)(2,1)})) %all-reduce.6.cloned.1.call-update) | async-done | bytes 147472 | tf_op jit(solution)/shard_map/psum | solution.py:256
  632.7 3.0 fusion.99
  635.8 3.0 fusion.101
  638.8 2.1 convolution_subtract_fusion.4
  641.0 2.1 convolution_add_fusion.5
  643.1 2.9 fusion.100
  646.1 3.2 fusion.161
  653.8 1.9 collective-permute-start.11
  655.7 2.4 collective-permute-start.12
  658.5 9.3 %collective-permute-start.13 = (bf16[64,64]{1,0:T(8,128)(2,1)S(1)}, bf16[64,64]{1,0:T(8,128)(2,1)S(1)}, u32[]{:S(2)}, u32[]{:S(2)}) collective-permute-start(bf16[64,64]{1,0:T(8,128)(2,1)S(1)} %get-tuple-element.671), channel_id=1, source_target_pairs={{0,56},{8,64},{16,72},{24,80},{32,88},{40,96},{48,104},{56,112},{6... | collective-permute-start | bytes 24584 | tf_op jit(solution)/shard_map/ppermute | solution.py:22
  668.8 8.5 %collective-permute-start.14 = (bf16[64,512]{1,0:T(8,128)(2,1)S(1)}, bf16[64,512]{1,0:T(8,128)(2,1)S(1)}, u32[]{:S(2)}, u32[]{:S(2)}) collective-permute-start(bf16[64,512]{1,0:T(8,128)(2,1)S(1)} %get-tuple-element.674), channel_id=1, source_target_pairs={{0,64},{8,72},{16,80},{24,88},{32,96},{40,104},{48,112},{56,120},{... | collective-permute-start | bytes 196616 | tf_op jit(solution)/shard_map/ppermute | solution.py:22
  677.4 6.9 collective-permute-start.15
  687.4 1.9 scatter-add.34
  689.4 2.0 add_select_fusion.4
  691.4 2.4 scatter-add.35
  (331 shorter events, 220.0 us)
Async XLA Ops:
  7.2 17.6 %copy-start = (f32[1,512,512]{2,1,0:T(8,128)S(1)}, f32[1,512,512]{2,1,0:T(8,128)}, u32[]{:S(2)}) copy-start(f32[1,512,512]{2,1,0:T(8,128)} %param.25) | copy-start | bytes 3145732
  7.2 307.2 %all-reduce.4.cloned.1.call-start = ((), (), s32[]{:S(2)}) async-start(), calls=%async_computation | async-start | bytes 1048576 | tf_op jit(solution)/shard_map/psum | solution.py:221
  8.6 16.4 %copy-start.6 = (s32[128,128]{1,0:T(8,128)S(1)}, s32[128,128]{1,0:T(8,128)}, u32[]{:S(2)}) copy-start(s32[128,128]{1,0:T(8,128)} %param.29) | copy-start | bytes 196612
  8.7 35.3 %collective-permute-start.4 = (bf16[512,64]{1,0:T(8,128)(2,1)S(1)}, bf16[512,64]{1,0:T(8,128)(2,1)S(1)}, u32[]{:S(2)}, u32[]{:S(2)}) collective-permute-start(bf16[512,64]{1,0:T(8,128)(2,1)S(1)} %get-tuple-element.687), channel_id=1, source_target_pairs={{8,0},{16,8},{24,16},{32,24},{40,32},{48,40},{56,48},{64,56},{72,6... | collective-permute-start | bytes 196616 | tf_op jit(solution)/shard_map/ppermute | solution.py:22
  10.6 33.4 %collective-permute-start.3 = (bf16[512,64]{1,0:T(8,128)(2,1)S(1)}, bf16[512,64]{1,0:T(8,128)(2,1)S(1)}, u32[]{:S(2)}, u32[]{:S(2)}) collective-permute-start(bf16[512,64]{1,0:T(8,128)(2,1)S(1)} %get-tuple-element.686), channel_id=1, source_target_pairs={{0,8},{8,16},{16,24},{24,32},{32,40},{40,48},{48,56},{56,64},{64,7... | collective-permute-start | bytes 196616 | tf_op jit(solution)/shard_map/ppermute | solution.py:22
  13.1 11.9 %collective-permute-start.7 = (bf16[64,64]{1,0:T(8,128)(2,1)S(1)}, bf16[64,64]{1,0:T(8,128)(2,1)S(1)}, u32[]{:S(2)}, u32[]{:S(2)}) collective-permute-start(bf16[64,64]{1,0:T(8,128)(2,1)S(1)} %get-tuple-element.681), channel_id=1, source_target_pairs={{72,0},{80,8},{88,16},{96,24},{104,32},{112,40},{120,48},{128,56},... | collective-permute-start | bytes 24584 | tf_op jit(solution)/shard_map/ppermute | solution.py:22
  14.4 19.7 %collective-permute-start.2 = (bf16[64,64]{1,0:T(8,128)(2,1)S(1)}, bf16[64,64]{1,0:T(8,128)(2,1)S(1)}, u32[]{:S(2)}, u32[]{:S(2)}) collective-permute-start(bf16[64,64]{1,0:T(8,128)(2,1)S(1)} %get-tuple-element.683), channel_id=1, source_target_pairs={{0,56},{8,64},{16,72},{24,80},{32,88},{40,96},{48,104},{56,112},{6... | collective-permute-start | bytes 24584 | tf_op jit(solution)/shard_map/ppermute | solution.py:22
  23.5 12.0 %collective-permute-start.5 = (bf16[64,64]{1,0:T(8,128)(2,1)S(1)}, bf16[64,64]{1,0:T(8,128)(2,1)S(1)}, u32[]{:S(2)}, u32[]{:S(2)}) collective-permute-start(bf16[64,64]{1,0:T(8,128)(2,1)S(1)} %get-tuple-element.682), channel_id=1, source_target_pairs={{56,0},{64,8},{72,16},{80,24},{88,32},{96,40},{104,48},{112,56},{1... | collective-permute-start | bytes 24584 | tf_op jit(solution)/shard_map/ppermute | solution.py:22
  25.0 18.9 %collective-permute-start = (bf16[64,64]{1,0:T(8,128)(2,1)S(1)}, bf16[64,64]{1,0:T(8,128)(2,1)S(1)}, u32[]{:S(2)}, u32[]{:S(2)}) collective-permute-start(bf16[64,64]{1,0:T(8,128)(2,1)S(1)} %get-tuple-element.680), channel_id=1, source_target_pairs={{0,72},{8,80},{16,88},{24,96},{32,104},{40,112},{48,120},{56,128},... | collective-permute-start | bytes 24584 | tf_op jit(solution)/shard_map/ppermute | solution.py:22
  34.1 11.4 %collective-permute-start.6 = (bf16[64,512]{1,0:T(8,128)(2,1)S(1)}, bf16[64,512]{1,0:T(8,128)(2,1)S(1)}, u32[]{:S(2)}, u32[]{:S(2)}) collective-permute-start(bf16[64,512]{1,0:T(8,128)(2,1)S(1)} %get-tuple-element.685), channel_id=1, source_target_pairs={{64,0},{72,8},{80,16},{88,24},{96,32},{104,40},{112,48},{120,56},{... | collective-permute-start | bytes 196616 | tf_op jit(solution)/shard_map/ppermute | solution.py:22
  35.5 10.6 %collective-permute-start.1 = (bf16[64,512]{1,0:T(8,128)(2,1)S(1)}, bf16[64,512]{1,0:T(8,128)(2,1)S(1)}, u32[]{:S(2)}, u32[]{:S(2)}) collective-permute-start(bf16[64,512]{1,0:T(8,128)(2,1)S(1)} %get-tuple-element.684), channel_id=1, source_target_pairs={{0,64},{8,72},{16,80},{24,88},{32,96},{40,104},{48,112},{56,120},{... | collective-permute-start | bytes 196616 | tf_op jit(solution)/shard_map/ppermute | solution.py:22
  55.6 4.2 copy-start.5
  60.3 8.7 %copy-start.3 = (f32[192,192]{1,0:T(8,128)}, f32[192,192]{1,0:T(8,128)S(1)}, u32[]{:S(2)}) copy-start(f32[192,192]{1,0:T(8,128)S(1)} %get-tuple-element.892) | copy-start | bytes 442372 | tf_op jit(solution)/shard_map/while
  71.8 3.9 copy-start.9
  78.7 1.1 copy-start.4
  79.8 8.7 %copy-start.3 = (f32[192,192]{1,0:T(8,128)}, f32[192,192]{1,0:T(8,128)S(1)}, u32[]{:S(2)}) copy-start(f32[192,192]{1,0:T(8,128)S(1)} %get-tuple-element.892) | copy-start | bytes 442372 | tf_op jit(solution)/shard_map/while
  91.3 3.9 copy-start.9
  98.2 1.1 copy-start.4
  99.3 8.7 %copy-start.3 = (f32[192,192]{1,0:T(8,128)}, f32[192,192]{1,0:T(8,128)S(1)}, u32[]{:S(2)}) copy-start(f32[192,192]{1,0:T(8,128)S(1)} %get-tuple-element.892) | copy-start | bytes 442372 | tf_op jit(solution)/shard_map/while
  110.7 4.0 copy-start.9
  117.7 1.1 copy-start.4
  118.7 8.7 %copy-start.3 = (f32[192,192]{1,0:T(8,128)}, f32[192,192]{1,0:T(8,128)S(1)}, u32[]{:S(2)}) copy-start(f32[192,192]{1,0:T(8,128)S(1)} %get-tuple-element.892) | copy-start | bytes 442372 | tf_op jit(solution)/shard_map/while
  130.2 3.9 copy-start.9
  137.1 1.1 copy-start.4
  138.2 8.7 %copy-start.3 = (f32[192,192]{1,0:T(8,128)}, f32[192,192]{1,0:T(8,128)S(1)}, u32[]{:S(2)}) copy-start(f32[192,192]{1,0:T(8,128)S(1)} %get-tuple-element.892) | copy-start | bytes 442372 | tf_op jit(solution)/shard_map/while
  149.6 4.0 copy-start.9
  156.6 1.1 copy-start.4
  157.7 8.7 %copy-start.3 = (f32[192,192]{1,0:T(8,128)}, f32[192,192]{1,0:T(8,128)S(1)}, u32[]{:S(2)}) copy-start(f32[192,192]{1,0:T(8,128)S(1)} %get-tuple-element.892) | copy-start | bytes 442372 | tf_op jit(solution)/shard_map/while
  169.1 4.0 copy-start.9
  176.1 1.1 copy-start.4
  177.1 8.7 %copy-start.3 = (f32[192,192]{1,0:T(8,128)}, f32[192,192]{1,0:T(8,128)S(1)}, u32[]{:S(2)}) copy-start(f32[192,192]{1,0:T(8,128)S(1)} %get-tuple-element.892) | copy-start | bytes 442372 | tf_op jit(solution)/shard_map/while
  188.6 3.9 copy-start.9
  195.5 1.1 copy-start.4
  196.6 8.7 %copy-start.3 = (f32[192,192]{1,0:T(8,128)}, f32[192,192]{1,0:T(8,128)S(1)}, u32[]{:S(2)}) copy-start(f32[192,192]{1,0:T(8,128)S(1)} %get-tuple-element.892) | copy-start | bytes 442372 | tf_op jit(solution)/shard_map/while
  208.0 4.1 copy-start.9
  215.1 1.1 copy-start.4
  216.1 98.3 %copy-start.2 = (s32[1,512,512]{2,1,0:T(8,128)S(1)}, s32[1,512,512]{2,1,0:T(8,128)}, u32[]{:S(2)}) copy-start(s32[1,512,512]{2,1,0:T(8,128)} %param.26) | copy-start | bytes 3145732
  217.0 415.7 %all-reduce.6.cloned.1.call-start = ((), (), s32[]{:S(2)}) async-start(), calls=%async_computation.1 | async-start | bytes 393216 | tf_op jit(solution)/shard_map/psum | solution.py:256
  219.3 97.7 %copy-start.10 = (f32[8]{0:T(128)S(1)}, f32[8]{0:T(128)}, u32[]{:S(2)}) copy-start(f32[8]{0:T(128)} %get-tuple-element.998) | copy-start | bytes 100
  632.7 6.1 copy-start.8
  635.8 5.2 copy-start.7
  649.4 9.1 %collective-permute-start.8 = (bf16[64,64]{1,0:T(8,128)(2,1)S(1)}, bf16[64,64]{1,0:T(8,128)(2,1)S(1)}, u32[]{:S(2)}, u32[]{:S(2)}) collective-permute-start(bf16[64,64]{1,0:T(8,128)(2,1)S(1)} %get-tuple-element.673), channel_id=1, source_target_pairs={{72,0},{80,8},{88,16},{96,24},{104,32},{112,40},{120,48},{128,56},... | collective-permute-start | bytes 24584 | tf_op jit(solution)/shard_map/ppermute | solution.py:22
  651.2 17.6 %collective-permute-start.9 = (bf16[64,512]{1,0:T(8,128)(2,1)S(1)}, bf16[64,512]{1,0:T(8,128)(2,1)S(1)}, u32[]{:S(2)}, u32[]{:S(2)}) collective-permute-start(bf16[64,512]{1,0:T(8,128)(2,1)S(1)} %get-tuple-element.675), channel_id=1, source_target_pairs={{64,0},{72,8},{80,16},{88,24},{96,32},{104,40},{112,48},{120,56},{... | collective-permute-start | bytes 196616 | tf_op jit(solution)/shard_map/ppermute | solution.py:22
  652.5 24.9 %collective-permute-start.10 = (bf16[64,64]{1,0:T(8,128)(2,1)S(1)}, bf16[64,64]{1,0:T(8,128)(2,1)S(1)}, u32[]{:S(2)}, u32[]{:S(2)}) collective-permute-start(bf16[64,64]{1,0:T(8,128)(2,1)S(1)} %get-tuple-element.672), channel_id=1, source_target_pairs={{56,0},{64,8},{72,16},{80,24},{88,32},{96,40},{104,48},{112,56},{1... | collective-permute-start | bytes 24584 | tf_op jit(solution)/shard_map/ppermute | solution.py:22
  653.8 31.4 %collective-permute-start.11 = (bf16[512,64]{1,0:T(8,128)(2,1)S(1)}, bf16[512,64]{1,0:T(8,128)(2,1)S(1)}, u32[]{:S(2)}, u32[]{:S(2)}) collective-permute-start(bf16[512,64]{1,0:T(8,128)(2,1)S(1)} %get-tuple-element.677), channel_id=1, source_target_pairs={{8,0},{16,8},{24,16},{32,24},{40,32},{48,40},{56,48},{64,56},{72,6... | collective-permute-start | bytes 196616 | tf_op jit(solution)/shard_map/ppermute | solution.py:22
  655.7 31.1 %collective-permute-start.12 = (bf16[512,64]{1,0:T(8,128)(2,1)S(1)}, bf16[512,64]{1,0:T(8,128)(2,1)S(1)}, u32[]{:S(2)}, u32[]{:S(2)}) collective-permute-start(bf16[512,64]{1,0:T(8,128)(2,1)S(1)} %get-tuple-element.676), channel_id=1, source_target_pairs={{0,8},{8,16},{16,24},{24,32},{32,40},{40,48},{48,56},{56,64},{64,7... | collective-permute-start | bytes 196616 | tf_op jit(solution)/shard_map/ppermute | solution.py:22
  658.5 30.9 %collective-permute-start.13 = (bf16[64,64]{1,0:T(8,128)(2,1)S(1)}, bf16[64,64]{1,0:T(8,128)(2,1)S(1)}, u32[]{:S(2)}, u32[]{:S(2)}) collective-permute-start(bf16[64,64]{1,0:T(8,128)(2,1)S(1)} %get-tuple-element.671), channel_id=1, source_target_pairs={{0,56},{8,64},{16,72},{24,80},{32,88},{40,96},{48,104},{56,112},{6... | collective-permute-start | bytes 24584 | tf_op jit(solution)/shard_map/ppermute | solution.py:22
  668.8 25.0 %collective-permute-start.14 = (bf16[64,512]{1,0:T(8,128)(2,1)S(1)}, bf16[64,512]{1,0:T(8,128)(2,1)S(1)}, u32[]{:S(2)}, u32[]{:S(2)}) collective-permute-start(bf16[64,512]{1,0:T(8,128)(2,1)S(1)} %get-tuple-element.674), channel_id=1, source_target_pairs={{0,64},{8,72},{16,80},{24,88},{32,96},{40,104},{48,112},{56,120},{... | collective-permute-start | bytes 196616 | tf_op jit(solution)/shard_map/ppermute | solution.py:22
  677.4 16.4 %collective-permute-start.15 = (bf16[64,64]{1,0:T(8,128)(2,1)S(1)}, bf16[64,64]{1,0:T(8,128)(2,1)S(1)}, u32[]{:S(2)}, u32[]{:S(2)}) collective-permute-start(bf16[64,64]{1,0:T(8,128)(2,1)S(1)} %get-tuple-element.670), channel_id=1, source_target_pairs={{0,72},{8,80},{16,88},{24,96},{32,104},{40,112},{48,120},{56,128},... | collective-permute-start | bytes 24584 | tf_op jit(solution)/shard_map/ppermute | solution.py:22
  687.4 7.6 %copy-start.1 = (f32[1,512,512]{2,1,0:T(8,128)S(1)}, f32[1,512,512]{2,1,0:T(8,128)}, u32[]{:S(2)}) copy-start(f32[1,512,512]{2,1,0:T(8,128)} %param.25) | copy-start | bytes 3145732
Sparse Core Ops, SparseCore 0:
  217.1 97.2 all-reduce.3
  545.6 87.1 all-reduce.5
where the time goes:
time: 716 us; the launch traced here: 703 us
  matrix products  218 us (30%)
  waiting for transfers between devices  184 us (26%)
  local copies, waits for them, and re-layouts  68.9 us (10%)
  starting transfers between devices  67.8 us (9%)
  loops' own time  65.2 us (9%)
  blocking collectives  49.3 us (7%)
  other arithmetic  34.5 us (5%)
  between operations  15.2 us (2%)
    psum x1, waiting for transfers between devices, per_device(): lax.psum(partial_image.astype(jnp.bfloat16), 'src').astype(jnp.float32)  95.2 us
    dot_general x66, matrix products, dot_nn(): return jnp.dot(left, right, preferred_element_type=jnp.float32)  90.5 us
    psum x1, waiting for transfers between devices, per_device(): lax.psum(grad_re.astype(jnp.bfloat16), 'src').astype(jnp.float32)  86.8 us
    dot_general x36, matrix products, dot_nt(): lax.dot_general(left, right, (((1,), (1,)), ((), ())), preferred_element_...  72 us
    ppermute x16, starting transfers between devices, passed_along(): return lax.ppermute(block, axis, route)  67.8 us
    psum x1, blocking collectives, per_device(): weight_total = lax.psum(weight_terms, 'tile')  49.3 us
    dot_general x32, matrix products, dot_tn(): lax.dot_general(left, right, (((0,), (0,)), ((), ())), preferred_element_...  39.2 us
    another operation x1, loops' own time, per_device(): lax.scan(backward, (zero_spec, zero_spec), (shifts, source_weights, field...  34.8 us
  transfers between devices with their start and end apart: 18, of which 5 were waited for; matrix products, arithmetic and copies ran while one was open for 2% of the time, Pallas kernels for 0%

commit v1 on v0

v1 whole, which is shorter than its diff:
```python
import math

import jax
import jax.numpy as jnp
import ml_dtypes
import numpy as np
from jax import lax
from jax.experimental import pallas as pl
from jax.experimental.pallas import tpu as pltpu
from jax.sharding import PartitionSpec as P

TS = 512
HALO = 64
BAND = 128
SHIFT_MAX = 32
GRID_ROWS = 4
NE = TS + 2 * HALO
SPAN = BAND + 2 * SHIFT_MAX
HALF = 256
BATCH = 4

steepness = 10.0
threshold = 0.25
mask_rate = 0.5
source_rate = 8.0

BF = jnp.bfloat16
F32 = jnp.float32

ORDER = np.concatenate([np.arange(HALO, HALO + TS), np.arange(HALO), np.arange(HALO + TS, NE)])


def make_tables():
    freq_index = np.arange(SPAN) - SPAN // 2
    phases = np.mod(freq_index[:, None] * ORDER[None, :], NE) * (2.0 * math.pi / NE)
    freq_re, freq_im = np.cos(phases) / NE, -np.sin(phases) / NE
    band_index = np.arange(BAND) - BAND // 2
    back_phase = np.mod((np.arange(TS) + HALO)[:, None] * band_index[None, :], NE) * (2.0 * math.pi / NE)
    back_re, back_im = np.cos(back_phase), np.sin(back_phase)

    def bf(table):
        return np.ascontiguousarray(table).astype(np.float32).astype(ml_dtypes.bfloat16)

    freq = np.concatenate([freq_re, freq_im], 0)
    gap = np.zeros((NE, HALF - SPAN))
    to_re = np.concatenate([freq_re.T, gap, freq_im.T, gap], 1)
    to_im = np.concatenate([-freq_im.T, gap, freq_re.T, gap], 1)
    back_t = np.block([[back_re.T, back_im.T], [-back_im.T, back_re.T]])
    rows = np.concatenate([back_re, back_im], 1)
    return tuple(bf(t) for t in (freq, to_re, to_im, back_t, back_t.T, rows, freq.T))


def rows_t_table(blocks):
    rows = make_tables()[5]
    step = TS // blocks
    parts = [
        np.concatenate([rows[i * step : (i + 1) * step, :BAND].T, rows[i * step : (i + 1) * step, BAND:].T], 1)
        for i in range(blocks)
    ]
    return np.stack(parts)


def dot(left, right):
    return lax.dot_general(left, right, (((1,), (0,)), ((), ())), preferred_element_type=F32)


def dot_nt(left, right):
    return lax.dot_general(left, right, (((1,), (1,)), ((), ())), preferred_element_type=F32)


def source_kernel(
    place, shift, weight, mask, vert_1, vert_2, side_1, side_2, target, pupil,
    freq, to_re, to_im, back_t, back, rows, rows_t,
    dspec_out, resist_out, weight_out,
    spec, fields, image, dspec, terms, bits, sem,
):
    step = resist_out.shape[0]
    k, row_odd, col_odd = place[0], place[1] == 1, place[2] == 1
    fetch = pltpu.make_async_copy(target.at[0, pl.ds(pl.multiple_of(k * step, step), step), :], bits, sem)
    fetch.start()

    v1, v2 = vert_1[...].astype(F32), vert_2[...].astype(F32)
    halo_rows = jnp.concatenate([jnp.where(row_odd, v1, v2), jnp.where(row_odd, v2, v1)], 0).astype(BF)
    s1, s2 = side_1[...].astype(F32), side_2[...].astype(F32)
    left, right = jnp.where(col_odd, s1, s2), jnp.where(col_odd, s2, s1)
    first = lax.broadcasted_iota(jnp.int32, left.shape, 1) < HALO
    halo_cols = jnp.concatenate(
        [jnp.where(first, left, pltpu.roll(right, HALO, 1)), jnp.where(first, pltpu.roll(left, HALO, 1), right)], 0
    ).astype(BF)
    prod_mid = dot(freq[:, :TS], mask[0].astype(BF)) + dot(freq[:, TS:], halo_rows)
    prod_side = dot(freq[...], halo_cols)
    prod = jnp.concatenate([prod_mid, prod_side], 1).astype(BF)
    whole = dot(prod[:SPAN], to_re[...]) + dot(prod[SPAN:], to_im[...])
    for j in range(4):
        spec[j] = whole[:, j * 128 : (j + 1) * 128]

    gain = pupil[...].astype(F32)
    own_rows = rows[pl.ds(pl.multiple_of(k * step, step), step), :]
    sources = shift.shape[0] * BATCH * 2
    image[...] = jnp.zeros_like(image)
    dspec[...] = jnp.zeros_like(dspec)
    terms[...] = jnp.zeros_like(terms)

    def where_of(s):
        return SHIFT_MAX - shift[s // 8, s % 8], SHIFT_MAX - shift[s // 8, 8 + s % 8], weight[s // 8, s % 8]

    def forward(i, _):
        amps = []
        for u in range(BATCH):
            down, over, _w = where_of(i * BATCH + u)
            band = [spec[j, pl.ds(down, BAND), :] for j in range(4)]
            turn = lax.bitwise_and(HALF - over, HALF - 1)
            win_re = pltpu.roll(jnp.concatenate(band[:2], 1), turn, 1)[:, :BAND] * gain
            win_im = pltpu.roll(jnp.concatenate(band[2:], 1), turn, 1)[:, :BAND] * gain
            window = jnp.concatenate(
                [jnp.concatenate([win_re, win_im], 1), jnp.concatenate([-win_im, win_re], 1)], 0
            ).astype(BF)
            amps.append(dot(own_rows, window).astype(BF))
        field = dot(jnp.concatenate(amps, 0), back_t[...])
        fields[pl.ds(pl.multiple_of(i * (BATCH * step), BATCH * step), BATCH * step), :] = field
        total = image[...]
        for u in range(BATCH):
            _d, _o, w = where_of(i * BATCH + u)
            part = field[u * step : (u + 1) * step]
            total = total + w * (part[:, :TS] * part[:, :TS] + part[:, TS:] * part[:, TS:])
        image[...] = total
        return 0

    lax.fori_loop(0, sources // BATCH, forward, 0)

    fetch.wait()
    resist = jax.nn.sigmoid(steepness * (image[...] * (1.0 / sources) - threshold))
    resist_out[...] = resist.astype(BF)
    image[...] = 2.0 * (resist - bits[...].astype(F32)) * resist * (1.0 - resist) * steepness

    rows_turned = rows_t[k]

    def backward(i, _):
        dfields = []
        grad = image[...]
        for u in range(BATCH):
            s = i * BATCH + u
            _d, _o, w = where_of(s)
            at = pl.ds(pl.multiple_of(i * (BATCH * step) + u * step, step), step)
            field_re, field_im = fields[at, :TS], fields[at, TS:]
            term = jnp.sum(grad * (field_re * field_re + field_im * field_im), 0, keepdims=True)
            terms[pl.ds(s, 1), :] = term[:, :128] + term[:, 128:256] + term[:, 256:384] + term[:, 384:]
            coef = (2.0 * w / sources) * grad
            dfields.append(jnp.concatenate([coef * field_re, coef * field_im], 1).astype(BF))
        damp = dot(jnp.concatenate(dfields, 0), back[...])
        for u in range(BATCH):
            down, over, _w = where_of(i * BATCH + u)
            part = damp[u * step : (u + 1) * step]
            damp_re, damp_im = part[:, :BAND], part[:, BAND:]
            pair = jnp.concatenate(
                [jnp.concatenate([damp_re, damp_im], 1), jnp.concatenate([damp_im, -damp_re], 1)], 0
            ).astype(BF)
            dwin = dot(rows_turned, pair)
            empty = jnp.zeros((BAND, HALF - BAND), F32)
            dwin_re = pltpu.roll(jnp.concatenate([dwin[:, :BAND] * gain, empty], 1), over, 1)
            dwin_im = pltpu.roll(jnp.concatenate([dwin[:, BAND:] * gain, empty], 1), over, 1)
            for j, piece in enumerate((dwin_re[:, :128], dwin_re[:, 128:], dwin_im[:, :128], dwin_im[:, 128:])):
                dspec[j, pl.ds(down, BAND), :] += piece
        return 0

    lax.fori_loop(0, sources // BATCH, backward, 0)
    for j in range(4):
        dspec_out[:, j * 128 : (j + 1) * 128] = dspec[j].astype(BF)
    weight_out[...] = lax.dot_general(
        jnp.ones((8, 128), F32), terms[...], (((1,), (1,)), ((), ())),
        precision=lax.Precision.HIGHEST, preferred_element_type=F32,
    )


def split(values):
    high = values.astype(BF)
    return high, (values - high.astype(F32)).astype(BF)


def mask_kernel(place, mask, part_1, part_2, to_re, to_im, freq_t, base_out, vert_1, vert_2, sides_out):
    row_odd = place[1] == 1
    high, low = split(part_1[...].astype(F32) + part_2[...].astype(F32))
    both = jnp.concatenate([high, low], 0)
    prod_re, prod_im = dot_nt(both, to_re[...]), dot_nt(both, to_im[...])
    prod = jnp.concatenate([prod_re[:SPAN] + prod_re[SPAN:], prod_im[:SPAN] + prod_im[SPAN:]], 0)
    high, low = split(prod)
    ext = dot(freq_t[...], high) + dot(freq_t[...], low)
    base_out[...] = mask[0] - mask_rate * ext[:TS, :TS]
    sides_out[...] = ext[:TS, TS:]
    above, below = ext[TS : TS + HALO], ext[TS + HALO :]
    vert_1[...] = jnp.where(row_odd, above, below).astype(BF)
    vert_2[...] = jnp.where(row_odd, below, above).astype(BF)


def side_kernel(place, sides, got_1, got_2, side_1, side_2, work):
    row_odd, col_odd = place[1] == 1, place[2] == 1
    g1, g2 = got_1[:, TS:].astype(F32), got_2[:, TS:].astype(F32)
    work[...] = sides[...]
    work[:HALO] += jnp.where(row_odd, g1, g2)
    work[TS - HALO :] += jnp.where(row_odd, g2, g1)
    upper, lower = work[: TS // 2], work[TS // 2 :]
    first = lax.broadcasted_iota(jnp.int32, upper.shape, 1) < HALO
    left = jnp.where(first, upper, pltpu.roll(lower, HALO, 1))
    right = jnp.where(first, pltpu.roll(upper, HALO, 1), lower)
    side_1[...] = jnp.where(col_odd, left, right).astype(BF)
    side_2[...] = jnp.where(col_odd, right, left).astype(BF)


def final_kernel(place, base, got_1, got_2, side_1, side_2, *rest):
    pieces, (mask_out, resist_out) = rest[:-2], rest[-2:]
    k, row_odd, col_odd = place[0], place[1] == 1, place[2] == 1
    step = pieces[0].shape[0]
    for m, piece in enumerate(pieces):
        at = lax.bitwise_xor(k, m)
        resist_out[0, pl.ds(pl.multiple_of(at * step, step), step), :] = piece[...].astype(F32)
    g1, g2 = got_1[:, :TS].astype(F32), got_2[:, :TS].astype(F32)
    mask_out[0] = base[...]
    mask_out[0, :HALO, :] -= mask_rate * jnp.where(row_odd, g1, g2)
    mask_out[0, TS - HALO :, :] -= mask_rate * jnp.where(row_odd, g2, g1)
    s1, s2 = side_1[...].astype(F32), side_2[...].astype(F32)
    left, right = jnp.where(col_odd, s1, s2), jnp.where(col_odd, s2, s1)
    first = lax.broadcasted_iota(jnp.int32, left.shape, 1) < HALO
    half = TS // 2
    mask_out[0, :half, :128] -= mask_rate * jnp.where(first, left, 0.0)
    mask_out[0, half:, :128] -= mask_rate * jnp.where(first, pltpu.roll(left, HALO, 1), 0.0)
    mask_out[0, :half, TS - 128 :] -= mask_rate * jnp.where(first, 0.0, pltpu.roll(right, HALO, 1))
    mask_out[0, half:, TS - 128 :] -= mask_rate * jnp.where(first, 0.0, right)


SMEM = pl.BlockSpec(memory_space=pltpu.SMEM)
VMEM = pl.BlockSpec(memory_space=pltpu.VMEM)
HBM = pl.BlockSpec(memory_space=pl.ANY)


def shaped(shape, dtype):
    return jax.ShapeDtypeStruct(shape, dtype)


def grid_routes(tiles, columns):
    row_swap = [(t, t ^ columns) for t in range(tiles)]
    row_next = [(t, t + columns) for t in range(tiles) if (t // columns) % 2 == 1 and t + columns < tiles]
    col_swap = [(t, t ^ 1) for t in range(tiles)]
    col_next = [(t, t + 1) for t in range(tiles) if t % 2 == 1 and (t + 1) % columns != 0]
    back = lambda route: route + [(b, a) for a, b in route]
    return row_swap, back(row_next), col_swap, back(col_next)


def src_swap(block, distance, count):
    return lax.ppermute(block, "src", [(i, i ^ distance) for i in range(count)])


def tile_swap(block, distance, count):
    return lax.ppermute(block, "tile", [(i, i ^ distance) for i in range(count)])


def per_device(mask, target, shifts, source_weights, pupil):
    tiles, groups = lax.axis_size("tile"), lax.axis_size("src")
    columns = tiles // GRID_ROWS
    tile, k = lax.axis_index("tile"), lax.axis_index("src")
    row_odd, col_odd = (tile // columns) % 2 == 1, tile % 2 == 1
    place = jnp.stack([k, row_odd.astype(jnp.int32), col_odd.astype(jnp.int32)]).astype(jnp.int32)
    row_swap, row_next, col_swap, col_next = grid_routes(tiles, columns)
    freq, to_re, to_im, back_t, back, rows, freq_t = (jnp.asarray(t) for t in make_tables())
    rows_t = jnp.asarray(rows_t_table(groups))
    own = shifts.shape[0]
    step = TS // groups

    line = jnp.concatenate([shifts[:, 0].astype(F32), shifts[:, 1].astype(F32), source_weights])
    line = jnp.pad(line, (0, 128 - line.shape[0]))
    info = jnp.where(jnp.arange(groups)[:, None] == k, line[None, :], 0.0)
    for distance in (1, 2, 4):
        info = info + src_swap(info, distance, groups)
    all_shifts = info[:, : 2 * own].astype(jnp.int32)
    all_weights = info[:, 2 * own : 3 * own]

    top, bottom = mask[0, :HALO].astype(BF), mask[0, TS - HALO :].astype(BF)
    vert_1 = lax.ppermute(jnp.where(row_odd, top, bottom), "tile", row_swap)
    vert_2 = lax.ppermute(jnp.where(row_odd, bottom, top), "tile", row_next)
    above, below = jnp.where(row_odd, vert_1, vert_2), jnp.where(row_odd, vert_2, vert_1)

    def packed(cols):
        edge = jnp.concatenate([mask[0][:, cols].astype(BF), above[:, cols], below[:, cols]], 0)
        return jnp.concatenate([edge[: NE // 2], edge[NE // 2 :]], 1)

    left, right = packed(slice(0, HALO)), packed(slice(TS - HALO, TS))
    side_1 = lax.ppermute(jnp.where(col_odd, left, right), "tile", col_swap)
    side_2 = lax.ppermute(jnp.where(col_odd, right, left), "tile", col_next)

    dspec, resist, terms = pl.pallas_call(
        source_kernel,
        out_shape=(shaped((SPAN, 2 * HALF), BF), shaped((step, TS), BF), shaped((8, 128), F32)),
        in_specs=[SMEM] * 3 + [VMEM] * 5 + [HBM] + [VMEM] * 8,
        out_specs=(VMEM, VMEM, VMEM),
        scratch_shapes=[
            pltpu.VMEM((4, SPAN, 128), F32),
            pltpu.VMEM((groups * own * step, 2 * TS), F32),
            pltpu.VMEM((step, TS), F32),
            pltpu.VMEM((4, SPAN, 128), F32),
            pltpu.VMEM((128, 128), F32),
            pltpu.VMEM((step, TS), jnp.int32),
            pltpu.SemaphoreType.DMA,
        ],
        compiler_params=pltpu.CompilerParams(vmem_limit_bytes=48 << 20),
        name="sources",
    )(
        place, all_shifts, all_weights, mask, vert_1, vert_2, side_1, side_2, target, pupil,
        freq, to_re, to_im, back_t, back, rows, rows_t,
    )

    pieces = [resist] + [src_swap(resist, m, groups) for m in range(1, groups)]
    part = dspec
    for distance in (2, 4, 1):
        other = src_swap(part, distance, groups)
        if distance != 1:
            part = (part.astype(F32) + other.astype(F32)).astype(BF)
    base, rim_1, rim_2, sides = pl.pallas_call(
        mask_kernel,
        out_shape=(
            shaped((TS, TS), F32), shaped((HALO, NE), BF), shaped((HALO, NE), BF), shaped((TS, 2 * HALO), F32),
        ),
        in_specs=[SMEM] + [VMEM] * 6,
        out_specs=(VMEM,) * 4,
        compiler_params=pltpu.CompilerParams(vmem_limit_bytes=40 << 20),
        name="mask_gradient",
    )(place, mask, part, other, to_re, to_im, freq_t)

    got_1 = lax.ppermute(rim_1, "tile", row_swap)
    got_2 = lax.ppermute(rim_2, "tile", row_next)
    send_1, send_2 = pl.pallas_call(
        side_kernel,
        out_shape=(shaped((TS // 2, 128), BF),) * 2,
        in_specs=[SMEM] + [VMEM] * 3,
        out_specs=(VMEM,) * 2,
        scratch_shapes=[pltpu.VMEM((TS, 2 * HALO), F32)],
        name="side_rims",
    )(place, sides, got_1, got_2)
    back_1 = lax.ppermute(send_1, "tile", col_swap)
    back_2 = lax.ppermute(send_2, "tile", col_next)
    new_mask, resist_tile = pl.pallas_call(
        final_kernel,
        out_shape=(shaped((1, TS, TS), F32),) * 2,
        in_specs=[SMEM] + [VMEM] * (5 + groups),
        out_specs=(VMEM,) * 2,
        compiler_params=pltpu.CompilerParams(vmem_limit_bytes=32 << 20),
        name="new_mask",
    )(place, base, got_1, got_2, back_1, back_2, *pieces)

    for distance in (1, 2, 4):
        terms = terms + src_swap(terms, distance, groups)
    for distance in (1, 2, 4, 8, 16):
        terms = terms + tile_swap(terms, distance, tiles)
    weight_total = lax.dynamic_slice(terms, (0, k * own), (1, own))[0]
    new_weights = source_weights - source_rate * weight_total / (TS * TS * tiles)
    return (new_mask, new_weights, resist_tile)


def solution(mesh):
    in_specs = (P("tile", None, None), P("tile", None, None), P("src", None), P("src"), P())
    out_specs = (P("tile", None, None), P("src"), P("tile", None, None))
    return jax.shard_map(
        per_device, mesh=mesh, in_specs=in_specs, out_specs=out_specs, check_vma=False
    )
```

time: 716 us -> 159 us (0.22)
  the two profiles are of different devices: /device:TPU:32 before, /device:TPU:1 now
where the time goes in v1:
time: 159 us
  starting transfers between devices  75.1 us (47%)
  waiting for transfers between devices  35.3 us (22%)
  Pallas kernels  31.8 us (20%)
  local copies, waits for them, and re-layouts  9.27 us (6%)
  other arithmetic  6.3 us (4%)
    ppermute x16, starting transfers between devices, src_swap(): return lax.ppermute(block, 'src', [(i, i ^ distance) for i in range(count)])  30.3 us
    pallas_call x1, Pallas kernels, per_device(): pl.pallas_call(source_kernel, out_shape=(shaped((SPAN, 2 * HALF), BF), sh...  25.2 us
    ppermute x16, waiting for transfers between devices, src_swap(): return lax.ppermute(block, 'src', [(i, i ^ distance) for i in range(count)])  23.1 us
    ppermute x5, starting transfers between devices, tile_swap(): lax.ppermute(block, 'tile', [(i, i ^ distance) for i in range(count)])  20.7 us
    ppermute x1, starting transfers between devices, per_device(): vert_1 = lax.ppermute(jnp.where(row_odd, top, bottom), 'tile', row_swap)  8.25 us
    unnamed x38, local copies, waits for them, and re-layouts  7.6 us
    ppermute x5, waiting for transfers between devices, tile_swap(): lax.ppermute(block, 'tile', [(i, i ^ distance) for i in range(count)])  7.16 us
    ppermute x1, starting transfers between devices, per_device(): side_2 = lax.ppermute(jnp.where(col_odd, right, left), 'tile', col_next)  6.07 us
  transfers between devices with their start and end apart: 29, of which 14 were waited for; matrix products, arithmetic and copies ran while one was open for 3% of the time, Pallas kernels for 1%

profile of v1, /device:TPU:1, one launch (start us, length us, event | category | flops | bytes accessed | tf_op | source)
XLA Modules:
  0.0 158.6 jit_solution(6682047645106940279)
XLA Ops:
  0.7 0.8 convert_bitcast_fusion.1
  1.4 0.7 select_maximum_fusion
  2.3 3.6 %collective-permute-start = (f32[8,128]{1,0:T(8,128)S(1)}, f32[8,128]{1,0:T(8,128)S(1)}, u32[]{:S(2)}, u32[]{:S(2)}) collective-permute-start(f32[8,128]{1,0:T(8,128)S(1)} %broadcast_select_fusion.4), channel_id=1, source_target_pairs={{0,1},{1,0},{2,3},{3,2},{4,5},{5,4},{6,7},{7,6},{8,9},{9,8},{10,11... | collective-permute-start | bytes 12296 | tf_op jit(solution)/shard_map/ppermute | solution.py:249
  5.8 1.3 convert.10
  7.1 0.7 select_bitcast_fusion
  7.8 0.7 collective-permute-start.4
  8.4 8.3 %collective-permute-start.3 = (bf16[64,512]{1,0:T(8,128)(2,1)}, bf16[64,512]{1,0:T(8,128)(2,1)S(1)}, u32[]{:S(2)}, u32[]{:S(2)}) collective-permute-start(bf16[64,512]{1,0:T(8,128)(2,1)} %get-tuple-element.30), channel_id=1, source_target_pairs={{0,64},{8,72},{16,80},{24,88},{32,96},{40,104},{48,112},{56,120},{... | collective-permute-start | bytes 196616 | tf_op jit(solution)/shard_map/ppermute | solution.py:277
  16.8 0.8 fusion.4
  17.5 0.7 fusion.2
  18.2 1.3 collective-permute-start.1
  19.5 0.7 fusion.3
  20.2 0.6 collective-permute-done.1
  20.9 2.9 %collective-permute-start.2 = (f32[8,128]{1,0:T(8,128)S(1)}, f32[8,128]{1,0:T(8,128)S(1)}, u32[]{:S(2)}, u32[]{:S(2)}) collective-permute-start(f32[8,128]{1,0:T(8,128)S(1)} %fusion.7), channel_id=1, source_target_pairs={{0,4},{1,5},{2,6},{3,7},{4,0},{5,1},{6,2},{7,3},{8,12},{9,13},{10,... | collective-permute-start | bytes 12296 | tf_op jit(solution)/shard_map/ppermute | solution.py:249
  23.9 1.0 collective-permute-done.2
  24.9 0.1 fusion.5
  25.0 1.1 broadcast_select_fusion
  26.2 6.1 %collective-permute-start.6 = (bf16[320,128]{1,0:T(8,128)(2,1)S(1)}, bf16[320,128]{1,0:T(8,128)(2,1)S(1)}, u32[]{:S(2)}, u32[]{:S(2)}) collective-permute-start(bf16[320,128]{1,0:T(8,128)(2,1)S(1)} %get-tuple-element.31), channel_id=1, source_target_pairs={{8,16},{24,32},{40,48},{72,80},{88,96},{104,112},{136,144},{152,16... | collective-permute-start | bytes 245768 | tf_op jit(solution)/shard_map/ppermute | solution.py:287
  32.2 0.1 collective-permute-start.5
  32.4 1.9 %collective-permute-done.6.side_2 = bf16[320,128]{1,0:T(8,128)(2,1)S(1)} collective-permute-done((bf16[320,128]{1,0:T(8,128)(2,1)S(1)}, bf16[320,128]{1,0:T(8,128)(2,1)S(1)}, u32[]{:S(2)}, u32[]{:S(2)}) %collective-permute-start.6) | collective-permute-done | bytes 81952 | tf_op jit(solution)/shard_map/ppermute | solution.py:287
  34.4 1.0 copy-done.4
  35.4 1.0 copy-done.5
  36.5 1.0 copy-done.7
  37.5 0.9 copy-done.12
  38.5 0.9 copy-done.13
  39.4 25.2 %sources.1 = (bf16[192,512]{1,0:T(8,128)(2,1)S(1)}, bf16[64,512]{1,0:T(8,128)(2,1)}, f32[8,128]{1,0:T(8,128)S(1)}) custom-call(s32[3]{0:T(128)S(1)} %pad_add_fusion.place, s32[8,16]{1,0:T(8,128)S(1)} %slice_convert_fusion.shift, f32[8,8]{1,0:T(8,128)S(1)} %slice.57.weight, f32[1,512,512]{2,1,0:T(8,128)S(1)} %copy-done, ...), custom_call_target="tpu_custom_call" | custom-call | tf_op jit(solution)/shard_map/sources/pallas_call | solution.py:289
  64.6 1.4 collective-permute-start.7
  66.0 5.3 %collective-permute-done.7 = bf16[192,512]{1,0:T(8,128)(2,1)S(1)} collective-permute-done((bf16[192,512]{1,0:T(8,128)(2,1)S(1)}, bf16[192,512]{1,0:T(8,128)(2,1)S(1)}, u32[]{:S(2)}, u32[]{:S(2)}) %collective-permute-start.7) | collective-permute-done | bytes 196640 | tf_op jit(solution)/shard_map/ppermute | solution.py:249
  71.4 3.0 %collective-permute-start.8 = (bf16[192,512]{1,0:T(8,128)(2,1)S(1)}, bf16[192,512]{1,0:T(8,128)(2,1)S(1)}, u32[]{:S(2)}, u32[]{:S(2)}) collective-permute-start(bf16[192,512]{1,0:T(8,128)(2,1)S(1)} %add_convert_fusion.1), channel_id=1, source_target_pairs={{0,4},{1,5},{2,6},{3,7},{4,0},{5,1},{6,2},{7,3},{8,12},{9,13},{10,... | collective-permute-start | bytes 589832 | tf_op jit(solution)/shard_map/ppermute | solution.py:249
  74.4 4.7 %collective-permute-done.8 = bf16[192,512]{1,0:T(8,128)(2,1)S(1)} collective-permute-done((bf16[192,512]{1,0:T(8,128)(2,1)S(1)}, bf16[192,512]{1,0:T(8,128)(2,1)S(1)}, u32[]{:S(2)}, u32[]{:S(2)}) %collective-permute-start.8) | collective-permute-done | bytes 196640 | tf_op jit(solution)/shard_map/ppermute | solution.py:249
  79.2 1.5 collective-permute-start.9
  80.6 5.3 %collective-permute-done.9.part_2 = bf16[192,512]{1,0:T(8,128)(2,1)S(1)} collective-permute-done((bf16[192,512]{1,0:T(8,128)(2,1)S(1)}, bf16[192,512]{1,0:T(8,128)(2,1)S(1)}, u32[]{:S(2)}, u32[]{:S(2)}) %collective-permute-start.9) | collective-permute-done | bytes 196640 | tf_op jit(solution)/shard_map/ppermute | solution.py:249
  85.9 2.4 %mask_gradient.1 = (f32[512,512]{1,0:T(8,128)S(1)}, bf16[64,640]{1,0:T(8,128)(2,1)S(1)}, bf16[64,640]{1,0:T(8,128)(2,1)S(1)}, f32[512,128]{1,0:T(8,128)S(1)}) custom-call(s32[3]{0:T(128)S(1)} %pad_add_fusion.place, f32[1,512,512]{2,1,0:T(8,128)S(1)} %copy-done, bf16[192,512]{1,0:T(8,128)(2,1)S(1)} %add_convert_fusion.part_1, ...), custom_call_target="tpu_custom_call" | custom-call | tf_op jit(solution)/shard_map/mask_gradient/pallas_call | solution.py:316
  88.3 0.7 copy-done.14
  89.0 1.2 collective-permute-start.10
  90.2 0.2 collective-permute-start.21
  90.4 3.7 %collective-permute-done.21 = f32[8,128]{1,0:T(8,128)S(1)} collective-permute-done((f32[8,128]{1,0:T(8,128)S(1)}, f32[8,128]{1,0:T(8,128)S(1)}, u32[]{:S(2)}, u32[]{:S(2)}) %collective-permute-start.21) | collective-permute-done | bytes 4128 | tf_op jit(solution)/shard_map/ppermute | solution.py:249
  94.2 1.3 collective-permute-start.22
  95.5 1.5 collective-permute-done.22
  96.9 2.9 %collective-permute-start.23 = (f32[8,128]{1,0:T(8,128)S(1)}, f32[8,128]{1,0:T(8,128)S(1)}, u32[]{:S(2)}, u32[]{:S(2)}) collective-permute-start(f32[8,128]{1,0:T(8,128)S(1)} %add.60), channel_id=1, source_target_pairs={{0,4},{1,5},{2,6},{3,7},{4,0},{5,1},{6,2},{7,3},{8,12},{9,13},{10,... | collective-permute-start | bytes 12296 | tf_op jit(solution)/shard_map/ppermute | solution.py:249
  99.8 1.0 collective-permute-done.23
  100.9 5.6 %collective-permute-start.24 = (f32[8,128]{1,0:T(8,128)S(1)}, f32[8,128]{1,0:T(8,128)S(1)}, u32[]{:S(2)}, u32[]{:S(2)}) collective-permute-start(f32[8,128]{1,0:T(8,128)S(1)} %add.61), channel_id=1, source_target_pairs={{0,8},{8,0},{16,24},{24,16},{32,40},{40,32},{48,56},{56,48},{64,72... | collective-permute-start | bytes 12296 | tf_op jit(solution)/shard_map/ppermute | solution.py:253
  106.5 0.8 collective-permute-done.24
  107.3 0.7 collective-permute-start.11
  108.0 0.3 collective-permute-start.25
  108.2 2.4 %collective-permute-done.25 = f32[8,128]{1,0:T(8,128)S(1)} collective-permute-done((f32[8,128]{1,0:T(8,128)S(1)}, f32[8,128]{1,0:T(8,128)S(1)}, u32[]{:S(2)}, u32[]{:S(2)}) %collective-permute-start.25) | collective-permute-done | bytes 4128 | tf_op jit(solution)/shard_map/ppermute | solution.py:253
  110.7 0.5 collective-permute-start.26
  111.2 2.9 %collective-permute-done.26 = f32[8,128]{1,0:T(8,128)S(1)} collective-permute-done((f32[8,128]{1,0:T(8,128)S(1)}, f32[8,128]{1,0:T(8,128)S(1)}, u32[]{:S(2)}, u32[]{:S(2)}) %collective-permute-start.26) | collective-permute-done | bytes 4128 | tf_op jit(solution)/shard_map/ppermute | solution.py:253
  114.0 12.7 %collective-permute-start.27 = (f32[8,128]{1,0:T(8,128)S(1)}, f32[8,128]{1,0:T(8,128)S(1)}, u32[]{:S(2)}, u32[]{:S(2)}) collective-permute-start(f32[8,128]{1,0:T(8,128)S(1)} %add.64), channel_id=1, source_target_pairs={{0,64},{8,72},{16,80},{24,88},{32,96},{40,104},{48,112},{56,120},{... | collective-permute-start | bytes 12296 | tf_op jit(solution)/shard_map/ppermute | solution.py:253
  126.7 1.0 collective-permute-done.27
  127.7 1.6 %collective-permute-start.28 = (f32[8,128]{1,0:T(8,128)S(1)}, f32[8,128]{1,0:T(8,128)S(1)}, u32[]{:S(2)}, u32[]{:S(2)}) collective-permute-start(f32[8,128]{1,0:T(8,128)S(1)} %add.65), channel_id=1, source_target_pairs={{0,128},{8,136},{16,144},{24,152},{32,160},{40,168},{48,176},{56,1... | collective-permute-start | bytes 12296 | tf_op jit(solution)/shard_map/ppermute | solution.py:253
  129.4 2.8 %collective-permute-start.20 = (bf16[64,512]{1,0:T(8,128)(2,1)}, bf16[64,512]{1,0:T(8,128)(2,1)S(1)}, u32[]{:S(2)}, u32[]{:S(2)}) collective-permute-start(bf16[64,512]{1,0:T(8,128)(2,1)} %get-tuple-element.21.rest_0_), channel_id=1, source_target_pairs={{0,7},{1,6},{2,5},{3,4},{4,3},{5,2},{6,1},{7,0},{8,15},{9,14},{10,... | collective-permute-start | bytes 196616 | tf_op jit(solution)/shard_map/ppermute | solution.py:249
  132.2 2.5 %collective-permute-start.18 = (bf16[64,512]{1,0:T(8,128)(2,1)}, bf16[64,512]{1,0:T(8,128)(2,1)S(1)}, u32[]{:S(2)}, u32[]{:S(2)}) collective-permute-start(bf16[64,512]{1,0:T(8,128)(2,1)} %get-tuple-element.21.rest_0_), channel_id=1, source_target_pairs={{0,5},{1,4},{2,7},{3,6},{4,1},{5,0},{6,3},{7,2},{8,13},{9,12},{10,... | collective-permute-start | bytes 196616 | tf_op jit(solution)/shard_map/ppermute | solution.py:249
  134.7 2.7 %collective-permute-start.17 = (bf16[64,512]{1,0:T(8,128)(2,1)}, bf16[64,512]{1,0:T(8,128)(2,1)S(1)}, u32[]{:S(2)}, u32[]{:S(2)}) collective-permute-start(bf16[64,512]{1,0:T(8,128)(2,1)} %get-tuple-element.21.rest_0_), channel_id=1, source_target_pairs={{0,4},{1,5},{2,6},{3,7},{4,0},{5,1},{6,2},{7,3},{8,12},{9,13},{10,... | collective-permute-start | bytes 196616 | tf_op jit(solution)/shard_map/ppermute | solution.py:249
  137.4 0.6 collective-permute-start.16
  138.1 1.8 %side_rims.1 = (bf16[256,128]{1,0:T(8,128)(2,1)}, bf16[256,128]{1,0:T(8,128)(2,1)}) custom-call(s32[3]{0:T(128)} %copy-done.16, f32[512,128]{1,0:T(8,128)} %copy-done.14, bf16[64,640]{1,0:T(8,128)(2,1)} %copy-done.8, bf16[64,640]{1,0:T(8,128)(2,1)} %copy-done.10), custom_call_target="tpu_custom_call" | custom-call | tf_op jit(solution)/shard_map/side_rims/pallas_call | solution.py:329
  139.9 1.1 collective-permute-start.15
  140.9 2.5 %collective-permute-start.14 = (bf16[64,512]{1,0:T(8,128)(2,1)}, bf16[64,512]{1,0:T(8,128)(2,1)S(1)}, u32[]{:S(2)}, u32[]{:S(2)}) collective-permute-start(bf16[64,512]{1,0:T(8,128)(2,1)} %get-tuple-element.21.rest_0_), channel_id=1, source_target_pairs={{0,1},{1,0},{2,3},{3,2},{4,5},{5,4},{6,7},{7,6},{8,9},{9,8},{10,11... | collective-permute-start | bytes 196616 | tf_op jit(solution)/shard_map/ppermute | solution.py:249
  143.5 5.2 %collective-permute-start.12 = (bf16[256,128]{1,0:T(8,128)(2,1)}, bf16[256,128]{1,0:T(8,128)(2,1)S(1)}, u32[]{:S(2)}, u32[]{:S(2)}) collective-permute-start(bf16[256,128]{1,0:T(8,128)(2,1)} %get-tuple-element.19), channel_id=1, source_target_pairs={{0,8},{8,0},{16,24},{24,16},{32,40},{40,32},{48,56},{56,48},{64,72... | collective-permute-start | bytes 196616 | tf_op jit(solution)/shard_map/ppermute | solution.py:337
  148.7 2.0 %collective-permute-start.13 = (bf16[256,128]{1,0:T(8,128)(2,1)}, bf16[256,128]{1,0:T(8,128)(2,1)S(1)}, u32[]{:S(2)}, u32[]{:S(2)}) collective-permute-start(bf16[256,128]{1,0:T(8,128)(2,1)} %get-tuple-element.20), channel_id=1, source_target_pairs={{8,16},{24,32},{40,48},{72,80},{88,96},{104,112},{136,144},{152,16... | collective-permute-start | bytes 196616 | tf_op jit(solution)/shard_map/ppermute | solution.py:338
  150.7 0.6 bitcast_subtract_fusion
  151.4 3.1 %collective-permute-done.13.side_2 = bf16[256,128]{1,0:T(8,128)(2,1)S(1)} collective-permute-done((bf16[256,128]{1,0:T(8,128)(2,1)}, bf16[256,128]{1,0:T(8,128)(2,1)S(1)}, u32[]{:S(2)}, u32[]{:S(2)}) %collective-permute-start.13) | collective-permute-done | bytes 65568 | tf_op jit(solution)/shard_map/ppermute | solution.py:338
  154.5 0.9 copy-done.9
  155.4 0.9 copy-done.11
  156.3 2.4 %new_mask.1 = (f32[1,512,512]{2,1,0:T(8,128)}, f32[1,512,512]{2,1,0:T(8,128)}) custom-call(s32[3]{0:T(128)S(1)} %copy-done.17, f32[512,512]{1,0:T(8,128)S(1)} %get-tuple-element.15.base, bf16[64,640]{1,0:T(8,128)(2,1)S(1)} %copy-done.9, bf16[64,640]{1,0:T(8,128)(2,1)S(1)} %copy-done.11, bf16[256,128]{1,0:T(8,128)(2,1)S(1)} %collective-permute-done.12.side_1, ...), custom_call_target="tpu_custom_call" | custom-call | tf_op jit(solution)/shard_map/new_mask/pallas_call | solution.py:339
  (65 shorter events, 0.7 us)
Async XLA Ops:
  0.6 16.1 %copy-start = (f32[1,512,512]{2,1,0:T(8,128)S(1)}, f32[1,512,512]{2,1,0:T(8,128)}, u32[]{:S(2)}) copy-start(f32[1,512,512]{2,1,0:T(8,128)} %mask.3) | copy-start | bytes 3145732
  2.3 15.3 %collective-permute-start = (f32[8,128]{1,0:T(8,128)S(1)}, f32[8,128]{1,0:T(8,128)S(1)}, u32[]{:S(2)}, u32[]{:S(2)}) collective-permute-start(f32[8,128]{1,0:T(8,128)S(1)} %broadcast_select_fusion.4), channel_id=1, source_target_pairs={{0,1},{1,0},{2,3},{3,2},{4,5},{5,4},{6,7},{7,6},{8,9},{9,8},{10,11... | collective-permute-start | bytes 12296 | tf_op jit(solution)/shard_map/ppermute | solution.py:249
  7.8 17.1 %collective-permute-start.4 = (bf16[64,512]{1,0:T(8,128)(2,1)}, bf16[64,512]{1,0:T(8,128)(2,1)S(1)}, u32[]{:S(2)}, u32[]{:S(2)}) collective-permute-start(bf16[64,512]{1,0:T(8,128)(2,1)} %get-tuple-element.29), channel_id=1, source_target_pairs={{64,128},{72,136},{80,144},{88,152},{96,160},{104,168},{112,176},{... | collective-permute-start | bytes 196616 | tf_op jit(solution)/shard_map/ppermute | solution.py:278
  8.4 16.5 %collective-permute-start.3 = (bf16[64,512]{1,0:T(8,128)(2,1)}, bf16[64,512]{1,0:T(8,128)(2,1)S(1)}, u32[]{:S(2)}, u32[]{:S(2)}) collective-permute-start(bf16[64,512]{1,0:T(8,128)(2,1)} %get-tuple-element.30), channel_id=1, source_target_pairs={{0,64},{8,72},{16,80},{24,88},{32,96},{40,104},{48,112},{56,120},{... | collective-permute-start | bytes 196616 | tf_op jit(solution)/shard_map/ppermute | solution.py:277
  16.7 17.7 %copy-start.3 = (s32[1,512,512]{2,1,0:T(8,128)S(1)}, s32[1,512,512]{2,1,0:T(8,128)}, u32[]{:S(2)}) copy-start(s32[1,512,512]{2,1,0:T(8,128)} %target.1) | copy-start | bytes 3145732
  18.2 16.2 %copy-start.1 = (bf16[640,512]{1,0:T(8,128)(2,1)S(1)}, bf16[640,512]{1,0:T(8,128)(2,1)}, u32[]{:S(2)}) copy-start(bf16[640,512]{1,0:T(8,128)(2,1)} %constant.71.clone.to_im) | copy-start | bytes 1966084
  18.2 16.2 %copy-start.2 = (bf16[640,512]{1,0:T(8,128)(2,1)S(1)}, bf16[640,512]{1,0:T(8,128)(2,1)}, u32[]{:S(2)}) copy-start(bf16[640,512]{1,0:T(8,128)(2,1)} %constant.70.clone.to_re) | copy-start | bytes 1966084
  18.2 2.7 %collective-permute-start.1 = (f32[8,128]{1,0:T(8,128)}, f32[8,128]{1,0:T(8,128)S(1)}, u32[]{:S(2)}, u32[]{:S(2)}) collective-permute-start(f32[8,128]{1,0:T(8,128)} %fusion.2), channel_id=1, source_target_pairs={{0,2},{1,3},{2,0},{3,1},{4,6},{5,7},{6,4},{7,5},{8,10},{9,11},{10,... | collective-permute-start | bytes 12296 | tf_op jit(solution)/shard_map/ppermute | solution.py:249
  20.9 4.0 %collective-permute-start.2 = (f32[8,128]{1,0:T(8,128)S(1)}, f32[8,128]{1,0:T(8,128)S(1)}, u32[]{:S(2)}, u32[]{:S(2)}) collective-permute-start(f32[8,128]{1,0:T(8,128)S(1)} %fusion.7), channel_id=1, source_target_pairs={{0,4},{1,5},{2,6},{3,7},{4,0},{5,1},{6,2},{7,3},{8,12},{9,13},{10,... | collective-permute-start | bytes 12296 | tf_op jit(solution)/shard_map/ppermute | solution.py:249
  23.9 62.0 %copy-start.16 = (s32[3]{0:T(128)}, s32[3]{0:T(128)S(1)}, u32[]{:S(2)}) copy-start(s32[3]{0:T(128)S(1)} %pad_add_fusion.place) | copy-start | bytes 40
  25.0 9.4 %copy-start.15 = (s32[128,128]{1,0:T(8,128)S(1)}, s32[128,128]{1,0:T(8,128)}, u32[]{:S(2)}) copy-start(s32[128,128]{1,0:T(8,128)} %pupil.1) | copy-start | bytes 196612
  26.2 8.2 %collective-permute-start.6 = (bf16[320,128]{1,0:T(8,128)(2,1)S(1)}, bf16[320,128]{1,0:T(8,128)(2,1)S(1)}, u32[]{:S(2)}, u32[]{:S(2)}) collective-permute-start(bf16[320,128]{1,0:T(8,128)(2,1)S(1)} %get-tuple-element.31), channel_id=1, source_target_pairs={{8,16},{24,32},{40,48},{72,80},{88,96},{104,112},{136,144},{152,16... | collective-permute-start | bytes 245768 | tf_op jit(solution)/shard_map/ppermute | solution.py:287
  32.2 2.1 %collective-permute-start.5 = (bf16[320,128]{1,0:T(8,128)(2,1)S(1)}, bf16[320,128]{1,0:T(8,128)(2,1)S(1)}, u32[]{:S(2)}, u32[]{:S(2)}) collective-permute-start(bf16[320,128]{1,0:T(8,128)(2,1)S(1)} %get-tuple-element.32), channel_id=1, source_target_pairs={{0,8},{8,0},{16,24},{24,16},{32,40},{40,32},{48,56},{56,48},{64,72... | collective-permute-start | bytes 245768 | tf_op jit(solution)/shard_map/ppermute | solution.py:286
  34.4 1.0 copy-start.4
  35.4 1.0 copy-start.5
  36.5 1.0 copy-start.7
  37.5 0.9 copy-start.12
  38.5 0.9 copy-start.13
  64.6 21.3 %copy-start.6 = (bf16[640,384]{1,0:T(8,128)(2,1)S(1)}, bf16[640,384]{1,0:T(8,128)(2,1)}, u32[]{:S(2)}) copy-start(bf16[640,384]{1,0:T(8,128)(2,1)} %constant.75.clone.freq_t) | copy-start | bytes 1474564
  64.6 6.7 %collective-permute-start.7 = (bf16[192,512]{1,0:T(8,128)(2,1)S(1)}, bf16[192,512]{1,0:T(8,128)(2,1)S(1)}, u32[]{:S(2)}, u32[]{:S(2)}) collective-permute-start(bf16[192,512]{1,0:T(8,128)(2,1)S(1)} %get-tuple-element.14), channel_id=1, source_target_pairs={{0,2},{1,3},{2,0},{3,1},{4,6},{5,7},{6,4},{7,5},{8,10},{9,11},{10,... | collective-permute-start | bytes 589832 | tf_op jit(solution)/shard_map/ppermute | solution.py:249
  71.4 7.7 %collective-permute-start.8 = (bf16[192,512]{1,0:T(8,128)(2,1)S(1)}, bf16[192,512]{1,0:T(8,128)(2,1)S(1)}, u32[]{:S(2)}, u32[]{:S(2)}) collective-permute-start(bf16[192,512]{1,0:T(8,128)(2,1)S(1)} %add_convert_fusion.1), channel_id=1, source_target_pairs={{0,4},{1,5},{2,6},{3,7},{4,0},{5,1},{6,2},{7,3},{8,12},{9,13},{10,... | collective-permute-start | bytes 589832 | tf_op jit(solution)/shard_map/ppermute | solution.py:249
  79.2 6.8 %collective-permute-start.9 = (bf16[192,512]{1,0:T(8,128)(2,1)S(1)}, bf16[192,512]{1,0:T(8,128)(2,1)S(1)}, u32[]{:S(2)}, u32[]{:S(2)}) collective-permute-start(bf16[192,512]{1,0:T(8,128)(2,1)S(1)} %add_convert_fusion.part_1), channel_id=1, source_target_pairs={{0,1},{1,0},{2,3},{3,2},{4,5},{5,4},{6,7},{7,6},{8,9},{9,8},{10,11... | collective-permute-start | bytes 589832 | tf_op jit(solution)/shard_map/ppermute | solution.py:249
  88.3 0.7 copy-start.14
  89.0 45.7 %collective-permute-start.10 = (bf16[64,640]{1,0:T(8,128)(2,1)S(1)}, bf16[64,640]{1,0:T(8,128)(2,1)S(1)}, u32[]{:S(2)}, u32[]{:S(2)}) collective-permute-start(bf16[64,640]{1,0:T(8,128)(2,1)S(1)} %get-tuple-element.16), channel_id=1, source_target_pairs={{0,64},{8,72},{16,80},{24,88},{32,96},{40,104},{48,112},{56,120},{... | collective-permute-start | bytes 245768 | tf_op jit(solution)/shard_map/ppermute | solution.py:327
  90.2 4.0 %collective-permute-start.21 = (f32[8,128]{1,0:T(8,128)S(1)}, f32[8,128]{1,0:T(8,128)S(1)}, u32[]{:S(2)}, u32[]{:S(2)}) collective-permute-start(f32[8,128]{1,0:T(8,128)S(1)} %get-tuple-element.23), channel_id=1, source_target_pairs={{0,1},{1,0},{2,3},{3,2},{4,5},{5,4},{6,7},{7,6},{8,9},{9,8},{10,11... | collective-permute-start | bytes 12296 | tf_op jit(solution)/shard_map/ppermute | solution.py:249
  94.2 2.8 %collective-permute-start.22 = (f32[8,128]{1,0:T(8,128)S(1)}, f32[8,128]{1,0:T(8,128)S(1)}, u32[]{:S(2)}, u32[]{:S(2)}) collective-permute-start(f32[8,128]{1,0:T(8,128)S(1)} %add.59), channel_id=1, source_target_pairs={{0,2},{1,3},{2,0},{3,1},{4,6},{5,7},{6,4},{7,5},{8,10},{9,11},{10,... | collective-permute-start | bytes 12296 | tf_op jit(solution)/shard_map/ppermute | solution.py:249
  96.9 4.0 %collective-permute-start.23 = (f32[8,128]{1,0:T(8,128)S(1)}, f32[8,128]{1,0:T(8,128)S(1)}, u32[]{:S(2)}, u32[]{:S(2)}) collective-permute-start(f32[8,128]{1,0:T(8,128)S(1)} %add.60), channel_id=1, source_target_pairs={{0,4},{1,5},{2,6},{3,7},{4,0},{5,1},{6,2},{7,3},{8,12},{9,13},{10,... | collective-permute-start | bytes 12296 | tf_op jit(solution)/shard_map/ppermute | solution.py:249
  100.9 6.4 %collective-permute-start.24 = (f32[8,128]{1,0:T(8,128)S(1)}, f32[8,128]{1,0:T(8,128)S(1)}, u32[]{:S(2)}, u32[]{:S(2)}) collective-permute-start(f32[8,128]{1,0:T(8,128)S(1)} %add.61), channel_id=1, source_target_pairs={{0,8},{8,0},{16,24},{24,16},{32,40},{40,32},{48,56},{56,48},{64,72... | collective-permute-start | bytes 12296 | tf_op jit(solution)/shard_map/ppermute | solution.py:253
  107.3 30.1 %collective-permute-start.11 = (bf16[64,640]{1,0:T(8,128)(2,1)S(1)}, bf16[64,640]{1,0:T(8,128)(2,1)S(1)}, u32[]{:S(2)}, u32[]{:S(2)}) collective-permute-start(bf16[64,640]{1,0:T(8,128)(2,1)S(1)} %get-tuple-element.17), channel_id=1, source_target_pairs={{64,128},{72,136},{80,144},{88,152},{96,160},{104,168},{112,176},{... | collective-permute-start | bytes 245768 | tf_op jit(solution)/shard_map/ppermute | solution.py:328
  108.0 2.7 %collective-permute-start.25 = (f32[8,128]{1,0:T(8,128)S(1)}, f32[8,128]{1,0:T(8,128)S(1)}, u32[]{:S(2)}, u32[]{:S(2)}) collective-permute-start(f32[8,128]{1,0:T(8,128)S(1)} %add.62), channel_id=1, source_target_pairs={{0,16},{8,24},{16,0},{24,8},{32,48},{40,56},{48,32},{56,40},{64,80... | collective-permute-start | bytes 12296 | tf_op jit(solution)/shard_map/ppermute | solution.py:253
  110.7 3.4 %collective-permute-start.26 = (f32[8,128]{1,0:T(8,128)S(1)}, f32[8,128]{1,0:T(8,128)S(1)}, u32[]{:S(2)}, u32[]{:S(2)}) collective-permute-start(f32[8,128]{1,0:T(8,128)S(1)} %add.63), channel_id=1, source_target_pairs={{0,32},{8,40},{16,48},{24,56},{32,0},{40,8},{48,16},{56,24},{64,96... | collective-permute-start | bytes 12296 | tf_op jit(solution)/shard_map/ppermute | solution.py:253
  114.0 13.7 %collective-permute-start.27 = (f32[8,128]{1,0:T(8,128)S(1)}, f32[8,128]{1,0:T(8,128)S(1)}, u32[]{:S(2)}, u32[]{:S(2)}) collective-permute-start(f32[8,128]{1,0:T(8,128)S(1)} %add.64), channel_id=1, source_target_pairs={{0,64},{8,72},{16,80},{24,88},{32,96},{40,104},{48,112},{56,120},{... | collective-permute-start | bytes 12296 | tf_op jit(solution)/shard_map/ppermute | solution.py:253
  127.7 4.5 %collective-permute-start.28 = (f32[8,128]{1,0:T(8,128)S(1)}, f32[8,128]{1,0:T(8,128)S(1)}, u32[]{:S(2)}, u32[]{:S(2)}) collective-permute-start(f32[8,128]{1,0:T(8,128)S(1)} %add.65), channel_id=1, source_target_pairs={{0,128},{8,136},{16,144},{24,152},{32,160},{40,168},{48,176},{56,1... | collective-permute-start | bytes 12296 | tf_op jit(solution)/shard_map/ppermute | solution.py:253
  129.4 10.5 %collective-permute-start.20 = (bf16[64,512]{1,0:T(8,128)(2,1)}, bf16[64,512]{1,0:T(8,128)(2,1)S(1)}, u32[]{:S(2)}, u32[]{:S(2)}) collective-permute-start(bf16[64,512]{1,0:T(8,128)(2,1)} %get-tuple-element.21.rest_0_), channel_id=1, source_target_pairs={{0,7},{1,6},{2,5},{3,4},{4,3},{5,2},{6,1},{7,0},{8,15},{9,14},{10,... | collective-permute-start | bytes 196616 | tf_op jit(solution)/shard_map/ppermute | solution.py:249
  132.2 8.7 %collective-permute-start.19 = (bf16[64,512]{1,0:T(8,128)(2,1)}, bf16[64,512]{1,0:T(8,128)(2,1)S(1)}, u32[]{:S(2)}, u32[]{:S(2)}) collective-permute-start(bf16[64,512]{1,0:T(8,128)(2,1)} %get-tuple-element.21.rest_0_), channel_id=1, source_target_pairs={{0,6},{1,7},{2,4},{3,5},{4,2},{5,3},{6,0},{7,1},{8,14},{9,15},{10,... | collective-permute-start | bytes 196616 | tf_op jit(solution)/shard_map/ppermute | solution.py:249
  132.2 11.3 %collective-permute-start.18 = (bf16[64,512]{1,0:T(8,128)(2,1)}, bf16[64,512]{1,0:T(8,128)(2,1)S(1)}, u32[]{:S(2)}, u32[]{:S(2)}) collective-permute-start(bf16[64,512]{1,0:T(8,128)(2,1)} %get-tuple-element.21.rest_0_), channel_id=1, source_target_pairs={{0,5},{1,4},{2,7},{3,6},{4,1},{5,0},{6,3},{7,2},{8,13},{9,12},{10,... | collective-permute-start | bytes 196616 | tf_op jit(solution)/shard_map/ppermute | solution.py:249
  134.7 3.3 %copy-start.8 = (bf16[64,640]{1,0:T(8,128)(2,1)}, bf16[64,640]{1,0:T(8,128)(2,1)S(1)}, u32[]{:S(2)}) copy-start(bf16[64,640]{1,0:T(8,128)(2,1)S(1)} %collective-permute-done.10.got_1) | copy-start | bytes 245764
  134.7 13.9 %collective-permute-start.17 = (bf16[64,512]{1,0:T(8,128)(2,1)}, bf16[64,512]{1,0:T(8,128)(2,1)S(1)}, u32[]{:S(2)}, u32[]{:S(2)}) collective-permute-start(bf16[64,512]{1,0:T(8,128)(2,1)} %get-tuple-element.21.rest_0_), channel_id=1, source_target_pairs={{0,4},{1,5},{2,6},{3,7},{4,0},{5,1},{6,2},{7,3},{8,12},{9,13},{10,... | collective-permute-start | bytes 196616 | tf_op jit(solution)/shard_map/ppermute | solution.py:249
  137.4 0.7 copy-start.10
  137.4 13.9 %collective-permute-start.16 = (bf16[64,512]{1,0:T(8,128)(2,1)}, bf16[64,512]{1,0:T(8,128)(2,1)S(1)}, u32[]{:S(2)}, u32[]{:S(2)}) collective-permute-start(bf16[64,512]{1,0:T(8,128)(2,1)} %get-tuple-element.21.rest_0_), channel_id=1, source_target_pairs={{0,3},{1,2},{2,1},{3,0},{4,7},{5,6},{6,5},{7,4},{8,11},{9,10},{10,... | collective-permute-start | bytes 196616 | tf_op jit(solution)/shard_map/ppermute | solution.py:249
  139.9 11.5 %collective-permute-start.15 = (bf16[64,512]{1,0:T(8,128)(2,1)}, bf16[64,512]{1,0:T(8,128)(2,1)S(1)}, u32[]{:S(2)}, u32[]{:S(2)}) collective-permute-start(bf16[64,512]{1,0:T(8,128)(2,1)} %get-tuple-element.21.rest_0_), channel_id=1, source_target_pairs={{0,2},{1,3},{2,0},{3,1},{4,6},{5,7},{6,4},{7,5},{8,10},{9,11},{10,... | collective-permute-start | bytes 196616 | tf_op jit(solution)/shard_map/ppermute | solution.py:249
  140.9 10.4 %collective-permute-start.14 = (bf16[64,512]{1,0:T(8,128)(2,1)}, bf16[64,512]{1,0:T(8,128)(2,1)S(1)}, u32[]{:S(2)}, u32[]{:S(2)}) collective-permute-start(bf16[64,512]{1,0:T(8,128)(2,1)} %get-tuple-element.21.rest_0_), channel_id=1, source_target_pairs={{0,1},{1,0},{2,3},{3,2},{4,5},{5,4},{6,7},{7,6},{8,9},{9,8},{10,11... | collective-permute-start | bytes 196616 | tf_op jit(solution)/shard_map/ppermute | solution.py:249
  143.5 7.3 %copy-start.18 = (f32[8]{0:T(128)S(1)}, f32[8]{0:T(128)}, u32[]{:S(2)}) copy-start(f32[8]{0:T(128)} %param.16) | copy-start | bytes 100
  143.5 7.9 %collective-permute-start.12 = (bf16[256,128]{1,0:T(8,128)(2,1)}, bf16[256,128]{1,0:T(8,128)(2,1)S(1)}, u32[]{:S(2)}, u32[]{:S(2)}) collective-permute-start(bf16[256,128]{1,0:T(8,128)(2,1)} %get-tuple-element.19), channel_id=1, source_target_pairs={{0,8},{8,0},{16,24},{24,16},{32,40},{40,32},{48,56},{56,48},{64,72... | collective-permute-start | bytes 196616 | tf_op jit(solution)/shard_map/ppermute | solution.py:337
  148.7 5.8 %collective-permute-start.13 = (bf16[256,128]{1,0:T(8,128)(2,1)}, bf16[256,128]{1,0:T(8,128)(2,1)S(1)}, u32[]{:S(2)}, u32[]{:S(2)}) collective-permute-start(bf16[256,128]{1,0:T(8,128)(2,1)} %get-tuple-element.20), channel_id=1, source_target_pairs={{8,16},{24,32},{40,48},{72,80},{88,96},{104,112},{136,144},{152,16... | collective-permute-start | bytes 196616 | tf_op jit(solution)/shard_map/ppermute | solution.py:338
  151.3 3.1 %copy-start.17 = (s32[3]{0:T(128)S(1)}, s32[3]{0:T(128)}, u32[]{:S(2)}) copy-start(s32[3]{0:T(128)} %copy-done.16) | copy-start | bytes 40
  154.5 0.9 copy-start.9
  155.4 0.9 copy-start.11

commit v2 on v1

v2 whole, which is shorter than its diff:
```python
import math

import jax
import jax.numpy as jnp
import ml_dtypes
import numpy as np
from jax import lax
from jax.experimental import pallas as pl
from jax.experimental.pallas import tpu as pltpu
from jax.sharding import PartitionSpec as P

TS = 512
HALO = 64
BAND = 128
SHIFT_MAX = 32
GRID_ROWS = 4
NE = TS + 2 * HALO
SPAN = BAND + 2 * SHIFT_MAX
HALF = 256
FOLD = SPAN // 2
ROWS = FOLD + 16
BATCH = 8
CHUNK = 256

steepness = 10.0
threshold = 0.25
mask_rate = 0.5
source_rate = 8.0

BF = jnp.bfloat16
F32 = jnp.float32

ORDER = np.concatenate([np.arange(HALO, HALO + TS), np.arange(HALO), np.arange(HALO + TS, NE)])


def make_tables():
    freq_index = np.arange(SPAN) - SPAN // 2
    phases = np.mod(freq_index[:, None] * ORDER[None, :], NE) * (2.0 * math.pi / NE)
    freq_re, freq_im = np.cos(phases) / NE, -np.sin(phases) / NE
    band_index = np.arange(BAND) - BAND // 2
    back_phase = np.mod((np.arange(TS) + HALO)[:, None] * band_index[None, :], NE) * (2.0 * math.pi / NE)
    back_re, back_im = np.cos(back_phase), np.sin(back_phase)

    def bf(table):
        return np.ascontiguousarray(table).astype(np.float32).astype(ml_dtypes.bfloat16)

    last = SPAN // 2 * ORDER * (2.0 * math.pi / NE)
    gap = np.zeros((HALF - SPAN - 1, NE))
    freq = np.concatenate([freq_re, np.cos(last)[None] / NE, gap, freq_im, -np.sin(last)[None] / NE, gap], 0)
    kept = np.concatenate([np.arange(FOLD, SPAN), [0]])
    rest = np.zeros((NE, ROWS - FOLD - 1))
    fold_t = np.concatenate([freq_re[kept].T, rest, freq_im[kept].T, rest], 1)
    back_t = np.block([[back_re.T, back_im.T], [-back_im.T, back_re.T]])
    rows = np.concatenate([back_re, back_im], 1)
    return tuple(bf(t) for t in (freq, back_t, back_t.T, rows, fold_t))


def rows_t_table(blocks):
    rows = make_tables()[3]
    step = TS // blocks
    parts = [
        np.concatenate([rows[i * step : (i + 1) * step, :BAND].T, rows[i * step : (i + 1) * step, BAND:].T], 1)
        for i in range(blocks)
    ]
    return np.stack(parts)


def dot(left, right):
    return lax.dot_general(left, right, (((1,), (0,)), ((), ())), preferred_element_type=F32)


def dot_nt(left, right):
    return lax.dot_general(left, right, (((1,), (1,)), ((), ())), preferred_element_type=F32)


def where_am_i():
    columns = lax.axis_size("tile") // GRID_ROWS
    tile = lax.axis_index("tile")
    row = tile // columns
    k = lax.axis_index("src")
    second = k // 2 % 2 == 1
    return k, row % 2 == 1, tile % 2 == 1, (row > 0) & (row < GRID_ROWS - 1), second


def fetch_all(pairs, sems):
    copies = [pltpu.make_async_copy(source, held, sems.at[n]) for n, (source, held) in enumerate(pairs)]
    for copy in copies:
        copy.start()
    return copies


def wait_all(copies):
    for copy in copies:
        copy.wait()


def edge_kernel(
    shifts, weights, mask_at, vert_out, side_1, side_2, info_out, top, bottom, left, right, sems
):
    k, row_odd, col_odd, _inner, second = where_am_i()
    wide = 2 * HALO
    copies = fetch_all(
        (
            (mask_at.at[0, pl.ds(0, HALO), :], top),
            (mask_at.at[0, pl.ds(TS - HALO, HALO), :], bottom),
            (mask_at.at[0, :, pl.ds(0, wide)], left),
            (mask_at.at[0, :, pl.ds(TS - wide, wide)], right),
        ),
        sems,
    )
    own = shifts.shape[1]
    high, low = split(weights[...])
    rest = weights[...] - high.astype(F32)
    mid, low = split(rest)
    parts = [shifts[:1].astype(F32), shifts[1:].astype(F32), high.astype(F32), mid.astype(F32), low.astype(F32)]
    wide_parts = [jnp.concatenate([part, jnp.zeros((1, 128 - own), F32)], 1) for part in parts]
    line = sum(wide_part if n == 0 else pltpu.roll(wide_part, n * own, 1) for n, wide_part in enumerate(wide_parts))
    row = lax.broadcasted_iota(jnp.int32, (16, 128), 0)
    info = jnp.where(row == k, line, 0.0).astype(BF)
    info_out[...] = jnp.concatenate([info, jnp.zeros((16, TS - 128), BF)], 1)
    vert_out[HALO:] = info_out[...]
    wait_all(copies)
    vert_out[:HALO] = jnp.where(row_odd ^ second, top[...], bottom[...]).astype(BF)
    half = TS // 2
    first = lax.broadcasted_iota(jnp.int32, (half, wide), 1) < HALO
    before = jnp.where(first, left[:half], pltpu.roll(left[half:], HALO, 1))
    after = jnp.where(first, pltpu.roll(right[:half], HALO, 1), right[half:])
    side_1[...] = jnp.where(col_odd, before, after).astype(BF)
    side_2[...] = jnp.where(col_odd, after, before).astype(BF)


def corner_kernel(mine_at, theirs_at, side_1_at, side_2_at, send_1, send_2, info_out, held, sems):
    _k, _row_odd, col_odd, _inner, _second = where_am_i()
    wide = 2 * HALO
    half = TS // 2
    ends = (pl.ds(0, wide), pl.ds(TS - wide, wide))
    copies = fetch_all(
        [(got.at[:, end], held.at[2 * n + m]) for n, got in enumerate((mine_at, theirs_at)) for m, end in enumerate(ends)]
        + [(side_1_at, send_1.at[pl.ds(0, half), :]), (side_2_at, send_2.at[pl.ds(0, half), :])],
        sems,
    )
    first = lax.broadcasted_iota(jnp.int32, (HALO, wide), 1) < HALO
    wait_all(copies)

    def above_below(m):
        return arrived(held[m, :HALO], held[2 + m, :HALO])

    info = held[0, HALO:].astype(F32) + held[2, HALO:].astype(F32)
    info_out[...] = info[:8]
    send_1[NE // 2 :] = info.astype(BF)
    above, below = above_below(0)
    before = jnp.where(first, above, pltpu.roll(below, HALO, 1))
    above, below = above_below(1)
    after = jnp.where(first, pltpu.roll(above, HALO, 1), below)
    send_1[half : NE // 2] = jnp.where(col_odd, before, after).astype(BF)
    send_2[half:] = jnp.where(col_odd, after, before).astype(BF)


def source_kernel(
    info, vert_1_at, vert_2_at, side_1_at, side_2_at,
    mask_at, target_at, pupil_at, freq_at, back_t_at, back_at, rows_at, rows_t_at,
    dspec_out, resist_out,
    spec, amps_a, amps_b, fields, image, dspec, terms, vert_1, vert_2, side_1, side_2,
    mask, freq, back_t, back, own_rows, rows_turned, pupil, bits, sems,
):
    step = resist_out.shape[0]
    k, row_odd, col_odd, _inner, second = where_am_i()
    own = pl.ds(pl.multiple_of(k * step, step), step)
    copies = fetch_all(
        (
            (vert_1_at.at[pl.ds(0, HALO), :], vert_1), (vert_2_at.at[pl.ds(0, HALO), :], vert_2),
            (side_1_at.at[pl.ds(0, NE // 2), :], side_1), (side_2_at, side_2),
            (freq_at, freq), (mask_at.at[0], mask), (pupil_at, pupil),
            (rows_at.at[own, :], own_rows), (back_t_at, back_t), (target_at.at[0, own, :], bits),
            (back_at, back), (rows_t_at.at[k], rows_turned),
        ),
        sems,
    )
    image[...] = jnp.zeros_like(image)
    dspec[...] = jnp.zeros_like(dspec)
    terms[...] = jnp.zeros_like(terms)
    wait_all(copies[:6])

    halo_rows = jnp.concatenate(arrived(vert_1[...], vert_2[...]), 0).astype(BF)
    s1, s2 = side_1[...].astype(F32), side_2[...].astype(F32)
    left, right = jnp.where(col_odd, s1, s2), jnp.where(col_odd, s2, s1)
    first = lax.broadcasted_iota(jnp.int32, left.shape, 1) < HALO
    one = jnp.where(first, left, pltpu.roll(right, HALO, 1)).astype(BF)
    two = jnp.where(first, pltpu.roll(left, HALO, 1), right).astype(BF)
    half = TS // 2
    halo_cols = jnp.concatenate([one[:half], two[:half], one[half:], two[half:]], 0)
    prod_mid = dot(freq[:, :TS], mask[...].astype(BF)) + dot(freq[:, TS:], halo_rows)
    prod_side = dot(freq[...], halo_cols)
    prod = jnp.concatenate([prod_mid, prod_side], 1).astype(BF)
    both = dot_nt(prod, freq[...])
    spec_re = both[:SPAN, :HALF] - both[HALF : HALF + SPAN, HALF:]
    spec_im = both[:SPAN, HALF:] + both[HALF : HALF + SPAN, :HALF]
    whole = jnp.concatenate([spec_re, spec_im], 1)
    for j in range(4):
        spec[j] = whole[:, j * 128 : (j + 1) * 128]

    wait_all(copies[6:9])
    gain = pupil[...].astype(F32).astype(BF)
    sources = info.shape[0] * 8

    def where_of(s):
        group, lane = s // 8, s % 8
        down, over = info[group, lane].astype(jnp.int32), info[group, lane + 8].astype(jnp.int32)
        w = (info[group, lane + 16] + info[group, lane + 24]) + info[group, lane + 32]
        return SHIFT_MAX - down, SHIFT_MAX - over, w

    def rows_of(i, u=0, count=BATCH):
        return pl.ds(pl.multiple_of(i * (BATCH * step) + u * step, step), count * step)

    def amplitudes(i, amps):
        for u in range(BATCH):
            down, over, _w = where_of(i * BATCH + u)
            turn = lax.bitwise_and(HALF - over, HALF - 1)
            band = [spec[j, pl.ds(down, BAND), :].astype(BF) for j in range(4)]
            win_re = pltpu.roll(jnp.concatenate(band[:2], 1), turn, 1)[:, :BAND] * gain
            win_im = pltpu.roll(jnp.concatenate(band[2:], 1), turn, 1)[:, :BAND] * gain
            window = jnp.concatenate(
                [jnp.concatenate([win_re, win_im], 1), jnp.concatenate([-win_im, win_re], 1)], 0
            )
            amps[u * step : (u + 1) * step, :] = dot(own_rows[...], window).astype(BF)

    def forward(i, amps):
        for c in range(0, TS, CHUNK):
            field_re = dot(amps[...], back_t[:, c : c + CHUNK])
            field_im = dot(amps[...], back_t[:, TS + c : TS + c + CHUNK])
            fields[rows_of(i), c : c + CHUNK] = field_re
            fields[rows_of(i), TS + c : TS + c + CHUNK] = field_im
            total = image[:, c : c + CHUNK]
            for u in range(BATCH):
                _d, _o, w = where_of(i * BATCH + u)
                re, im = field_re[u * step : (u + 1) * step], field_im[u * step : (u + 1) * step]
                total = total + w * (re * re + im * im)
            image[:, c : c + CHUNK] = total

    batches = sources // BATCH
    amplitudes(0, amps_a)

    def forward_pair(p, _):
        forward(2 * p, amps_a)
        amplitudes(2 * p + 1, amps_b)
        forward(2 * p + 1, amps_b)
        amplitudes(jnp.minimum(2 * p + 2, batches - 1), amps_a)
        return 0

    lax.fori_loop(0, batches // 2, forward_pair, 0)

    wait_all(copies[9:])
    resist = jax.nn.sigmoid(steepness * (image[...] * (1.0 / sources) - threshold))
    resist_out[...] = resist.astype(BF)
    image[...] = 2.0 * (resist - bits[...].astype(F32)) * resist * (1.0 - resist) * steepness

    def backward(i, damps):
        damp = jnp.zeros((BATCH * step, 2 * BAND), F32)
        for c in range(0, TS, CHUNK):
            grad = image[:, c : c + CHUNK]
            parts_re, parts_im = [], []
            for u in range(BATCH):
                s = i * BATCH + u
                _d, _o, w = where_of(s)
                re, im = fields[rows_of(i, u, 1), c : c + CHUNK], fields[rows_of(i, u, 1), TS + c : TS + c + CHUNK]
                term = jnp.sum((grad * (re * re + im * im)).reshape(step // 8, 8, CHUNK), 0)
                terms[s] += sum(term[:, n : n + 128] for n in range(0, CHUNK, 128))
                coef = (2.0 * w / sources) * grad
                parts_re.append((coef * re).astype(BF))
                parts_im.append((coef * im).astype(BF))
            damp = damp + dot(jnp.concatenate(parts_re, 0), back[c : c + CHUNK, :])
            damp = damp + dot(jnp.concatenate(parts_im, 0), back[TS + c : TS + c + CHUNK, :])
        damps[...] = damp.astype(BF)

    empty = jnp.zeros((step, HALF - BAND), BF)
    wide_gain = jnp.concatenate([gain, jnp.zeros((BAND, HALF - BAND), BF)], 1)

    def windows(i, damps):
        for u in range(BATCH):
            down, over, _w = where_of(i * BATCH + u)
            damp = damps[u * step : (u + 1) * step, :]
            damp_re = pltpu.roll(jnp.concatenate([damp[:, :BAND], empty], 1), over, 1)
            damp_im = pltpu.roll(jnp.concatenate([damp[:, BAND:], empty], 1), over, 1)
            inside = pltpu.roll(wide_gain, over, 1).astype(F32)
            pair = jnp.concatenate(
                [jnp.concatenate([damp_re, damp_im], 1), jnp.concatenate([damp_im, -damp_re], 1)], 0
            )
            dwin = dot(rows_turned[...], pair)
            for j in range(4):
                lanes = slice(j % 2 * 128, j % 2 * 128 + 128)
                dspec[u % 2 * 4 + j, pl.ds(down, BAND), :] += dwin[:, j * 128 : (j + 1) * 128] * inside[:, lanes]

    backward(0, amps_a)

    def backward_pair(p, _):
        backward(2 * p + 1, amps_b)
        windows(2 * p, amps_a)
        backward(2 * p + 2, amps_a)
        windows(2 * p + 1, amps_b)
        return 0

    lax.fori_loop(0, batches // 2 - 1, backward_pair, 0)
    backward(batches - 1, amps_b)
    windows(batches - 2, amps_a)
    windows(batches - 1, amps_b)

    whole = jnp.concatenate([dspec[j] + dspec[4 + j] for j in range(4)], 1)
    high, low = split(whole[:FOLD])
    both = jnp.concatenate([high, low], 0)
    turn_cols = (
        lax.broadcasted_iota(jnp.int32, (HALF, HALF), 0) + lax.broadcasted_iota(jnp.int32, (HALF, HALF), 1) == SPAN
    ).astype(BF)
    turned = jnp.concatenate([dot(both[:, :HALF], turn_cols), dot(both[:, HALF:], turn_cols)], 1).astype(BF)
    at_row = lax.broadcasted_iota(jnp.int32, (FOLD, 2 * FOLD), 0)
    at_col = lax.broadcasted_iota(jnp.int32, (FOLD, 2 * FOLD), 1)
    turn_rows = (
        ((at_row + at_col == FOLD) & (at_col < FOLD)) | ((at_row + at_col == 2 * FOLD) & (at_col > FOLD))
    ).astype(BF)
    folded = dot(turn_rows, turned)
    sign = jnp.where(lax.broadcasted_iota(jnp.int32, (FOLD, 2 * HALF), 1) < HALF, 1.0, -1.0)
    dspec_out[:FOLD] = (whole[FOLD:] + sign * folded).astype(BF)
    sums = lax.dot_general(
        jnp.ones((8, 128), F32), jnp.sum(terms[...], 1), (((1,), (1,)), ((), ())),
        precision=lax.Precision.HIGHEST, preferred_element_type=F32,
    )
    dspec_out[FOLD:] = weight_rows(jnp.concatenate([whole[:8], jnp.zeros_like(whole[:8])], 0), sums[:1])


def weight_rows(line, sums):
    high = sums.astype(BF).astype(F32)
    mid = (sums - high).astype(BF).astype(F32)
    low = sums - high - mid
    row = lax.broadcasted_iota(jnp.int32, line.shape, 0)
    kept = jnp.where(row == 0, line, 0.0)
    for n, piece in enumerate((high, mid, low)):
        if line.shape[1] > 128:
            piece = jnp.concatenate([piece, jnp.zeros((1, line.shape[1] - 128), F32)], 1)
        kept = jnp.where(row == n + 1, piece, kept)
    return kept.astype(BF)


def weight_sums(rows):
    return rows[1:2] + rows[2:3] + rows[3:4]


def add(one, two):
    one, two = one.astype(F32), two.astype(F32)
    sums = weight_sums(one[FOLD:]) + weight_sums(two[FOLD:])
    high = lax.reduce_precision(sums, 8, 7)
    mid = lax.reduce_precision(sums - high, 8, 7)
    row = lax.broadcasted_iota(jnp.int32, one.shape, 0) - FOLD
    total = one + two
    for n, piece in enumerate((high, mid, sums - high - mid)):
        total = jnp.where(row == n + 1, piece, total)
    return total.astype(BF)


def split(values):
    high = values.astype(BF)
    return high, (values - high.astype(F32)).astype(BF)


def pack_sides(before, after, col_odd, side_1, side_2):
    side_1[...] = jnp.where(col_odd, before, after).astype(BF)
    side_2[...] = jnp.where(col_odd, after, before).astype(BF)


def mask_kernel(mask, part_1, part_2, freq, fold_t, base_out, rims_out, side_1, side_2):
    _k, _row_odd, col_odd, _inner, _second = where_am_i()
    total = part_1[...].astype(F32) + part_2[...].astype(F32)
    swapped = jnp.concatenate([total[:, HALF:], -total[:, :HALF]], 1)
    both = dot(jnp.concatenate([*split(total), *split(swapped)], 0), freq[...])
    prod = jnp.concatenate([both[:ROWS] + both[ROWS : 2 * ROWS], both[2 * ROWS : 3 * ROWS] + both[3 * ROWS :]], 0)
    high, low = split(prod)
    ext = dot(fold_t[...], high) + dot(fold_t[...], low)
    base_out[...] = mask[0] - mask_rate * ext[:TS, :TS]
    rims_out[...] = ext[TS:, :TS]
    sides = ext[:, TS:]
    half, quarter = TS // 2, HALO
    upper = jnp.concatenate([sides[:half], sides[TS : TS + quarter]], 0)
    lower = jnp.concatenate([sides[half:TS], sides[TS + quarter :]], 0)
    first = lax.broadcasted_iota(jnp.int32, upper.shape, 1) < HALO
    before = jnp.where(first, upper, pltpu.roll(lower, HALO, 1))
    after = jnp.where(first, pltpu.roll(upper, HALO, 1), lower)
    pack_sides(before, after, col_odd, side_1, side_2)


def arrived(mine, theirs):
    mine, theirs = mine.astype(F32), theirs.astype(F32)
    _k, row_odd, _col_odd, inner, second = where_am_i()
    g1 = jnp.where(second, theirs, mine)
    g2 = jnp.where(inner, jnp.where(second, mine, theirs), 0.0)
    return jnp.where(row_odd, g1, g2), jnp.where(row_odd, g2, g1)


def from_sides(side_1, side_2):
    _k, _row_odd, col_odd, _inner, _second = where_am_i()
    s1, s2 = side_1.astype(F32), side_2.astype(F32)
    before, after = jnp.where(col_odd, s1, s2), jnp.where(col_odd, s2, s1)
    first = lax.broadcasted_iota(jnp.int32, before.shape, 1) < HALO
    left = jnp.where(first, before, 0.0), jnp.where(first, pltpu.roll(before, HALO, 1), 0.0)
    right = jnp.where(first, 0.0, pltpu.roll(after, HALO, 1)), jnp.where(first, 0.0, after)
    return left, right


def rim_kernel(rims_at, side_1_at, side_2_at, weight_at, vert_out, rims, side_1, side_2, weight, sems):
    _k, row_odd, _col_odd, _inner, second = where_am_i()
    corner = pl.ds(TS // 2, HALO)
    copies = fetch_all(
        (
            (rims_at, rims), (side_1_at.at[corner, :], side_1), (side_2_at.at[corner, :], side_2), (weight_at, weight),
        ),
        sems,
    )
    wait_all(copies)
    left, right = from_sides(side_1[...], side_2[...])
    wide = 2 * HALO
    for n in range(2):
        rows = slice(n * HALO, (n + 1) * HALO)
        rims[rows, :wide] += left[n]
        rims[rows, TS - wide :] += right[n]
    vert_out[:HALO] = jnp.where(row_odd ^ second, rims[:HALO], rims[HALO:]).astype(BF)
    vert_out[HALO:] = weight_rows(jnp.zeros((16, TS), F32), weight[:1])


def final_kernel(
    base_at, side_1_at, side_2_at, mine_at, theirs_at, weight_at, other_at, near_at, far_at,
    mask_at, resist_at, weight_out,
    base, side_1, side_2, mine, theirs, weight, other, near, far, resist, sems,
):
    k, _row_odd, _col_odd, _inner, second = where_am_i()
    step = near.shape[0] // 4
    half = TS // 2
    inside = (pl.ds(0, half), slice(None))
    copies = fetch_all(
        (
            (near_at, near), (far_at, far), (base_at, base), (side_1_at.at[inside], side_1),
            (side_2_at.at[inside], side_2), (mine_at, mine), (theirs_at, theirs), (weight_at, weight), (other_at, other),
        ),
        sems,
    )
    wait_all(copies[:2])
    for m in range(8):
        piece = (near, far)[m % 2][m // 2 * step : (m // 2 + 1) * step, :]
        at = lax.bitwise_xor(k, m)
        resist[pl.ds(pl.multiple_of(at * step, step), step), :] = piece.astype(F32)
    resist_done = pltpu.make_async_copy(resist, resist_at.at[0], sems.at[0])
    resist_done.start()
    wait_all(copies[2:])
    left, right = from_sides(side_1[...], side_2[...])
    wide = 2 * HALO
    for n in range(2):
        rows = slice(n * half, (n + 1) * half)
        base[rows, :wide] -= mask_rate * left[n]
        base[rows, TS - wide :] -= mask_rate * right[n]
    above, below = arrived(mine[:HALO], theirs[:HALO])
    base[:HALO] -= mask_rate * above
    base[TS - HALO :] -= mask_rate * below
    mask_done = pltpu.make_async_copy(base, mask_at.at[0], sems.at[1])
    mask_done.start()
    from_1, from_2 = weight_sums(mine[HALO:, :128].astype(F32)), weight_sums(theirs[HALO:, :128].astype(F32))
    from_1, from_2 = jnp.where(second, from_2, from_1), jnp.where(second, from_1, from_2)
    weight_out[...] = jnp.broadcast_to((weight[:1] + from_1) + (from_2 + other[:1]), weight_out.shape)
    mask_done.wait()
    resist_done.wait()


SMEM = pl.BlockSpec(memory_space=pltpu.SMEM)
VMEM = pl.BlockSpec(memory_space=pltpu.VMEM)
HBM = pl.BlockSpec(memory_space=pl.ANY)


def shaped(shape, dtype):
    return jax.ShapeDtypeStruct(shape, dtype)


def grid_routes(tiles, columns):
    row_swap = [(t, t ^ columns) for t in range(tiles)]
    row_next = [(t, t + columns) for t in range(tiles) if (t // columns) % 2 == 1 and t + columns < tiles]
    col_swap = [(t, t ^ 1) for t in range(tiles)]
    col_next = [(t, t + 1) for t in range(tiles) if t % 2 == 1 and (t + 1) % columns != 0]
    back = lambda route: route + [(b, a) for a, b in route]
    return row_swap, back(row_next), col_swap, back(col_next)


def route_of(first, second, groups, distance=0):
    return [
        (a * groups + k, b * groups + (k ^ distance)) for k in range(groups) for a, b in (second if k // 2 % 2 == 1 else first)
    ]


def src_swap(block, distance, count):
    return lax.ppermute(block, "src", [(i, i ^ distance) for i in range(count)])


def tile_swap(block, distance, count):
    return lax.ppermute(block, "tile", [(i, i ^ distance) for i in range(count)])


def per_device(mask, target, shifts, source_weights, pupil):
    tiles, groups = lax.axis_size("tile"), lax.axis_size("src")
    columns = tiles // GRID_ROWS
    k = lax.axis_index("src")
    row_swap, row_next, col_swap, col_next = grid_routes(tiles, columns)
    row_ring = row_next + [(t, t ^ (3 * columns)) for t in range(tiles) if (t // columns) % 3 == 0]
    freq, back_t, back, rows, fold_t = (jnp.asarray(t) for t in make_tables())
    rows_t = jnp.asarray(rows_t_table(groups))
    own = shifts.shape[0]
    step = TS // groups

    vert, side_1, side_2, info = pl.pallas_call(
        edge_kernel,
        out_shape=(shaped((HALO + 16, TS), BF),) + (shaped((TS // 2, 128), BF),) * 2 + (shaped((16, TS), BF),),
        in_specs=[VMEM] * 2 + [HBM],
        out_specs=(VMEM,) * 4,
        scratch_shapes=[pltpu.VMEM((HALO, TS), F32)] * 2
        + [pltpu.VMEM((TS, 2 * HALO), F32)] * 2
        + [pltpu.SemaphoreType.DMA((4,))],
        name="edges",
    )(shifts.T, source_weights[None], mask)
    mine = lax.ppermute(vert, ("tile", "src"), route_of(row_swap, row_ring, groups, 4))
    mine = jnp.concatenate([mine[:HALO], mine[HALO:] + info], 0)
    theirs = src_swap(mine, 2, groups)
    side_1, side_2, info = pl.pallas_call(
        corner_kernel,
        out_shape=(shaped((NE // 2 + 16, 128), BF), shaped((NE // 2, 128), BF), shaped((8, 128), F32)),
        in_specs=[HBM] * 4,
        out_specs=(VMEM,) * 3,
        scratch_shapes=[pltpu.VMEM((4, HALO + 16, 2 * HALO), BF), pltpu.SemaphoreType.DMA((6,))],
        name="corners",
    )(mine, theirs, side_1, side_2)
    side_1 = lax.ppermute(side_1, ("tile", "src"), route_of(col_swap, col_swap, groups, 1))
    side_2 = lax.ppermute(side_2, "tile", col_next)
    info = info + side_1[NE // 2 : NE // 2 + 8].astype(F32)

    part, resist = pl.pallas_call(
        source_kernel,
        out_shape=(shaped((ROWS, 2 * HALF), BF), shaped((step, TS), BF)),
        in_specs=[SMEM] + [HBM] * 12,
        out_specs=(VMEM, VMEM),
        scratch_shapes=[
            pltpu.VMEM((4, SPAN, 128), F32),
            pltpu.VMEM((BATCH * step, 2 * BAND), BF),
            pltpu.VMEM((BATCH * step, 2 * BAND), BF),
            pltpu.VMEM((groups * own * step, 2 * TS), F32),
            pltpu.VMEM((step, TS), F32),
            pltpu.VMEM((8, SPAN, 128), F32),
            pltpu.VMEM((128, 8, 128), F32),
            pltpu.VMEM((HALO, TS), BF),
            pltpu.VMEM((HALO, TS), BF),
            pltpu.VMEM((NE // 2, 128), BF),
            pltpu.VMEM((NE // 2, 128), BF),
            pltpu.VMEM((TS, TS), F32),
            pltpu.VMEM((2 * HALF, NE), BF),
            pltpu.VMEM((2 * BAND, 2 * TS), BF),
            pltpu.VMEM((2 * TS, 2 * BAND), BF),
            pltpu.VMEM((step, 2 * BAND), BF),
            pltpu.VMEM((BAND, 2 * step), BF),
            pltpu.VMEM((BAND, BAND), jnp.int32),
            pltpu.VMEM((step, TS), jnp.int32),
            pltpu.SemaphoreType.DMA((12,)),
        ],
        compiler_params=pltpu.CompilerParams(vmem_limit_bytes=60 << 20),
        name="sources",
    )(
        info, mine, theirs, side_1, side_2, mask, target, pupil,
        freq, back_t, back, rows, rows_t,
    )

    other = src_swap(part, 2, groups)
    near = src_swap(resist, 2, groups)
    part, near = lax.optimization_barrier((add(part, other), near))
    other = src_swap(part, 4, groups)
    part = add(part, other)
    other = src_swap(part, 1, groups)
    weight = weight_sums(part[FOLD:, :128].astype(F32)) + weight_sums(other[FOLD:, :128].astype(F32))
    weight = jnp.broadcast_to(weight, (8, 128))
    weight = weight + tile_swap(weight, 1, tiles)
    base, rims, side_1, side_2 = pl.pallas_call(
        mask_kernel,
        out_shape=(shaped((TS, TS), F32), shaped((2 * HALO, TS), F32)) + (shaped((NE // 2, 128), BF),) * 2,
        in_specs=[VMEM] * 5,
        out_specs=(VMEM,) * 4,
        compiler_params=pltpu.CompilerParams(vmem_limit_bytes=40 << 20),
        name="mask_gradient",
    )(mask, part, other, freq, fold_t)

    near = jnp.concatenate([resist, near], 0)
    side_1, side_2, weight, near = lax.optimization_barrier((side_1, side_2, weight, near))
    far = src_swap(near, 4, groups)
    side_1 = lax.ppermute(side_1, "tile", col_swap)
    side_2 = lax.ppermute(side_2, "tile", col_next)
    for distance in (2, 4):
        weight = weight + tile_swap(weight, distance, tiles)
    side_1, side_2, weight, far = lax.optimization_barrier((side_1, side_2, weight, far))
    rim = pl.pallas_call(
        rim_kernel,
        out_shape=shaped((HALO + 16, TS), BF),
        in_specs=[HBM] * 4,
        out_specs=VMEM,
        scratch_shapes=[
            pltpu.VMEM((2 * HALO, TS), F32),
            pltpu.VMEM((HALO, 128), BF),
            pltpu.VMEM((HALO, 128), BF),
            pltpu.VMEM((8, 128), F32),
            pltpu.SemaphoreType.DMA((4,)),
        ],
        name="row_rims",
    )(rims, side_1, side_2, weight)
    near = jnp.concatenate([near, far], 0)
    rim, weight, near = lax.optimization_barrier((rim, weight, near))
    mine = lax.ppermute(rim, ("tile", "src"), route_of(row_swap, row_ring, groups))
    other = tile_swap(weight, 2 * columns, tiles)
    far = src_swap(near, 1, groups)
    theirs = src_swap(mine, 2, groups)
    new_mask, resist_tile, terms = pl.pallas_call(
        final_kernel,
        out_shape=(shaped((1, TS, TS), F32),) * 2 + (shaped((8, 128), F32),),
        in_specs=[HBM] * 9,
        out_specs=(HBM, HBM, VMEM),
        scratch_shapes=[
            pltpu.VMEM((TS, TS), F32),
            pltpu.VMEM((TS // 2, 128), BF),
            pltpu.VMEM((TS // 2, 128), BF),
            pltpu.VMEM((HALO + 16, TS), BF),
            pltpu.VMEM((HALO + 16, TS), BF),
            pltpu.VMEM((8, 128), F32),
            pltpu.VMEM((8, 128), F32),
            pltpu.VMEM((4 * step, TS), BF),
            pltpu.VMEM((4 * step, TS), BF),
            pltpu.VMEM((TS, TS), F32),
            pltpu.SemaphoreType.DMA((9,)),
        ],
        name="new_mask",
    )(base, side_1, side_2, mine, theirs, weight, other, near, far)

    weight_total = lax.dynamic_slice(terms, (0, k * own), (1, own))[0]
    new_weights = source_weights - source_rate * weight_total / (TS * TS * tiles)
    return (new_mask, new_weights, resist_tile)


def solution(mesh):
    in_specs = (P("tile", None, None), P("tile", None, None), P("src", None), P("src"), P())
    out_specs = (P("tile", None, None), P("src"), P("tile", None, None))
    return jax.shard_map(
        per_device, mesh=mesh, in_specs=in_specs, out_specs=out_specs, check_vma=False
    )
```

time: 159 us -> 114 us (0.72)
  the two profiles are of different devices: /device:TPU:1 before, /device:TPU:32 now
where the time goes in v2:
time: 114 us
  starting transfers between devices  39 us (34%)
  waiting for transfers between devices  35.8 us (31%)
  Pallas kernels  29.5 us (26%)
  local copies, waits for them, and re-layouts  4.3 us (4%)
  other arithmetic  3.87 us (3%)
    pallas_call x1, Pallas kernels, per_device(): pl.pallas_call(source_kernel, out_shape=(shaped((ROWS, 2 * HALF), BF), sh...  18.9 us
    ppermute x8, waiting for transfers between devices, src_swap(): return lax.ppermute(block, 'src', [(i, i ^ distance) for i in range(count)])  17.2 us
    ppermute x8, starting transfers between devices, src_swap(): return lax.ppermute(block, 'src', [(i, i ^ distance) for i in range(count)])  11.6 us
    ppermute x4, waiting for transfers between devices, tile_swap(): lax.ppermute(block, 'tile', [(i, i ^ distance) for i in range(count)])  9.05 us
    ppermute x1, starting transfers between devices, per_device(): lax.ppermute(vert, ('tile', 'src'), route_of(row_swap, row_ring, groups, 4))  9.01 us
    ppermute x2, starting transfers between devices, per_device(): side_2 = lax.ppermute(side_2, 'tile', col_next)  7.02 us
    ppermute x1, starting transfers between devices, per_device(): lax.ppermute(rim, ('tile', 'src'), route_of(row_swap, row_ring, groups))  5.71 us
    unnamed x44, local copies, waits for them, and re-layouts  4.29 us
  transfers between devices with their start and end apart: 18, of which 12 were waited for; matrix products, arithmetic and copies ran while one was open for 2% of the time, Pallas kernels for 1%

profile of v2, /device:TPU:32, one launch (start us, length us, event | category | flops | bytes accessed | tf_op | source)
XLA Modules:
  0.0 113.5 jit_solution(13388071694672066553)
XLA Ops:
  0.6 2.7 %edges.1 = (bf16[80,512]{1,0:T(8,128)(2,1)}, bf16[256,128]{1,0:T(8,128)(2,1)}, bf16[256,128]{1,0:T(8,128)(2,1)}, bf16[16,512]{1,0:T(8,128)(2,1)}) custom-call(s32[2,8]{1,0:T(2,128)} %bitcast.19, f32[1,8]{1,0:T(1,128)} %bitcast.18, f32[1,512,512]{2,1,0:T(8,128)} %mask.1), custom_call_target="tpu_custom_call" | custom-call | tf_op jit(solution)/shard_map/edges/pallas_call | solution.py:511
  3.3 0.0 copy-start.18
  3.3 9.0 %collective-permute-start = (bf16[80,512]{1,0:T(8,128)(2,1)}, bf16[80,512]{1,0:T(8,128)(2,1)S(1)}, u32[]{:S(2)}, u32[]{:S(2)}) collective-permute-start(bf16[80,512]{1,0:T(8,128)(2,1)} %get-tuple-element.32), channel_id=1, source_target_pairs={{0,68},{8,76},{16,84},{24,92},{32,100},{40,108},{48,116},{56,124},... | collective-permute-start | bytes 245768 | tf_op jit(solution)/shard_map/ppermute | solution.py:521
  12.3 4.0 %collective-permute-done = bf16[80,512]{1,0:T(8,128)(2,1)S(1)} collective-permute-done((bf16[80,512]{1,0:T(8,128)(2,1)}, bf16[80,512]{1,0:T(8,128)(2,1)S(1)}, u32[]{:S(2)}, u32[]{:S(2)}) %collective-permute-start) | collective-permute-done | bytes 81952 | tf_op jit(solution)/shard_map/ppermute | solution.py:521
  16.3 0.0 copy-start.6
  16.3 1.7 %collective-permute-start.1 = (bf16[80,512]{1,0:T(8,128)(2,1)S(1)}, bf16[80,512]{1,0:T(8,128)(2,1)S(1)}, u32[]{:S(2)}, u32[]{:S(2)}) collective-permute-start(bf16[80,512]{1,0:T(8,128)(2,1)S(1)} %pad_maximum_fusion.2.mine_at.vert_1_at), channel_id=1, source_target_pairs={{0,2},{1,3},{2,0},{3,1},{4,6},{5,7},{6,4},{7,5},{8,10},{9,11},{10,... | collective-permute-start | bytes 245768 | tf_op jit(solution)/shard_map/ppermute | solution.py:493
  18.0 2.8 %collective-permute-done.1.theirs_at.vert_2_at = bf16[80,512]{1,0:T(8,128)(2,1)S(1)} collective-permute-done((bf16[80,512]{1,0:T(8,128)(2,1)S(1)}, bf16[80,512]{1,0:T(8,128)(2,1)S(1)}, u32[]{:S(2)}, u32[]{:S(2)}) %collective-permute-start.1) | collective-permute-done | bytes 81952 | tf_op jit(solution)/shard_map/ppermute | solution.py:493
  20.9 0.6 copy-done.10
  21.5 1.7 %corners.1 = (bf16[336,128]{1,0:T(8,128)(2,1)}, bf16[320,128]{1,0:T(8,128)(2,1)}, f32[8,128]{1,0:T(8,128)}) custom-call(bf16[80,512]{1,0:T(8,128)(2,1)} %copy-done.6, bf16[80,512]{1,0:T(8,128)(2,1)} %copy-done.10, bf16[256,128]{1,0:T(8,128)(2,1)} %get-tuple-element.34.side_1_at, bf16[256,128]{1,0:T(8,128)(2,1)} %get-tuple-element.35.side_2_at), custom_call_target="tpu_custom_call" | custom-call | tf_op jit(solution)/shard_map/corners/pallas_call | solution.py:524
  23.3 0.1 collective-permute-start.2
  23.4 5.1 %collective-permute-start.3 = (bf16[320,128]{1,0:T(8,128)(2,1)}, bf16[320,128]{1,0:T(8,128)(2,1)S(1)}, u32[]{:S(2)}, u32[]{:S(2)}) collective-permute-start(bf16[320,128]{1,0:T(8,128)(2,1)} %get-tuple-element.38), channel_id=1, source_target_pairs={{8,16},{24,32},{40,48},{72,80},{88,96},{104,112},{136,144},{152,16... | collective-permute-start | bytes 245768 | tf_op jit(solution)/shard_map/ppermute | solution.py:533
  28.5 1.4 %collective-permute-done.2.side_1_at = bf16[336,128]{1,0:T(8,128)(2,1)S(1)} collective-permute-done((bf16[336,128]{1,0:T(8,128)(2,1)}, bf16[336,128]{1,0:T(8,128)(2,1)S(1)}, u32[]{:S(2)}, u32[]{:S(2)}) %collective-permute-start.2) | collective-permute-done | bytes 86048 | tf_op jit(solution)/shard_map/ppermute | solution.py:532
  29.8 0.6 convert_add_fusion.info
  30.4 0.4 collective-permute-done.3.side_2_at
  30.8 0.6 copy-done.15
  31.5 18.9 %sources.1 = (bf16[112,512]{1,0:T(8,128)(2,1)}, bf16[64,512]{1,0:T(8,128)(2,1)}) custom-call(f32[8,128]{1,0:T(8,128)} %convert_add_fusion.info, bf16[80,512]{1,0:T(8,128)(2,1)} %copy-done.6, bf16[80,512]{1,0:T(8,128)(2,1)} %copy-done.10, bf16[336,128]{1,0:T(8,128)(2,1)} %copy-done.12, bf16[320,128]{1,0:T(8,128)(2,1)} %copy-done.15, f32[1,512,512]{2,1,0:T(8,128)} %mask.1, ...), custom_call_target="tpu_custom_call" | custom-call | tf_op jit(solution)/shard_map/sources/pallas_call | solution.py:536
  50.3 1.4 %collective-permute-start.4 = (bf16[112,512]{1,0:T(8,128)(2,1)}, bf16[112,512]{1,0:T(8,128)(2,1)S(1)}, u32[]{:S(2)}, u32[]{:S(2)}) collective-permute-start(bf16[112,512]{1,0:T(8,128)(2,1)} %get-tuple-element.39), channel_id=1, source_target_pairs={{0,2},{1,3},{2,0},{3,1},{4,6},{5,7},{6,4},{7,5},{8,10},{9,11},{10,... | collective-permute-start | bytes 344072 | tf_op jit(solution)/shard_map/ppermute | solution.py:493
  51.8 0.0 copy-start.7
  51.8 1.0 convert_element_type.28
  52.8 0.0 copy-start
  52.8 0.8 collective-permute-start.5
  53.6 2.4 %collective-permute-done.4 = bf16[112,512]{1,0:T(8,128)(2,1)S(1)} collective-permute-done((bf16[112,512]{1,0:T(8,128)(2,1)}, bf16[112,512]{1,0:T(8,128)(2,1)S(1)}, u32[]{:S(2)}, u32[]{:S(2)}) %collective-permute-start.4) | collective-permute-done | bytes 114720 | tf_op jit(solution)/shard_map/ppermute | solution.py:493
  56.1 0.1 select_convert_fusion.1
  56.2 0.0 copy-start.1
  56.3 1.6 %collective-permute-done.5 = bf16[64,512]{1,0:T(8,128)(2,1)S(1)} collective-permute-done((bf16[64,512]{1,0:T(8,128)(2,1)S(1)}, bf16[64,512]{1,0:T(8,128)(2,1)S(1)}, u32[]{:S(2)}, u32[]{:S(2)}) %collective-permute-start.5) | collective-permute-done | bytes 65568 | tf_op jit(solution)/shard_map/ppermute | solution.py:493
  57.9 1.7 %collective-permute-start.6 = (bf16[112,512]{1,0:T(8,128)(2,1)S(1)}, bf16[112,512]{1,0:T(8,128)(2,1)S(1)}, u32[]{:S(2)}, u32[]{:S(2)}) collective-permute-start(bf16[112,512]{1,0:T(8,128)(2,1)S(1)} %select_convert_fusion.1), channel_id=1, source_target_pairs={{0,4},{1,5},{2,6},{3,7},{4,0},{5,1},{6,2},{7,3},{8,12},{9,13},{10,... | collective-permute-start | bytes 344072 | tf_op jit(solution)/shard_map/ppermute | solution.py:493
  59.6 5.0 %collective-permute-done.6 = bf16[112,512]{1,0:T(8,128)(2,1)S(1)} collective-permute-done((bf16[112,512]{1,0:T(8,128)(2,1)S(1)}, bf16[112,512]{1,0:T(8,128)(2,1)S(1)}, u32[]{:S(2)}, u32[]{:S(2)}) %collective-permute-start.6) | collective-permute-done | bytes 114720 | tf_op jit(solution)/shard_map/ppermute | solution.py:493
  64.6 0.0 copy-start.3
  64.6 0.1 select_convert_fusion.part_1
  64.8 1.1 collective-permute-start.7
  65.8 5.3 %collective-permute-done.7.part_2 = bf16[112,512]{1,0:T(8,128)(2,1)S(1)} collective-permute-done((bf16[112,512]{1,0:T(8,128)(2,1)S(1)}, bf16[112,512]{1,0:T(8,128)(2,1)S(1)}, u32[]{:S(2)}, u32[]{:S(2)}) %collective-permute-start.7) | collective-permute-done | bytes 114720 | tf_op jit(solution)/shard_map/ppermute | solution.py:493
  71.2 0.3 collective-permute-start.8
  71.5 1.2 %mask_gradient.1 = (f32[512,512]{1,0:T(8,128)S(1)}, f32[128,512]{1,0:T(8,128)S(1)}, bf16[320,128]{1,0:T(8,128)(2,1)S(1)}, bf16[320,128]{1,0:T(8,128)(2,1)S(1)}) custom-call(f32[1,512,512]{2,1,0:T(8,128)S(1)} %copy-done, bf16[112,512]{1,0:T(8,128)(2,1)S(1)} %select_convert_fusion.part_1, bf16[112,512]{1,0:T(8,128)(2,1)S(1)} %collective-permute-done.7.part_2, ...), custom_call_target="tpu_custom_call" | custom-call | tf_op jit(solution)/shard_map/mask_gradient/pallas_call | solution.py:579
  72.8 1.0 copy-done.2
  73.7 0.0 collective-permute-done.8
  73.8 1.8 %collective-permute-start.13 = (bf16[128,512]{1,0:T(8,128)(2,1)S(1)}, bf16[128,512]{1,0:T(8,128)(2,1)S(1)}, u32[]{:S(2)}, u32[]{:S(2)}) collective-permute-start(bf16[128,512]{1,0:T(8,128)(2,1)S(1)} %pad_maximum_fusion.1), channel_id=1, source_target_pairs={{0,4},{1,5},{2,6},{3,7},{4,0},{5,1},{6,2},{7,3},{8,12},{9,13},{10,... | collective-permute-start | bytes 393224 | tf_op jit(solution)/shard_map/ppermute | solution.py:493
  75.6 1.9 %collective-permute-start.10 = (bf16[320,128]{1,0:T(8,128)(2,1)S(1)}, bf16[320,128]{1,0:T(8,128)(2,1)S(1)}, u32[]{:S(2)}, u32[]{:S(2)}) collective-permute-start(bf16[320,128]{1,0:T(8,128)(2,1)S(1)} %get-tuple-element.47), channel_id=1, source_target_pairs={{8,16},{24,32},{40,48},{72,80},{88,96},{104,112},{136,144},{152,16... | collective-permute-start | bytes 245768 | tf_op jit(solution)/shard_map/ppermute | solution.py:592
  77.5 2.6 %collective-permute-start.9 = (bf16[320,128]{1,0:T(8,128)(2,1)S(1)}, bf16[320,128]{1,0:T(8,128)(2,1)S(1)}, u32[]{:S(2)}, u32[]{:S(2)}) collective-permute-start(bf16[320,128]{1,0:T(8,128)(2,1)S(1)} %get-tuple-element.46), channel_id=1, source_target_pairs={{0,8},{8,0},{16,24},{24,16},{32,40},{40,32},{48,56},{56,48},{64,72... | collective-permute-start | bytes 245768 | tf_op jit(solution)/shard_map/ppermute | solution.py:591
  80.1 0.0 collective-permute-start.11
  80.1 3.6 %collective-permute-done.11 = f32[8,128]{1,0:T(8,128)S(1)} collective-permute-done((f32[8,128]{1,0:T(8,128)S(1)}, f32[8,128]{1,0:T(8,128)S(1)}, u32[]{:S(2)}, u32[]{:S(2)}) %collective-permute-start.11) | collective-permute-done | bytes 4128 | tf_op jit(solution)/shard_map/ppermute | solution.py:497
  83.7 1.3 %collective-permute-start.12 = (f32[8,128]{1,0:T(8,128)S(1)}, f32[8,128]{1,0:T(8,128)S(1)}, u32[]{:S(2)}, u32[]{:S(2)}) collective-permute-start(f32[8,128]{1,0:T(8,128)S(1)} %add.91), channel_id=1, source_target_pairs={{0,32},{8,40},{16,48},{24,56},{32,0},{40,8},{48,16},{56,24},{64,96... | collective-permute-start | bytes 12296 | tf_op jit(solution)/shard_map/ppermute | solution.py:497
  84.9 3.2 %collective-permute-done.12 = f32[8,128]{1,0:T(8,128)S(1)} collective-permute-done((f32[8,128]{1,0:T(8,128)S(1)}, f32[8,128]{1,0:T(8,128)S(1)}, u32[]{:S(2)}, u32[]{:S(2)}) %collective-permute-start.12) | collective-permute-done | bytes 4128 | tf_op jit(solution)/shard_map/ppermute | solution.py:497
  88.2 0.6 add.92.weight_at
  88.8 0.0 collective-permute-done.10.side_2_at
  88.8 0.0 collective-permute-done.9.side_1_at
  88.8 0.0 collective-permute-done.13
  88.9 0.6 copy-done.8
  89.4 0.0 copy-done.9
  89.5 1.8 %row_rims.1 = bf16[80,512]{1,0:T(8,128)(2,1)} custom-call(f32[128,512]{1,0:T(8,128)} %copy-done.4, bf16[320,128]{1,0:T(8,128)(2,1)} %copy-done.9, bf16[320,128]{1,0:T(8,128)(2,1)} %copy-done.8, f32[8,128]{1,0:T(8,128)} %add.92.weight_at), custom_call_target="tpu_custom_call" | custom-call | tf_op jit(solution)/shard_map/row_rims/pallas_call | solution.py:596
  91.3 1.4 %collective-permute-start.17 = (bf16[256,512]{1,0:T(8,128)(2,1)S(1)}, bf16[256,512]{1,0:T(8,128)(2,1)S(1)}, u32[]{:S(2)}, u32[]{:S(2)}) collective-permute-start(bf16[256,512]{1,0:T(8,128)(2,1)S(1)} %pad_maximum_fusion.near_at), channel_id=1, source_target_pairs={{0,1},{1,0},{2,3},{3,2},{4,5},{5,4},{6,7},{7,6},{8,9},{9,8},{10,11... | collective-permute-start | bytes 786440 | tf_op jit(solution)/shard_map/ppermute | solution.py:493
  92.7 5.7 %collective-permute-start.14 = (bf16[80,512]{1,0:T(8,128)(2,1)}, bf16[80,512]{1,0:T(8,128)(2,1)S(1)}, u32[]{:S(2)}, u32[]{:S(2)}) collective-permute-start(bf16[80,512]{1,0:T(8,128)(2,1)} %row_rims.1), channel_id=1, source_target_pairs={{0,64},{8,72},{16,80},{24,88},{32,96},{40,104},{48,112},{56,120},{... | collective-permute-start | bytes 245768 | tf_op jit(solution)/shard_map/ppermute | solution.py:612
  98.4 3.8 %collective-permute-done.14.mine_at = bf16[80,512]{1,0:T(8,128)(2,1)S(1)} collective-permute-done((bf16[80,512]{1,0:T(8,128)(2,1)}, bf16[80,512]{1,0:T(8,128)(2,1)S(1)}, u32[]{:S(2)}, u32[]{:S(2)}) %collective-permute-start.14) | collective-permute-done | bytes 81952 | tf_op jit(solution)/shard_map/ppermute | solution.py:612
  102.2 1.8 %collective-permute-start.15 = (bf16[80,512]{1,0:T(8,128)(2,1)S(1)}, bf16[80,512]{1,0:T(8,128)(2,1)S(1)}, u32[]{:S(2)}, u32[]{:S(2)}) collective-permute-start(bf16[80,512]{1,0:T(8,128)(2,1)S(1)} %collective-permute-done.14.mine_at), channel_id=1, source_target_pairs={{0,2},{1,3},{2,0},{3,1},{4,6},{5,7},{6,4},{7,5},{8,10},{9,11},{10,... | collective-permute-start | bytes 245768 | tf_op jit(solution)/shard_map/ppermute | solution.py:493
  104.0 1.4 %collective-permute-start.16 = (f32[8,128]{1,0:T(8,128)S(1)}, f32[8,128]{1,0:T(8,128)S(1)}, u32[]{:S(2)}, u32[]{:S(2)}) collective-permute-start(f32[8,128]{1,0:T(8,128)S(1)} %copy-done.17), channel_id=1, source_target_pairs={{0,128},{8,136},{16,144},{24,152},{32,160},{40,168},{48,176},{56,1... | collective-permute-start | bytes 12296 | tf_op jit(solution)/shard_map/ppermute | solution.py:497
  105.4 2.2 %collective-permute-done.16.other_at = f32[8,128]{1,0:T(8,128)S(1)} collective-permute-done((f32[8,128]{1,0:T(8,128)S(1)}, f32[8,128]{1,0:T(8,128)S(1)}, u32[]{:S(2)}, u32[]{:S(2)}) %collective-permute-start.16) | collective-permute-done | bytes 4128 | tf_op jit(solution)/shard_map/ppermute | solution.py:497
  107.6 0.0 collective-permute-done.15.theirs_at
  107.7 0.0 collective-permute-done.17.far_at
  107.7 0.6 copy-done.19
  108.2 0.0 copy-done.14
  108.3 0.1 copy-done.11
  108.4 3.2 %new_mask.1 = (f32[1,512,512]{2,1,0:T(8,128)}, f32[1,512,512]{2,1,0:T(8,128)}, f32[8,128]{1,0:T(8,128)}) custom-call(f32[512,512]{1,0:T(8,128)} %copy-done.2, bf16[320,128]{1,0:T(8,128)(2,1)} %copy-done.9, bf16[320,128]{1,0:T(8,128)(2,1)} %copy-done.8, bf16[80,512]{1,0:T(8,128)(2,1)} %copy-done.13, bf16[80,512]{1,0:T(8,128)(2,1)} %copy-done.14, ...), custom_call_target="tpu_custom_call" | custom-call | tf_op jit(solution)/shard_map/new_mask/pallas_call | solution.py:616
  111.6 0.0 copy-start.21
  111.6 0.6 copy-done.21
  112.3 1.3 %bitcast_subtract_fusion = f32[8]{0:T(128)} fusion(f32[8]{0:T(128)S(1)} %copy-done.21, f32[8,128]{1,0:T(8,128)} %get-tuple-element.59, s32[]{:T(128)S(6)} %select_n.28), kind=kLoop, calls=%fused_computation.25 | loop fusion | flops 16 | bytes 100 | tf_op jit(solution)/shard_map/sub | solution.py:638
  (48 shorter events, 0.2 us)
Async XLA Ops:
  3.3 13.0 %copy-start.18 = (bf16[16,512]{1,0:T(8,128)(2,1)S(1)}, bf16[16,512]{1,0:T(8,128)(2,1)}, u32[]{:S(2)}) copy-start(bf16[16,512]{1,0:T(8,128)(2,1)} %get-tuple-element.33) | copy-start | bytes 49156
  3.3 13.0 %collective-permute-start = (bf16[80,512]{1,0:T(8,128)(2,1)}, bf16[80,512]{1,0:T(8,128)(2,1)S(1)}, u32[]{:S(2)}, u32[]{:S(2)}) collective-permute-start(bf16[80,512]{1,0:T(8,128)(2,1)} %get-tuple-element.32), channel_id=1, source_target_pairs={{0,68},{8,76},{16,84},{24,92},{32,100},{40,108},{48,116},{56,124},... | collective-permute-start | bytes 245768 | tf_op jit(solution)/shard_map/ppermute | solution.py:521
  16.3 4.5 %copy-start.6 = (bf16[80,512]{1,0:T(8,128)(2,1)}, bf16[80,512]{1,0:T(8,128)(2,1)S(1)}, u32[]{:S(2)}) copy-start(bf16[80,512]{1,0:T(8,128)(2,1)S(1)} %pad_maximum_fusion.2.mine_at.vert_1_at) | copy-start | bytes 245764
  16.3 4.5 %collective-permute-start.1 = (bf16[80,512]{1,0:T(8,128)(2,1)S(1)}, bf16[80,512]{1,0:T(8,128)(2,1)S(1)}, u32[]{:S(2)}, u32[]{:S(2)}) collective-permute-start(bf16[80,512]{1,0:T(8,128)(2,1)S(1)} %pad_maximum_fusion.2.mine_at.vert_1_at), channel_id=1, source_target_pairs={{0,2},{1,3},{2,0},{3,1},{4,6},{5,7},{6,4},{7,5},{8,10},{9,11},{10,... | collective-permute-start | bytes 245768 | tf_op jit(solution)/shard_map/ppermute | solution.py:493
  20.9 0.6 copy-start.10
  23.3 6.6 %copy-start.20 = (f32[8,128]{1,0:T(8,128)S(1)}, f32[8,128]{1,0:T(8,128)}, u32[]{:S(2)}) copy-start(f32[8,128]{1,0:T(8,128)} %get-tuple-element.36) | copy-start | bytes 12292
  23.3 6.6 %collective-permute-start.2 = (bf16[336,128]{1,0:T(8,128)(2,1)}, bf16[336,128]{1,0:T(8,128)(2,1)S(1)}, u32[]{:S(2)}, u32[]{:S(2)}) collective-permute-start(bf16[336,128]{1,0:T(8,128)(2,1)} %get-tuple-element.37), channel_id=1, source_target_pairs={{0,9},{8,1},{16,25},{24,17},{32,41},{40,33},{48,57},{56,49},{64,73... | collective-permute-start | bytes 258056 | tf_op jit(solution)/shard_map/ppermute | solution.py:532
  23.4 7.5 %collective-permute-start.3 = (bf16[320,128]{1,0:T(8,128)(2,1)}, bf16[320,128]{1,0:T(8,128)(2,1)S(1)}, u32[]{:S(2)}, u32[]{:S(2)}) collective-permute-start(bf16[320,128]{1,0:T(8,128)(2,1)} %get-tuple-element.38), channel_id=1, source_target_pairs={{8,16},{24,32},{40,48},{72,80},{88,96},{104,112},{136,144},{152,16... | collective-permute-start | bytes 245768 | tf_op jit(solution)/shard_map/ppermute | solution.py:533
  29.8 1.0 copy-start.12
  30.8 0.6 copy-start.15
  50.3 5.7 %collective-permute-start.4 = (bf16[112,512]{1,0:T(8,128)(2,1)}, bf16[112,512]{1,0:T(8,128)(2,1)S(1)}, u32[]{:S(2)}, u32[]{:S(2)}) collective-permute-start(bf16[112,512]{1,0:T(8,128)(2,1)} %get-tuple-element.39), channel_id=1, source_target_pairs={{0,2},{1,3},{2,0},{3,1},{4,6},{5,7},{6,4},{7,5},{8,10},{9,11},{10,... | collective-permute-start | bytes 344072 | tf_op jit(solution)/shard_map/ppermute | solution.py:493
  51.8 1.0 copy-start.16
  51.8 4.3 %copy-start.7 = (bf16[112,512]{1,0:T(8,128)(2,1)S(1)}, bf16[112,512]{1,0:T(8,128)(2,1)}, u32[]{:S(2)}) copy-start(bf16[112,512]{1,0:T(8,128)(2,1)} %get-tuple-element.39) | copy-start | bytes 344068
  52.8 18.7 %copy-start = (f32[1,512,512]{2,1,0:T(8,128)S(1)}, f32[1,512,512]{2,1,0:T(8,128)}, u32[]{:S(2)}) copy-start(f32[1,512,512]{2,1,0:T(8,128)} %mask.1) | copy-start | bytes 3145732
  52.8 5.1 %collective-permute-start.5 = (bf16[64,512]{1,0:T(8,128)(2,1)S(1)}, bf16[64,512]{1,0:T(8,128)(2,1)S(1)}, u32[]{:S(2)}, u32[]{:S(2)}) collective-permute-start(bf16[64,512]{1,0:T(8,128)(2,1)S(1)} %copy-done.16), channel_id=1, source_target_pairs={{0,2},{1,3},{2,0},{3,1},{4,6},{5,7},{6,4},{7,5},{8,10},{9,11},{10,... | collective-permute-start | bytes 196616 | tf_op jit(solution)/shard_map/ppermute | solution.py:493
  56.2 15.2 %copy-start.1 = (bf16[512,640]{1,0:T(8,128)(2,1)S(1)}, bf16[512,640]{1,0:T(8,128)(2,1)}, u32[]{:S(2)}) copy-start(bf16[512,640]{1,0:T(8,128)(2,1)} %constant.36.clone.freq_at.freq) | copy-start | bytes 1966084
  57.9 6.7 %collective-permute-start.6 = (bf16[112,512]{1,0:T(8,128)(2,1)S(1)}, bf16[112,512]{1,0:T(8,128)(2,1)S(1)}, u32[]{:S(2)}, u32[]{:S(2)}) collective-permute-start(bf16[112,512]{1,0:T(8,128)(2,1)S(1)} %select_convert_fusion.1), channel_id=1, source_target_pairs={{0,4},{1,5},{2,6},{3,7},{4,0},{5,1},{6,2},{7,3},{8,12},{9,13},{10,... | collective-permute-start | bytes 344072 | tf_op jit(solution)/shard_map/ppermute | solution.py:493
  64.6 6.9 %copy-start.3 = (bf16[640,224]{1,0:T(8,128)(2,1)S(1)}, bf16[640,224]{1,0:T(8,128)(2,1)}, u32[]{:S(2)}) copy-start(bf16[640,224]{1,0:T(8,128)(2,1)} %constant.40.clone.fold_t) | copy-start | bytes 860164
  64.8 6.4 %collective-permute-start.7 = (bf16[112,512]{1,0:T(8,128)(2,1)S(1)}, bf16[112,512]{1,0:T(8,128)(2,1)S(1)}, u32[]{:S(2)}, u32[]{:S(2)}) collective-permute-start(bf16[112,512]{1,0:T(8,128)(2,1)S(1)} %select_convert_fusion.part_1), channel_id=1, source_target_pairs={{0,1},{1,0},{2,3},{3,2},{4,5},{5,4},{6,7},{7,6},{8,9},{9,8},{10,11... | collective-permute-start | bytes 344072 | tf_op jit(solution)/shard_map/ppermute | solution.py:493
  71.2 2.6 %collective-permute-start.8 = (f32[8,128]{1,0:T(8,128)S(1)}, f32[8,128]{1,0:T(8,128)S(1)}, u32[]{:S(2)}, u32[]{:S(2)}) collective-permute-start(f32[8,128]{1,0:T(8,128)S(1)} %broadcast_in_dim.69), channel_id=1, source_target_pairs={{0,8},{8,0},{16,24},{24,16},{32,40},{40,32},{48,56},{56,48},{64,72... | collective-permute-start | bytes 12296 | tf_op jit(solution)/shard_map/ppermute | solution.py:497
  72.7 1.0 copy-start.2
  73.7 15.1 %copy-start.4 = (f32[128,512]{1,0:T(8,128)}, f32[128,512]{1,0:T(8,128)S(1)}, u32[]{:S(2)}) copy-start(f32[128,512]{1,0:T(8,128)S(1)} %get-tuple-element.52.rims_at) | copy-start | bytes 786436
  73.8 15.1 %collective-permute-start.13 = (bf16[128,512]{1,0:T(8,128)(2,1)S(1)}, bf16[128,512]{1,0:T(8,128)(2,1)S(1)}, u32[]{:S(2)}, u32[]{:S(2)}) collective-permute-start(bf16[128,512]{1,0:T(8,128)(2,1)S(1)} %pad_maximum_fusion.1), channel_id=1, source_target_pairs={{0,4},{1,5},{2,6},{3,7},{4,0},{5,1},{6,2},{7,3},{8,12},{9,13},{10,... | collective-permute-start | bytes 393224 | tf_op jit(solution)/shard_map/ppermute | solution.py:493
  75.6 13.2 %collective-permute-start.10 = (bf16[320,128]{1,0:T(8,128)(2,1)S(1)}, bf16[320,128]{1,0:T(8,128)(2,1)S(1)}, u32[]{:S(2)}, u32[]{:S(2)}) collective-permute-start(bf16[320,128]{1,0:T(8,128)(2,1)S(1)} %get-tuple-element.47), channel_id=1, source_target_pairs={{8,16},{24,32},{40,48},{72,80},{88,96},{104,112},{136,144},{152,16... | collective-permute-start | bytes 245768 | tf_op jit(solution)/shard_map/ppermute | solution.py:592
  77.5 11.3 %collective-permute-start.9 = (bf16[320,128]{1,0:T(8,128)(2,1)S(1)}, bf16[320,128]{1,0:T(8,128)(2,1)S(1)}, u32[]{:S(2)}, u32[]{:S(2)}) collective-permute-start(bf16[320,128]{1,0:T(8,128)(2,1)S(1)} %get-tuple-element.46), channel_id=1, source_target_pairs={{0,8},{8,0},{16,24},{24,16},{32,40},{40,32},{48,56},{56,48},{64,72... | collective-permute-start | bytes 245768 | tf_op jit(solution)/shard_map/ppermute | solution.py:591
  80.1 3.6 %collective-permute-start.11 = (f32[8,128]{1,0:T(8,128)S(1)}, f32[8,128]{1,0:T(8,128)S(1)}, u32[]{:S(2)}, u32[]{:S(2)}) collective-permute-start(f32[8,128]{1,0:T(8,128)S(1)} %broadcast_add_fusion), channel_id=1, source_target_pairs={{0,16},{8,24},{16,0},{24,8},{32,48},{40,56},{48,32},{56,40},{64,80... | collective-permute-start | bytes 12296 | tf_op jit(solution)/shard_map/ppermute | solution.py:497
  83.7 4.5 %collective-permute-start.12 = (f32[8,128]{1,0:T(8,128)S(1)}, f32[8,128]{1,0:T(8,128)S(1)}, u32[]{:S(2)}, u32[]{:S(2)}) collective-permute-start(f32[8,128]{1,0:T(8,128)S(1)} %add.91), channel_id=1, source_target_pairs={{0,32},{8,40},{16,48},{24,56},{32,0},{40,8},{48,16},{56,24},{64,96... | collective-permute-start | bytes 12296 | tf_op jit(solution)/shard_map/ppermute | solution.py:497
  88.8 0.6 copy-start.8
  88.8 0.7 copy-start.9
  89.5 16.0 %copy-start.5 = (bf16[256,512]{1,0:T(8,128)(2,1)}, bf16[256,512]{1,0:T(8,128)(2,1)S(1)}, u32[]{:S(2)}) copy-start(bf16[256,512]{1,0:T(8,128)(2,1)S(1)} %pad_maximum_fusion.near_at) | copy-start | bytes 786436
  89.5 14.6 %copy-start.17 = (f32[8,128]{1,0:T(8,128)S(1)}, f32[8,128]{1,0:T(8,128)}, u32[]{:S(2)}) copy-start(f32[8,128]{1,0:T(8,128)} %add.92.weight_at) | copy-start | bytes 12292
  91.3 16.4 %collective-permute-start.17 = (bf16[256,512]{1,0:T(8,128)(2,1)S(1)}, bf16[256,512]{1,0:T(8,128)(2,1)S(1)}, u32[]{:S(2)}, u32[]{:S(2)}) collective-permute-start(bf16[256,512]{1,0:T(8,128)(2,1)S(1)} %pad_maximum_fusion.near_at), channel_id=1, source_target_pairs={{0,1},{1,0},{2,3},{3,2},{4,5},{5,4},{6,7},{7,6},{8,9},{9,8},{10,11... | collective-permute-start | bytes 786440 | tf_op jit(solution)/shard_map/ppermute | solution.py:493
  92.7 9.5 %collective-permute-start.14 = (bf16[80,512]{1,0:T(8,128)(2,1)}, bf16[80,512]{1,0:T(8,128)(2,1)S(1)}, u32[]{:S(2)}, u32[]{:S(2)}) collective-permute-start(bf16[80,512]{1,0:T(8,128)(2,1)} %row_rims.1), channel_id=1, source_target_pairs={{0,64},{8,72},{16,80},{24,88},{32,96},{40,104},{48,112},{56,120},{... | collective-permute-start | bytes 245768 | tf_op jit(solution)/shard_map/ppermute | solution.py:612
  102.2 5.4 %copy-start.13 = (bf16[80,512]{1,0:T(8,128)(2,1)}, bf16[80,512]{1,0:T(8,128)(2,1)S(1)}, u32[]{:S(2)}) copy-start(bf16[80,512]{1,0:T(8,128)(2,1)S(1)} %collective-permute-done.14.mine_at) | copy-start | bytes 245764
  102.2 5.4 %collective-permute-start.15 = (bf16[80,512]{1,0:T(8,128)(2,1)S(1)}, bf16[80,512]{1,0:T(8,128)(2,1)S(1)}, u32[]{:S(2)}, u32[]{:S(2)}) collective-permute-start(bf16[80,512]{1,0:T(8,128)(2,1)S(1)} %collective-permute-done.14.mine_at), channel_id=1, source_target_pairs={{0,2},{1,3},{2,0},{3,1},{4,6},{5,7},{6,4},{7,5},{8,10},{9,11},{10,... | collective-permute-start | bytes 245768 | tf_op jit(solution)/shard_map/ppermute | solution.py:493
  104.0 3.6 %collective-permute-start.16 = (f32[8,128]{1,0:T(8,128)S(1)}, f32[8,128]{1,0:T(8,128)S(1)}, u32[]{:S(2)}, u32[]{:S(2)}) collective-permute-start(f32[8,128]{1,0:T(8,128)S(1)} %copy-done.17), channel_id=1, source_target_pairs={{0,128},{8,136},{16,144},{24,152},{32,160},{40,168},{48,176},{56,1... | collective-permute-start | bytes 12296 | tf_op jit(solution)/shard_map/ppermute | solution.py:497
  107.6 0.6 copy-start.19
  107.6 0.6 copy-start.14
  107.7 0.8 copy-start.11
  111.6 0.7 copy-start.21

commit v3 on v2

--- a/solution.py
+++ b/solution.py
@@ -129,23 +129,19 @@
     side_2[...] = jnp.where(col_odd, after, before).astype(BF)
 
 
-def corner_kernel(mine_at, theirs_at, side_1_at, side_2_at, send_1, send_2, info_out, held, sems):
+def corner_kernel(mine, theirs, side_1, side_2, send_1, send_2, info_out):
     _k, _row_odd, col_odd, _inner, _second = where_am_i()
     wide = 2 * HALO
     half = TS // 2
-    ends = (pl.ds(0, wide), pl.ds(TS - wide, wide))
-    copies = fetch_all(
-        [(got.at[:, end], held.at[2 * n + m]) for n, got in enumerate((mine_at, theirs_at)) for m, end in enumerate(ends)]
-        + [(side_1_at, send_1.at[pl.ds(0, half), :]), (side_2_at, send_2.at[pl.ds(0, half), :])],
-        sems,
-    )
+    ends = (slice(0, wide), slice(TS - wide, TS))
+    send_1[:half] = side_1[...]
+    send_2[:half] = side_2[...]
     first = lax.broadcasted_iota(jnp.int32, (HALO, wide), 1) < HALO
-    wait_all(copies)
 
     def above_below(m):
-        return arrived(held[m, :HALO], held[2 + m, :HALO])
-
-    info = held[0, HALO:].astype(F32) + held[2, HALO:].astype(F32)
+        return arrived(mine[:HALO, ends[m]], theirs[:HALO, ends[m]])
+
+    info = mine[HALO:, :wide].astype(F32) + theirs[HALO:, :wide].astype(F32)
     info_out[...] = info[:8]
     send_1[NE // 2 :] = info.astype(BF)
     above, below = above_below(0)
@@ -157,10 +153,10 @@
 
 
 def source_kernel(
-    info, vert_1_at, vert_2_at, side_1_at, side_2_at,
+    info, mine, theirs, side_1, side_2,
     mask_at, target_at, pupil_at, freq_at, back_t_at, back_at, rows_at, rows_t_at,
     dspec_out, resist_out,
-    spec, amps_a, amps_b, fields, image, dspec, terms, vert_1, vert_2, side_1, side_2,
+    spec, amps_a, amps_b, fields, image, dspec, terms,
     mask, freq, back_t, back, own_rows, rows_turned, pupil, bits, sems,
 ):
     step = resist_out.shape[0]
@@ -168,8 +164,6 @@
     own = pl.ds(pl.multiple_of(k * step, step), step)
     copies = fetch_all(
         (
-            (vert_1_at.at[pl.ds(0, HALO), :], vert_1), (vert_2_at.at[pl.ds(0, HALO), :], vert_2),
-            (side_1_at.at[pl.ds(0, NE // 2), :], side_1), (side_2_at, side_2),
             (freq_at, freq), (mask_at.at[0], mask), (pupil_at, pupil),
             (rows_at.at[own, :], own_rows), (back_t_at, back_t), (target_at.at[0, own, :], bits),
             (back_at, back), (rows_t_at.at[k], rows_turned),
@@ -179,10 +173,10 @@
     image[...] = jnp.zeros_like(image)
     dspec[...] = jnp.zeros_like(dspec)
     terms[...] = jnp.zeros_like(terms)
-    wait_all(copies[:6])
-
-    halo_rows = jnp.concatenate(arrived(vert_1[...], vert_2[...]), 0).astype(BF)
-    s1, s2 = side_1[...].astype(F32), side_2[...].astype(F32)
+    wait_all(copies[:2])
+
+    halo_rows = jnp.concatenate(arrived(mine[:HALO], theirs[:HALO]), 0).astype(BF)
+    s1, s2 = side_1[: NE // 2].astype(F32), side_2[...].astype(F32)
     left, right = jnp.where(col_odd, s1, s2), jnp.where(col_odd, s2, s1)
     first = lax.broadcasted_iota(jnp.int32, left.shape, 1) < HALO
     one = jnp.where(first, left, pltpu.roll(right, HALO, 1)).astype(BF)
@@ -199,7 +193,7 @@
     for j in range(4):
         spec[j] = whole[:, j * 128 : (j + 1) * 128]
 
-    wait_all(copies[6:9])
+    wait_all(copies[2:5])
     gain = pupil[...].astype(F32).astype(BF)
     sources = info.shape[0] * 8
 
@@ -249,7 +243,7 @@
 
     lax.fori_loop(0, batches // 2, forward_pair, 0)
 
-    wait_all(copies[9:])
+    wait_all(copies[5:])
     resist = jax.nn.sigmoid(steepness * (image[...] * (1.0 / sources) - threshold))
     resist_out[...] = resist.astype(BF)
     image[...] = 2.0 * (resist - bits[...].astype(F32)) * resist * (1.0 - resist) * steepness
@@ -403,17 +397,10 @@
     return left, right
 
 
-def rim_kernel(rims_at, side_1_at, side_2_at, weight_at, vert_out, rims, side_1, side_2, weight, sems):
+def rim_kernel(rims_in, side_1, side_2, weight, vert_out, rims):
     _k, row_odd, _col_odd, _inner, second = where_am_i()
-    corner = pl.ds(TS // 2, HALO)
-    copies = fetch_all(
-        (
-            (rims_at, rims), (side_1_at.at[corner, :], side_1), (side_2_at.at[corner, :], side_2), (weight_at, weight),
-        ),
-        sems,
-    )
-    wait_all(copies)
-    left, right = from_sides(side_1[...], side_2[...])
+    rims[...] = rims_in[...]
+    left, right = from_sides(side_1[TS // 2 :], side_2[TS // 2 :])
     wide = 2 * HALO
     for n in range(2):
         rows = slice(n * HALO, (n + 1) * HALO)
@@ -424,30 +411,20 @@
 
 
 def final_kernel(
-    base_at, side_1_at, side_2_at, mine_at, theirs_at, weight_at, other_at, near_at, far_at,
-    mask_at, resist_at, weight_out,
-    base, side_1, side_2, mine, theirs, weight, other, near, far, resist, sems,
+    base_in, side_1, side_2, mine, theirs, weight, other, near, far, source_weights,
+    mask_at, resist_at, weights_out, base, resist, sems,
 ):
     k, _row_odd, _col_odd, _inner, second = where_am_i()
     step = near.shape[0] // 4
     half = TS // 2
-    inside = (pl.ds(0, half), slice(None))
-    copies = fetch_all(
-        (
-            (near_at, near), (far_at, far), (base_at, base), (side_1_at.at[inside], side_1),
-            (side_2_at.at[inside], side_2), (mine_at, mine), (theirs_at, theirs), (weight_at, weight), (other_at, other),
-        ),
-        sems,
-    )
-    wait_all(copies[:2])
     for m in range(8):
         piece = (near, far)[m % 2][m // 2 * step : (m // 2 + 1) * step, :]
         at = lax.bitwise_xor(k, m)
         resist[pl.ds(pl.multiple_of(at * step, step), step), :] = piece.astype(F32)
     resist_done = pltpu.make_async_copy(resist, resist_at.at[0], sems.at[0])
     resist_done.start()
-    wait_all(copies[2:])
-    left, right = from_sides(side_1[...], side_2[...])
+    base[...] = base_in[...]
+    left, right = from_sides(side_1[:half], side_2[:half])
     wide = 2 * HALO
     for n in range(2):
         rows = slice(n * half, (n + 1) * half)
@@ -460,7 +437,11 @@
     mask_done.start()
     from_1, from_2 = weight_sums(mine[HALO:, :128].astype(F32)), weight_sums(theirs[HALO:, :128].astype(F32))
     from_1, from_2 = jnp.where(second, from_2, from_1), jnp.where(second, from_1, from_2)
-    weight_out[...] = jnp.broadcast_to((weight[:1] + from_1) + (from_2 + other[:1]), weight_out.shape)
+    total = (weight[:1] + from_1) + (from_2 + other[:1])
+    own = source_weights.shape[1]
+    total = pltpu.roll(jnp.broadcast_to(total, (8, 128)), lax.bitwise_and(128 - own * k, 127), 1)
+    tiles = lax.axis_size("tile")
+    weights_out[...] = source_weights[...] - source_rate * total[:1, :own] / (TS * TS * tiles)
     mask_done.wait()
     resist_done.wait()
 
@@ -524,9 +505,8 @@
     side_1, side_2, info = pl.pallas_call(
         corner_kernel,
         out_shape=(shaped((NE // 2 + 16, 128), BF), shaped((NE // 2, 128), BF), shaped((8, 128), F32)),
-        in_specs=[HBM] * 4,
+        in_specs=[VMEM] * 4,
         out_specs=(VMEM,) * 3,
-        scratch_shapes=[pltpu.VMEM((4, HALO + 16, 2 * HALO), BF), pltpu.SemaphoreType.DMA((6,))],
         name="corners",
     )(mine, theirs, side_1, side_2)
     side_1 = lax.ppermute(side_1, ("tile", "src"), route_of(col_swap, col_swap, groups, 1))
@@ -536,7 +516,7 @@
     part, resist = pl.pallas_call(
         source_kernel,
         out_shape=(shaped((ROWS, 2 * HALF), BF), shaped((step, TS), BF)),
-        in_specs=[SMEM] + [HBM] * 12,
+        in_specs=[SMEM] + [VMEM] * 4 + [HBM] * 8,
         out_specs=(VMEM, VMEM),
         scratch_shapes=[
             pltpu.VMEM((4, SPAN, 128), F32),
@@ -546,10 +526,6 @@
             pltpu.VMEM((step, TS), F32),
             pltpu.VMEM((8, SPAN, 128), F32),
             pltpu.VMEM((128, 8, 128), F32),
-            pltpu.VMEM((HALO, TS), BF),
-            pltpu.VMEM((HALO, TS), BF),
-            pltpu.VMEM((NE // 2, 128), BF),
-            pltpu.VMEM((NE // 2, 128), BF),
             pltpu.VMEM((TS, TS), F32),
             pltpu.VMEM((2 * HALF, NE), BF),
             pltpu.VMEM((2 * BAND, 2 * TS), BF),
@@ -558,7 +534,7 @@
             pltpu.VMEM((BAND, 2 * step), BF),
             pltpu.VMEM((BAND, BAND), jnp.int32),
             pltpu.VMEM((step, TS), jnp.int32),
-            pltpu.SemaphoreType.DMA((12,)),
+            pltpu.SemaphoreType.DMA((8,)),
         ],
         compiler_params=pltpu.CompilerParams(vmem_limit_bytes=60 << 20),
         name="sources",
@@ -569,9 +545,9 @@
 
     other = src_swap(part, 2, groups)
     near = src_swap(resist, 2, groups)
+    part = add(part, other)
+    other = src_swap(part, 4, groups)
     part, near = lax.optimization_barrier((add(part, other), near))
-    other = src_swap(part, 4, groups)
-    part = add(part, other)
     other = src_swap(part, 1, groups)
     weight = weight_sums(part[FOLD:, :128].astype(F32)) + weight_sums(other[FOLD:, :128].astype(F32))
     weight = jnp.broadcast_to(weight, (8, 128))
@@ -596,15 +572,9 @@
     rim = pl.pallas_call(
         rim_kernel,
         out_shape=shaped((HALO + 16, TS), BF),
-        in_specs=[HBM] * 4,
+        in_specs=[VMEM] * 4,
         out_specs=VMEM,
-        scratch_shapes=[
-            pltpu.VMEM((2 * HALO, TS), F32),
-            pltpu.VMEM((HALO, 128), BF),
-            pltpu.VMEM((HALO, 128), BF),
-            pltpu.VMEM((8, 128), F32),
-            pltpu.SemaphoreType.DMA((4,)),
-        ],
+        scratch_shapes=[pltpu.VMEM((2 * HALO, TS), F32)],
         name="row_rims",
     )(rims, side_1, side_2, weight)
     near = jnp.concatenate([near, far], 0)
@@ -613,30 +583,21 @@
     other = tile_swap(weight, 2 * columns, tiles)
     far = src_swap(near, 1, groups)
     theirs = src_swap(mine, 2, groups)
-    new_mask, resist_tile, terms = pl.pallas_call(
+    new_mask, resist_tile, new_weights = pl.pallas_call(
         final_kernel,
-        out_shape=(shaped((1, TS, TS), F32),) * 2 + (shaped((8, 128), F32),),
-        in_specs=[HBM] * 9,
+        out_shape=(shaped((1, TS, TS), F32),) * 2 + (shaped((1, own), F32),),
+        in_specs=[VMEM] * 10,
         out_specs=(HBM, HBM, VMEM),
         scratch_shapes=[
             pltpu.VMEM((TS, TS), F32),
-            pltpu.VMEM((TS // 2, 128), BF),
-            pltpu.VMEM((TS // 2, 128), BF),
-            pltpu.VMEM((HALO + 16, TS), BF),
-            pltpu.VMEM((HALO + 16, TS), BF),
-            pltpu.VMEM((8, 128), F32),
-            pltpu.VMEM((8, 128), F32),
-            pltpu.VMEM((4 * step, TS), BF),
-            pltpu.VMEM((4 * step, TS), BF),
             pltpu.VMEM((TS, TS), F32),
-            pltpu.SemaphoreType.DMA((9,)),
+            pltpu.SemaphoreType.DMA((2,)),
         ],
+        compiler_params=pltpu.CompilerParams(vmem_limit_bytes=24 << 20),
         name="new_mask",
-    )(base, side_1, side_2, mine, theirs, weight, other, near, far)
-
-    weight_total = lax.dynamic_slice(terms, (0, k * own), (1, own))[0]
-    new_weights = source_weights - source_rate * weight_total / (TS * TS * tiles)
-    return (new_mask, new_weights, resist_tile)
+    )(base, side_1, side_2, mine, theirs, weight, other, near, far, source_weights[None])
+
+    return (new_mask, new_weights[0], resist_tile)
 
 
 def solution(mesh):

time: 114 us -> 109 us (0.956)
  waiting for transfers between devices: 35.8 us -> 32.8 us
  local copies, waits for them, and re-layouts: 4.3 us -> 1.93 us
  starting transfers between devices: 39 us -> 41 us
  other arithmetic: 3.87 us -> 2.57 us
    unnamed x44 -> x36, local copies, waits for them, and re-layouts: 4.29 us -> 1.91 us
    ppermute x1, starting transfers between devices: 2.56 us -> 0.21 us  [per_device(): side_1 = lax.ppermute(side_1, 'tile', col_swap)]
    ppermute x8, starting transfers between devices: 11.6 us -> 13.6 us  [src_swap(): return lax.ppermute(block, 'src', [(i, i ^ distance) for i in range(count)])]
    ppermute x8, waiting for transfers between devices: 17.2 us -> 15.5 us  [src_swap(): return lax.ppermute(block, 'src', [(i, i ^ distance) for i in range(count)])]
    ppermute x4, starting transfers between devices: 2.95 us -> 4.34 us  [tile_swap(): lax.ppermute(block, 'tile', [(i, i ^ distance) for i in range(count)])]
    sub x1 -> x0, other arithmetic: 1.26 us -> none  [per_device(): source_weights - source_rate * weight_total / (TS * TS * tiles)]
  transfers between devices with their start and end apart: 18 -> 18, of which waited for: 12 -> 11; matrix products, arithmetic and copies ran while one was open for 2% -> 2% of each run, Pallas kernels for 1% -> 1%
where the time goes in v3:
time: 109 us; the launch traced here: 108 us
  starting transfers between devices  41 us (38%)
  waiting for transfers between devices  32.8 us (30%)
  Pallas kernels  28.4 us (26%)
  other arithmetic  2.57 us (2%)
  local copies, waits for them, and re-layouts  1.93 us (2%)
  between operations  1.12 us (1%)
    pallas_call x1, Pallas kernels, per_device(): pl.pallas_call(source_kernel, out_shape=(shaped((ROWS, 2 * HALF), BF), sh...  19 us
    ppermute x8, waiting for transfers between devices, src_swap(): return lax.ppermute(block, 'src', [(i, i ^ distance) for i in range(count)])  15.5 us
    ppermute x8, starting transfers between devices, src_swap(): return lax.ppermute(block, 'src', [(i, i ^ distance) for i in range(count)])  13.6 us
    ppermute x1, starting transfers between devices, per_device(): lax.ppermute(vert, ('tile', 'src'), route_of(row_swap, row_ring, groups, 4))  9.01 us
    ppermute x4, waiting for transfers between devices, tile_swap(): lax.ppermute(block, 'tile', [(i, i ^ distance) for i in range(count)])  8.32 us
    ppermute x2, starting transfers between devices, per_device(): side_2 = lax.ppermute(side_2, 'tile', col_next)  7.23 us
    ppermute x1, starting transfers between devices, per_device(): lax.ppermute(rim, ('tile', 'src'), route_of(row_swap, row_ring, groups))  6.58 us
    ppermute x4, starting transfers between devices, tile_swap(): lax.ppermute(block, 'tile', [(i, i ^ distance) for i in range(count)])  4.34 us
  transfers between devices with their start and end apart: 18, of which 11 were waited for; matrix products, arithmetic and copies ran while one was open for 2% of the time, Pallas kernels for 1%

profile of v3, /device:TPU:32, one launch (start us, length us, event | category | flops | bytes accessed | tf_op | source)
XLA Modules:
  0.0 107.8 jit_solution(13778032347123615437)
XLA Ops:
  0.6 2.6 %edges.1 = (bf16[80,512]{1,0:T(8,128)(2,1)}, bf16[256,128]{1,0:T(8,128)(2,1)}, bf16[256,128]{1,0:T(8,128)(2,1)}, bf16[16,512]{1,0:T(8,128)(2,1)}) custom-call(s32[2,8]{1,0:T(2,128)} %bitcast.19, f32[1,8]{1,0:T(1,128)} %bitcast.11, f32[1,512,512]{2,1,0:T(8,128)} %mask.1), custom_call_target="tpu_custom_call" | custom-call | tf_op jit(solution)/shard_map/edges/pallas_call | solution.py:492
  3.3 0.0 copy-start.16
  3.3 9.0 %collective-permute-start = (bf16[80,512]{1,0:T(8,128)(2,1)}, bf16[80,512]{1,0:T(8,128)(2,1)S(1)}, u32[]{:S(2)}, u32[]{:S(2)}) collective-permute-start(bf16[80,512]{1,0:T(8,128)(2,1)} %get-tuple-element.32), channel_id=1, source_target_pairs={{0,68},{8,76},{16,84},{24,92},{32,100},{40,108},{48,116},{56,124},... | collective-permute-start | bytes 245768 | tf_op jit(solution)/shard_map/ppermute | solution.py:502
  12.3 4.0 %collective-permute-done = bf16[80,512]{1,0:T(8,128)(2,1)S(1)} collective-permute-done((bf16[80,512]{1,0:T(8,128)(2,1)}, bf16[80,512]{1,0:T(8,128)(2,1)S(1)}, u32[]{:S(2)}, u32[]{:S(2)}) %collective-permute-start) | collective-permute-done | bytes 81952 | tf_op jit(solution)/shard_map/ppermute | solution.py:502
  16.3 0.0 copy-done.16
  16.3 0.0 copy-start.10
  16.3 1.7 %collective-permute-start.1 = (bf16[80,512]{1,0:T(8,128)(2,1)S(1)}, bf16[80,512]{1,0:T(8,128)(2,1)S(1)}, u32[]{:S(2)}, u32[]{:S(2)}) collective-permute-start(bf16[80,512]{1,0:T(8,128)(2,1)S(1)} %pad_maximum_fusion.2.mine), channel_id=1, source_target_pairs={{0,2},{1,3},{2,0},{3,1},{4,6},{5,7},{6,4},{7,5},{8,10},{9,11},{10,... | collective-permute-start | bytes 245768 | tf_op jit(solution)/shard_map/ppermute | solution.py:474
  18.0 2.8 %collective-permute-done.1.theirs = bf16[80,512]{1,0:T(8,128)(2,1)S(1)} collective-permute-done((bf16[80,512]{1,0:T(8,128)(2,1)S(1)}, bf16[80,512]{1,0:T(8,128)(2,1)S(1)}, u32[]{:S(2)}, u32[]{:S(2)}) %collective-permute-start.1) | collective-permute-done | bytes 81952 | tf_op jit(solution)/shard_map/ppermute | solution.py:474
  20.9 0.0 copy-done.10
  20.9 0.6 copy-done.12
  21.5 1.7 %corners.1 = (bf16[336,128]{1,0:T(8,128)(2,1)}, bf16[320,128]{1,0:T(8,128)(2,1)}, f32[8,128]{1,0:T(8,128)}) custom-call(bf16[80,512]{1,0:T(8,128)(2,1)} %copy-done.10, bf16[80,512]{1,0:T(8,128)(2,1)} %copy-done.12, bf16[256,128]{1,0:T(8,128)(2,1)} %get-tuple-element.34.side_1, bf16[256,128]{1,0:T(8,128)(2,1)} %get-tuple-element.35.side_2), custom_call_target="tpu_custom_call" | custom-call | tf_op jit(solution)/shard_map/corners/pallas_call | solution.py:505
  23.2 0.0 collective-permute-start.2
  23.2 5.1 %collective-permute-start.3 = (bf16[320,128]{1,0:T(8,128)(2,1)}, bf16[320,128]{1,0:T(8,128)(2,1)S(1)}, u32[]{:S(2)}, u32[]{:S(2)}) collective-permute-start(bf16[320,128]{1,0:T(8,128)(2,1)} %get-tuple-element.38), channel_id=1, source_target_pairs={{8,16},{24,32},{40,48},{72,80},{88,96},{104,112},{136,144},{152,16... | collective-permute-start | bytes 245768 | tf_op jit(solution)/shard_map/ppermute | solution.py:513
  28.3 1.4 %collective-permute-done.2.side_1 = bf16[336,128]{1,0:T(8,128)(2,1)S(1)} collective-permute-done((bf16[336,128]{1,0:T(8,128)(2,1)}, bf16[336,128]{1,0:T(8,128)(2,1)S(1)}, u32[]{:S(2)}, u32[]{:S(2)}) %collective-permute-start.2) | collective-permute-done | bytes 86048 | tf_op jit(solution)/shard_map/ppermute | solution.py:512
  29.7 0.0 copy-done.17
  29.7 0.6 convert_add_fusion.info
  30.3 0.4 collective-permute-done.3.side_2
  30.7 0.0 copy-done.13
  30.7 0.6 copy-done.14
  31.3 19.0 %sources.1 = (bf16[112,512]{1,0:T(8,128)(2,1)}, bf16[64,512]{1,0:T(8,128)(2,1)}) custom-call(f32[8,128]{1,0:T(8,128)} %convert_add_fusion.info, bf16[80,512]{1,0:T(8,128)(2,1)} %copy-done.10, bf16[80,512]{1,0:T(8,128)(2,1)} %copy-done.12, bf16[336,128]{1,0:T(8,128)(2,1)} %copy-done.13, bf16[320,128]{1,0:T(8,128)(2,1)} %copy-done.14, f32[1,512,512]{2,1,0:T(8,128)} %mask.1, ...), custom_call_target="tpu_custom_call" | custom-call | tf_op jit(solution)/shard_map/sources/pallas_call | solution.py:516
  50.3 1.4 %collective-permute-start.4 = (bf16[112,512]{1,0:T(8,128)(2,1)}, bf16[112,512]{1,0:T(8,128)(2,1)S(1)}, u32[]{:S(2)}, u32[]{:S(2)}) collective-permute-start(bf16[112,512]{1,0:T(8,128)(2,1)} %get-tuple-element.39), channel_id=1, source_target_pairs={{0,2},{1,3},{2,0},{3,1},{4,6},{5,7},{6,4},{7,5},{8,10},{9,11},{10,... | collective-permute-start | bytes 344072 | tf_op jit(solution)/shard_map/ppermute | solution.py:474
  51.7 0.0 copy-start.11
  51.7 0.0 copy-start.15
  51.7 0.0 copy-start.6
  51.7 1.0 convert_element_type.28
  52.7 0.0 copy-start
  52.7 3.3 %collective-permute-done.4 = bf16[112,512]{1,0:T(8,128)(2,1)S(1)} collective-permute-done((bf16[112,512]{1,0:T(8,128)(2,1)}, bf16[112,512]{1,0:T(8,128)(2,1)S(1)}, u32[]{:S(2)}, u32[]{:S(2)}) %collective-permute-start.4) | collective-permute-done | bytes 114720 | tf_op jit(solution)/shard_map/ppermute | solution.py:474
  56.0 0.0 copy-done.11
  56.0 0.1 fusion.8
  56.2 0.0 copy-start.1
  56.2 1.1 collective-permute-start.5
  57.3 1.7 %collective-permute-start.6 = (bf16[64,512]{1,0:T(8,128)(2,1)S(1)}, bf16[64,512]{1,0:T(8,128)(2,1)S(1)}, u32[]{:S(2)}, u32[]{:S(2)}) collective-permute-start(bf16[64,512]{1,0:T(8,128)(2,1)S(1)} %copy-done.15), channel_id=1, source_target_pairs={{0,2},{1,3},{2,0},{3,1},{4,6},{5,7},{6,4},{7,5},{8,10},{9,11},{10,... | collective-permute-start | bytes 196616 | tf_op jit(solution)/shard_map/ppermute | solution.py:474
  59.0 4.7 %collective-permute-done.5 = bf16[112,512]{1,0:T(8,128)(2,1)S(1)} collective-permute-done((bf16[112,512]{1,0:T(8,128)(2,1)S(1)}, bf16[112,512]{1,0:T(8,128)(2,1)S(1)}, u32[]{:S(2)}, u32[]{:S(2)}) %collective-permute-start.5) | collective-permute-done | bytes 114720 | tf_op jit(solution)/shard_map/ppermute | solution.py:474
  63.8 0.1 select_convert_fusion.part_1
  63.9 0.0 collective-permute-done.6
  63.9 1.7 %collective-permute-start.7 = (bf16[112,512]{1,0:T(8,128)(2,1)S(1)}, bf16[112,512]{1,0:T(8,128)(2,1)S(1)}, u32[]{:S(2)}, u32[]{:S(2)}) collective-permute-start(bf16[112,512]{1,0:T(8,128)(2,1)S(1)} %select_convert_fusion.part_1), channel_id=1, source_target_pairs={{0,1},{1,0},{2,3},{3,2},{4,5},{5,4},{6,7},{7,6},{8,9},{9,8},{10,11... | collective-permute-start | bytes 344072 | tf_op jit(solution)/shard_map/ppermute | solution.py:474
  65.6 4.7 %collective-permute-done.7.part_2 = bf16[112,512]{1,0:T(8,128)(2,1)S(1)} collective-permute-done((bf16[112,512]{1,0:T(8,128)(2,1)S(1)}, bf16[112,512]{1,0:T(8,128)(2,1)S(1)}, u32[]{:S(2)}, u32[]{:S(2)}) %collective-permute-start.7) | collective-permute-done | bytes 114720 | tf_op jit(solution)/shard_map/ppermute | solution.py:474
  70.3 0.3 collective-permute-start.8
  70.7 1.2 %mask_gradient.1 = (f32[512,512]{1,0:T(8,128)S(1)}, f32[128,512]{1,0:T(8,128)S(1)}, bf16[320,128]{1,0:T(8,128)(2,1)S(1)}, bf16[320,128]{1,0:T(8,128)(2,1)S(1)}) custom-call(f32[1,512,512]{2,1,0:T(8,128)S(1)} %copy-done, bf16[112,512]{1,0:T(8,128)(2,1)S(1)} %select_convert_fusion.part_1, bf16[112,512]{1,0:T(8,128)(2,1)S(1)} %collective-permute-done.7.part_2, ...), custom_call_target="tpu_custom_call" | custom-call | tf_op jit(solution)/shard_map/mask_gradient/pallas_call | solution.py:555
  71.9 0.0 copy-start.7
  71.9 0.0 collective-permute-done.8
  71.9 2.7 %collective-permute-start.13 = (bf16[128,512]{1,0:T(8,128)(2,1)S(1)}, bf16[128,512]{1,0:T(8,128)(2,1)S(1)}, u32[]{:S(2)}, u32[]{:S(2)}) collective-permute-start(bf16[128,512]{1,0:T(8,128)(2,1)S(1)} %pad_maximum_fusion.1), channel_id=1, source_target_pairs={{0,4},{1,5},{2,6},{3,7},{4,0},{5,1},{6,2},{7,3},{8,12},{9,13},{10,... | collective-permute-start | bytes 393224 | tf_op jit(solution)/shard_map/ppermute | solution.py:474
  74.6 0.2 collective-permute-start.9
  74.8 2.1 %collective-permute-start.10 = (bf16[320,128]{1,0:T(8,128)(2,1)S(1)}, bf16[320,128]{1,0:T(8,128)(2,1)S(1)}, u32[]{:S(2)}, u32[]{:S(2)}) collective-permute-start(bf16[320,128]{1,0:T(8,128)(2,1)S(1)} %get-tuple-element.47), channel_id=1, source_target_pairs={{8,16},{24,32},{40,48},{72,80},{88,96},{104,112},{136,144},{152,16... | collective-permute-start | bytes 245768 | tf_op jit(solution)/shard_map/ppermute | solution.py:568
  77.0 0.1 collective-permute-start.11
  77.1 3.6 %collective-permute-done.11 = f32[8,128]{1,0:T(8,128)S(1)} collective-permute-done((f32[8,128]{1,0:T(8,128)S(1)}, f32[8,128]{1,0:T(8,128)S(1)}, u32[]{:S(2)}, u32[]{:S(2)}) %collective-permute-start.11) | collective-permute-done | bytes 4128 | tf_op jit(solution)/shard_map/ppermute | solution.py:478
  80.7 3.5 %collective-permute-start.12 = (f32[8,128]{1,0:T(8,128)S(1)}, f32[8,128]{1,0:T(8,128)S(1)}, u32[]{:S(2)}, u32[]{:S(2)}) collective-permute-start(f32[8,128]{1,0:T(8,128)S(1)} %add.88), channel_id=1, source_target_pairs={{0,32},{8,40},{16,48},{24,56},{32,0},{40,8},{48,16},{56,24},{64,96... | collective-permute-start | bytes 12296 | tf_op jit(solution)/shard_map/ppermute | solution.py:478
  84.2 1.6 %collective-permute-done.12 = f32[8,128]{1,0:T(8,128)S(1)} collective-permute-done((f32[8,128]{1,0:T(8,128)S(1)}, f32[8,128]{1,0:T(8,128)S(1)}, u32[]{:S(2)}, u32[]{:S(2)}) %collective-permute-start.12) | collective-permute-done | bytes 4128 | tf_op jit(solution)/shard_map/ppermute | solution.py:478
  85.7 0.6 add.89.weight
  86.3 0.0 collective-permute-done.9.side_1
  86.3 0.0 collective-permute-done.10.side_2
  86.3 0.0 collective-permute-done.13
  86.4 0.6 copy-done.2
  87.0 0.0 copy-done.4
  87.0 1.8 %row_rims.1 = bf16[80,512]{1,0:T(8,128)(2,1)} custom-call(f32[128,512]{1,0:T(8,128)} %copy-done.7, bf16[320,128]{1,0:T(8,128)(2,1)} %copy-done.2, bf16[320,128]{1,0:T(8,128)(2,1)} %copy-done.4, f32[8,128]{1,0:T(8,128)} %add.89.weight), custom_call_target="tpu_custom_call" | custom-call | tf_op jit(solution)/shard_map/row_rims/pallas_call | solution.py:572
  88.7 1.5 %collective-permute-start.17 = (bf16[256,512]{1,0:T(8,128)(2,1)S(1)}, bf16[256,512]{1,0:T(8,128)(2,1)S(1)}, u32[]{:S(2)}, u32[]{:S(2)}) collective-permute-start(bf16[256,512]{1,0:T(8,128)(2,1)S(1)} %pad_maximum_fusion.near), channel_id=1, source_target_pairs={{0,1},{1,0},{2,3},{3,2},{4,5},{5,4},{6,7},{7,6},{8,9},{9,8},{10,11... | collective-permute-start | bytes 786440 | tf_op jit(solution)/shard_map/ppermute | solution.py:474
  90.3 6.6 %collective-permute-start.14 = (bf16[80,512]{1,0:T(8,128)(2,1)}, bf16[80,512]{1,0:T(8,128)(2,1)S(1)}, u32[]{:S(2)}, u32[]{:S(2)}) collective-permute-start(bf16[80,512]{1,0:T(8,128)(2,1)} %row_rims.1), channel_id=1, source_target_pairs={{0,64},{8,72},{16,80},{24,88},{32,96},{40,104},{48,112},{56,120},{... | collective-permute-start | bytes 245768 | tf_op jit(solution)/shard_map/ppermute | solution.py:582
  96.9 3.2 %collective-permute-done.14.mine = bf16[80,512]{1,0:T(8,128)(2,1)S(1)} collective-permute-done((bf16[80,512]{1,0:T(8,128)(2,1)}, bf16[80,512]{1,0:T(8,128)(2,1)S(1)}, u32[]{:S(2)}, u32[]{:S(2)}) %collective-permute-start.14) | collective-permute-done | bytes 81952 | tf_op jit(solution)/shard_map/ppermute | solution.py:582
  100.1 1.8 %collective-permute-start.15 = (bf16[80,512]{1,0:T(8,128)(2,1)S(1)}, bf16[80,512]{1,0:T(8,128)(2,1)S(1)}, u32[]{:S(2)}, u32[]{:S(2)}) collective-permute-start(bf16[80,512]{1,0:T(8,128)(2,1)S(1)} %collective-permute-done.14.mine), channel_id=1, source_target_pairs={{0,2},{1,3},{2,0},{3,1},{4,6},{5,7},{6,4},{7,5},{8,10},{9,11},{10,... | collective-permute-start | bytes 245768 | tf_op jit(solution)/shard_map/ppermute | solution.py:474
  101.9 0.5 collective-permute-start.16
  102.3 3.1 %collective-permute-done.16.other = f32[8,128]{1,0:T(8,128)S(1)} collective-permute-done((f32[8,128]{1,0:T(8,128)S(1)}, f32[8,128]{1,0:T(8,128)S(1)}, u32[]{:S(2)}, u32[]{:S(2)}) %collective-permute-start.16) | collective-permute-done | bytes 4128 | tf_op jit(solution)/shard_map/ppermute | solution.py:478
  105.5 0.0 collective-permute-done.15.theirs
  105.5 0.0 collective-permute-done.17.far
  105.5 2.1 %new_mask.1 = (f32[1,512,512]{2,1,0:T(8,128)}, f32[1,512,512]{2,1,0:T(8,128)}, f32[1,8]{1,0:T(1,128)}) custom-call(f32[512,512]{1,0:T(8,128)S(1)} %get-tuple-element.42.base_in, bf16[320,128]{1,0:T(8,128)(2,1)S(1)} %copy-done.3, bf16[320,128]{1,0:T(8,128)(2,1)S(1)} %copy-done.5, bf16[80,512]{1,0:T(8,128)(2,1)S(1)} %collective-permute-done.14.mine, ...), custom_call_target="tpu_custom_call" | custom-call | tf_op jit(solution)/shard_map/new_mask/pallas_call | solution.py:586
  (38 shorter events, 0.2 us)
Async XLA Ops:
  3.3 13.0 %copy-start.16 = (bf16[16,512]{1,0:T(8,128)(2,1)S(1)}, bf16[16,512]{1,0:T(8,128)(2,1)}, u32[]{:S(2)}) copy-start(bf16[16,512]{1,0:T(8,128)(2,1)} %get-tuple-element.33) | copy-start | bytes 49156
  3.3 13.0 %collective-permute-start = (bf16[80,512]{1,0:T(8,128)(2,1)}, bf16[80,512]{1,0:T(8,128)(2,1)S(1)}, u32[]{:S(2)}, u32[]{:S(2)}) collective-permute-start(bf16[80,512]{1,0:T(8,128)(2,1)} %get-tuple-element.32), channel_id=1, source_target_pairs={{0,68},{8,76},{16,84},{24,92},{32,100},{40,108},{48,116},{56,124},... | collective-permute-start | bytes 245768 | tf_op jit(solution)/shard_map/ppermute | solution.py:502
  16.3 4.5 %copy-start.10 = (bf16[80,512]{1,0:T(8,128)(2,1)}, bf16[80,512]{1,0:T(8,128)(2,1)S(1)}, u32[]{:S(2)}) copy-start(bf16[80,512]{1,0:T(8,128)(2,1)S(1)} %pad_maximum_fusion.2.mine) | copy-start | bytes 245764
  16.3 4.5 %collective-permute-start.1 = (bf16[80,512]{1,0:T(8,128)(2,1)S(1)}, bf16[80,512]{1,0:T(8,128)(2,1)S(1)}, u32[]{:S(2)}, u32[]{:S(2)}) collective-permute-start(bf16[80,512]{1,0:T(8,128)(2,1)S(1)} %pad_maximum_fusion.2.mine), channel_id=1, source_target_pairs={{0,2},{1,3},{2,0},{3,1},{4,6},{5,7},{6,4},{7,5},{8,10},{9,11},{10,... | collective-permute-start | bytes 245768 | tf_op jit(solution)/shard_map/ppermute | solution.py:474
  20.9 0.6 copy-start.12
  23.2 6.5 %copy-start.17 = (f32[8,128]{1,0:T(8,128)S(1)}, f32[8,128]{1,0:T(8,128)}, u32[]{:S(2)}) copy-start(f32[8,128]{1,0:T(8,128)} %get-tuple-element.36) | copy-start | bytes 12292
  23.2 6.5 %collective-permute-start.2 = (bf16[336,128]{1,0:T(8,128)(2,1)}, bf16[336,128]{1,0:T(8,128)(2,1)S(1)}, u32[]{:S(2)}, u32[]{:S(2)}) collective-permute-start(bf16[336,128]{1,0:T(8,128)(2,1)} %get-tuple-element.37), channel_id=1, source_target_pairs={{0,9},{8,1},{16,25},{24,17},{32,41},{40,33},{48,57},{56,49},{64,73... | collective-permute-start | bytes 258056 | tf_op jit(solution)/shard_map/ppermute | solution.py:512
  23.2 7.5 %collective-permute-start.3 = (bf16[320,128]{1,0:T(8,128)(2,1)}, bf16[320,128]{1,0:T(8,128)(2,1)S(1)}, u32[]{:S(2)}, u32[]{:S(2)}) collective-permute-start(bf16[320,128]{1,0:T(8,128)(2,1)} %get-tuple-element.38), channel_id=1, source_target_pairs={{8,16},{24,32},{40,48},{72,80},{88,96},{104,112},{136,144},{152,16... | collective-permute-start | bytes 245768 | tf_op jit(solution)/shard_map/ppermute | solution.py:513
  29.7 1.0 copy-start.13
  30.7 0.6 copy-start.14
  50.3 5.7 %collective-permute-start.4 = (bf16[112,512]{1,0:T(8,128)(2,1)}, bf16[112,512]{1,0:T(8,128)(2,1)S(1)}, u32[]{:S(2)}, u32[]{:S(2)}) collective-permute-start(bf16[112,512]{1,0:T(8,128)(2,1)} %get-tuple-element.39), channel_id=1, source_target_pairs={{0,2},{1,3},{2,0},{3,1},{4,6},{5,7},{6,4},{7,5},{8,10},{9,11},{10,... | collective-permute-start | bytes 344072 | tf_op jit(solution)/shard_map/ppermute | solution.py:474
  51.7 4.3 %copy-start.11 = (bf16[112,512]{1,0:T(8,128)(2,1)S(1)}, bf16[112,512]{1,0:T(8,128)(2,1)}, u32[]{:S(2)}) copy-start(bf16[112,512]{1,0:T(8,128)(2,1)} %get-tuple-element.39) | copy-start | bytes 344068
  51.7 5.6 %copy-start.15 = (bf16[64,512]{1,0:T(8,128)(2,1)S(1)}, bf16[64,512]{1,0:T(8,128)(2,1)}, u32[]{:S(2)}) copy-start(bf16[64,512]{1,0:T(8,128)(2,1)} %get-tuple-element.40) | copy-start | bytes 196612
  51.7 18.9 %copy-start.6 = (bf16[640,224]{1,0:T(8,128)(2,1)S(1)}, bf16[640,224]{1,0:T(8,128)(2,1)}, u32[]{:S(2)}) copy-start(bf16[640,224]{1,0:T(8,128)(2,1)} %constant.25.clone.fold_t) | copy-start | bytes 860164
  52.7 17.9 %copy-start = (f32[1,512,512]{2,1,0:T(8,128)S(1)}, f32[1,512,512]{2,1,0:T(8,128)}, u32[]{:S(2)}) copy-start(f32[1,512,512]{2,1,0:T(8,128)} %mask.1) | copy-start | bytes 3145732
  56.2 14.5 %copy-start.1 = (bf16[512,640]{1,0:T(8,128)(2,1)S(1)}, bf16[512,640]{1,0:T(8,128)(2,1)}, u32[]{:S(2)}) copy-start(bf16[512,640]{1,0:T(8,128)(2,1)} %constant.21.clone.freq_at.freq) | copy-start | bytes 1966084
  56.2 7.5 %collective-permute-start.5 = (bf16[112,512]{1,0:T(8,128)(2,1)S(1)}, bf16[112,512]{1,0:T(8,128)(2,1)S(1)}, u32[]{:S(2)}, u32[]{:S(2)}) collective-permute-start(bf16[112,512]{1,0:T(8,128)(2,1)S(1)} %get-tuple-element.64), channel_id=1, source_target_pairs={{0,4},{1,5},{2,6},{3,7},{4,0},{5,1},{6,2},{7,3},{8,12},{9,13},{10,... | collective-permute-start | bytes 344072 | tf_op jit(solution)/shard_map/ppermute | solution.py:474
  57.3 6.7 %collective-permute-start.6 = (bf16[64,512]{1,0:T(8,128)(2,1)S(1)}, bf16[64,512]{1,0:T(8,128)(2,1)S(1)}, u32[]{:S(2)}, u32[]{:S(2)}) collective-permute-start(bf16[64,512]{1,0:T(8,128)(2,1)S(1)} %copy-done.15), channel_id=1, source_target_pairs={{0,2},{1,3},{2,0},{3,1},{4,6},{5,7},{6,4},{7,5},{8,10},{9,11},{10,... | collective-permute-start | bytes 196616 | tf_op jit(solution)/shard_map/ppermute | solution.py:474
  63.9 6.4 %collective-permute-start.7 = (bf16[112,512]{1,0:T(8,128)(2,1)S(1)}, bf16[112,512]{1,0:T(8,128)(2,1)S(1)}, u32[]{:S(2)}, u32[]{:S(2)}) collective-permute-start(bf16[112,512]{1,0:T(8,128)(2,1)S(1)} %select_convert_fusion.part_1), channel_id=1, source_target_pairs={{0,1},{1,0},{2,3},{3,2},{4,5},{5,4},{6,7},{7,6},{8,9},{9,8},{10,11... | collective-permute-start | bytes 344072 | tf_op jit(solution)/shard_map/ppermute | solution.py:474
  70.3 1.6 %collective-permute-start.8 = (f32[8,128]{1,0:T(8,128)S(1)}, f32[8,128]{1,0:T(8,128)S(1)}, u32[]{:S(2)}, u32[]{:S(2)}) collective-permute-start(f32[8,128]{1,0:T(8,128)S(1)} %broadcast_in_dim.70), channel_id=1, source_target_pairs={{0,8},{8,0},{16,24},{24,16},{32,40},{40,32},{48,56},{56,48},{64,72... | collective-permute-start | bytes 12296 | tf_op jit(solution)/shard_map/ppermute | solution.py:478
  71.9 14.5 %copy-start.7 = (f32[128,512]{1,0:T(8,128)}, f32[128,512]{1,0:T(8,128)S(1)}, u32[]{:S(2)}) copy-start(f32[128,512]{1,0:T(8,128)S(1)} %get-tuple-element.52.rims_in) | copy-start | bytes 786436
  71.9 14.4 %collective-permute-start.13 = (bf16[128,512]{1,0:T(8,128)(2,1)S(1)}, bf16[128,512]{1,0:T(8,128)(2,1)S(1)}, u32[]{:S(2)}, u32[]{:S(2)}) collective-permute-start(bf16[128,512]{1,0:T(8,128)(2,1)S(1)} %pad_maximum_fusion.1), channel_id=1, source_target_pairs={{0,4},{1,5},{2,6},{3,7},{4,0},{5,1},{6,2},{7,3},{8,12},{9,13},{10,... | collective-permute-start | bytes 393224 | tf_op jit(solution)/shard_map/ppermute | solution.py:474
  74.6 11.7 %collective-permute-start.9 = (bf16[320,128]{1,0:T(8,128)(2,1)S(1)}, bf16[320,128]{1,0:T(8,128)(2,1)S(1)}, u32[]{:S(2)}, u32[]{:S(2)}) collective-permute-start(bf16[320,128]{1,0:T(8,128)(2,1)S(1)} %get-tuple-element.46), channel_id=1, source_target_pairs={{0,8},{8,0},{16,24},{24,16},{32,40},{40,32},{48,56},{56,48},{64,72... | collective-permute-start | bytes 245768 | tf_op jit(solution)/shard_map/ppermute | solution.py:567
  74.8 11.5 %collective-permute-start.10 = (bf16[320,128]{1,0:T(8,128)(2,1)S(1)}, bf16[320,128]{1,0:T(8,128)(2,1)S(1)}, u32[]{:S(2)}, u32[]{:S(2)}) collective-permute-start(bf16[320,128]{1,0:T(8,128)(2,1)S(1)} %get-tuple-element.47), channel_id=1, source_target_pairs={{8,16},{24,32},{40,48},{72,80},{88,96},{104,112},{136,144},{152,16... | collective-permute-start | bytes 245768 | tf_op jit(solution)/shard_map/ppermute | solution.py:568
  77.0 3.7 %collective-permute-start.11 = (f32[8,128]{1,0:T(8,128)S(1)}, f32[8,128]{1,0:T(8,128)S(1)}, u32[]{:S(2)}, u32[]{:S(2)}) collective-permute-start(f32[8,128]{1,0:T(8,128)S(1)} %broadcast_add_fusion), channel_id=1, source_target_pairs={{0,16},{8,24},{16,0},{24,8},{32,48},{40,56},{48,32},{56,40},{64,80... | collective-permute-start | bytes 12296 | tf_op jit(solution)/shard_map/ppermute | solution.py:478
  80.7 5.1 %collective-permute-start.12 = (f32[8,128]{1,0:T(8,128)S(1)}, f32[8,128]{1,0:T(8,128)S(1)}, u32[]{:S(2)}, u32[]{:S(2)}) collective-permute-start(f32[8,128]{1,0:T(8,128)S(1)} %add.88), channel_id=1, source_target_pairs={{0,32},{8,40},{16,48},{24,56},{32,0},{40,8},{48,16},{56,24},{64,96... | collective-permute-start | bytes 12296 | tf_op jit(solution)/shard_map/ppermute | solution.py:478
  86.3 0.6 copy-start.2
  86.3 0.6 copy-start.4
  87.0 14.9 %copy-start.8 = (f32[8,128]{1,0:T(8,128)S(1)}, f32[8,128]{1,0:T(8,128)}, u32[]{:S(2)}) copy-start(f32[8,128]{1,0:T(8,128)} %add.89.weight) | copy-start | bytes 12292
  87.0 18.5 %copy-start.3 = (bf16[320,128]{1,0:T(8,128)(2,1)S(1)}, bf16[320,128]{1,0:T(8,128)(2,1)}, u32[]{:S(2)}) copy-start(bf16[320,128]{1,0:T(8,128)(2,1)} %copy-done.2) | copy-start | bytes 245764
  87.0 18.5 %copy-start.5 = (bf16[320,128]{1,0:T(8,128)(2,1)S(1)}, bf16[320,128]{1,0:T(8,128)(2,1)}, u32[]{:S(2)}) copy-start(bf16[320,128]{1,0:T(8,128)(2,1)} %copy-done.4) | copy-start | bytes 245764
  88.7 16.8 %copy-start.9 = (f32[8]{0:T(128)S(1)}, f32[8]{0:T(128)}, u32[]{:S(2)}) copy-start(f32[8]{0:T(128)} %param.14) | copy-start | bytes 100
  88.7 16.7 %collective-permute-start.17 = (bf16[256,512]{1,0:T(8,128)(2,1)S(1)}, bf16[256,512]{1,0:T(8,128)(2,1)S(1)}, u32[]{:S(2)}, u32[]{:S(2)}) collective-permute-start(bf16[256,512]{1,0:T(8,128)(2,1)S(1)} %pad_maximum_fusion.near), channel_id=1, source_target_pairs={{0,1},{1,0},{2,3},{3,2},{4,5},{5,4},{6,7},{7,6},{8,9},{9,8},{10,11... | collective-permute-start | bytes 786440 | tf_op jit(solution)/shard_map/ppermute | solution.py:474
  90.3 9.8 %collective-permute-start.14 = (bf16[80,512]{1,0:T(8,128)(2,1)}, bf16[80,512]{1,0:T(8,128)(2,1)S(1)}, u32[]{:S(2)}, u32[]{:S(2)}) collective-permute-start(bf16[80,512]{1,0:T(8,128)(2,1)} %row_rims.1), channel_id=1, source_target_pairs={{0,64},{8,72},{16,80},{24,88},{32,96},{40,104},{48,112},{56,120},{... | collective-permute-start | bytes 245768 | tf_op jit(solution)/shard_map/ppermute | solution.py:582
  100.1 5.4 %collective-permute-start.15 = (bf16[80,512]{1,0:T(8,128)(2,1)S(1)}, bf16[80,512]{1,0:T(8,128)(2,1)S(1)}, u32[]{:S(2)}, u32[]{:S(2)}) collective-permute-start(bf16[80,512]{1,0:T(8,128)(2,1)S(1)} %collective-permute-done.14.mine), channel_id=1, source_target_pairs={{0,2},{1,3},{2,0},{3,1},{4,6},{5,7},{6,4},{7,5},{8,10},{9,11},{10,... | collective-permute-start | bytes 245768 | tf_op jit(solution)/shard_map/ppermute | solution.py:474
  101.9 3.6 %collective-permute-start.16 = (f32[8,128]{1,0:T(8,128)S(1)}, f32[8,128]{1,0:T(8,128)S(1)}, u32[]{:S(2)}, u32[]{:S(2)}) collective-permute-start(f32[8,128]{1,0:T(8,128)S(1)} %copy-done.8), channel_id=1, source_target_pairs={{0,128},{8,136},{16,144},{24,152},{32,160},{40,168},{48,176},{56,1... | collective-permute-start | bytes 12296 | tf_op jit(solution)/shard_map/ppermute | solution.py:478

commit v4 on v3

--- a/solution.py
+++ b/solution.py
@@ -337,13 +337,14 @@
     return rows[1:2] + rows[2:3] + rows[3:4]
 
 
-def add(one, two):
-    one, two = one.astype(F32), two.astype(F32)
-    sums = weight_sums(one[FOLD:]) + weight_sums(two[FOLD:])
+def add(*parts):
+    parts = [part.astype(F32) for part in parts]
+    rows = [weight_sums(part[FOLD:]) for part in parts]
+    sums = (rows[0] + rows[1]) + (rows[2] + rows[3])
+    total = (parts[0] + parts[1]) + (parts[2] + parts[3])
     high = lax.reduce_precision(sums, 8, 7)
     mid = lax.reduce_precision(sums - high, 8, 7)
-    row = lax.broadcasted_iota(jnp.int32, one.shape, 0) - FOLD
-    total = one + two
+    row = lax.broadcasted_iota(jnp.int32, total.shape, 0) - FOLD
     for n, piece in enumerate((high, mid, sums - high - mid)):
         total = jnp.where(row == n + 1, piece, total)
     return total.astype(BF)
@@ -543,11 +544,8 @@
         freq, back_t, back, rows, rows_t,
     )
 
-    other = src_swap(part, 2, groups)
     near = src_swap(resist, 2, groups)
-    part = add(part, other)
-    other = src_swap(part, 4, groups)
-    part, near = lax.optimization_barrier((add(part, other), near))
+    part = add(part, *(src_swap(part, distance, groups) for distance in (2, 4, 6)))
     other = src_swap(part, 1, groups)
     weight = weight_sums(part[FOLD:, :128].astype(F32)) + weight_sums(other[FOLD:, :128].astype(F32))
     weight = jnp.broadcast_to(weight, (8, 128))

time: 109 us -> 106 us (0.972)
  waiting for transfers between devices: 32.8 us -> 29 us
  starting transfers between devices: 41 us -> 42.4 us
    ppermute x8 -> x9, waiting for transfers between devices: 15.5 us -> 12.2 us  [src_swap(): return lax.ppermute(block, 'src', [(i, i ^ distance) for i in range(count)])]
    ppermute x8 -> x9, starting transfers between devices: 13.6 us -> 14 us  [src_swap(): return lax.ppermute(block, 'src', [(i, i ^ distance) for i in range(count)])]
  transfers between devices with their start and end apart: 18 -> 19, of which waited for: 11 -> 10; matrix products, arithmetic and copies ran while one was open for 2% -> 2% of each run, Pallas kernels for 1% -> 1%
where the time goes in v4:
time: 106 us; the launch traced here: 105 us
  starting transfers between devices  42.4 us (40%)
  waiting for transfers between devices  29 us (27%)
  Pallas kernels  28.5 us (27%)
  other arithmetic  2.48 us (2%)
  local copies, waits for them, and re-layouts  1.92 us (2%)
  between operations  1.13 us (1%)
    pallas_call x1, Pallas kernels, per_device(): pl.pallas_call(source_kernel, out_shape=(shaped((ROWS, 2 * HALF), BF), sh...  19.1 us
    ppermute x9, starting transfers between devices, src_swap(): return lax.ppermute(block, 'src', [(i, i ^ distance) for i in range(count)])  14 us
    ppermute x9, waiting for transfers between devices, src_swap(): return lax.ppermute(block, 'src', [(i, i ^ distance) for i in range(count)])  12.2 us
    ppermute x1, starting transfers between devices, per_device(): lax.ppermute(vert, ('tile', 'src'), route_of(row_swap, row_ring, groups, 4))  9.01 us
    ppermute x4, waiting for transfers between devices, tile_swap(): lax.ppermute(block, 'tile', [(i, i ^ distance) for i in range(count)])  7.91 us
    ppermute x1, starting transfers between devices, per_device(): lax.ppermute(rim, ('tile', 'src'), route_of(row_swap, row_ring, groups))  7.16 us
    ppermute x2, starting transfers between devices, per_device(): side_2 = lax.ppermute(side_2, 'tile', col_next)  7.12 us
    ppermute x4, starting transfers between devices, tile_swap(): lax.ppermute(block, 'tile', [(i, i ^ distance) for i in range(count)])  5 us
  transfers between devices with their start and end apart: 19, of which 10 were waited for; matrix products, arithmetic and copies ran while one was open for 2% of the time, Pallas kernels for 1%

profile of v4, /device:TPU:32, one launch (start us, length us, event | category | flops | bytes accessed | tf_op | source)
XLA Modules:
  0.0 105.4 jit_solution(14590495669810213796)
XLA Ops:
  0.6 2.7 %edges.1 = (bf16[80,512]{1,0:T(8,128)(2,1)}, bf16[256,128]{1,0:T(8,128)(2,1)}, bf16[256,128]{1,0:T(8,128)(2,1)}, bf16[16,512]{1,0:T(8,128)(2,1)}) custom-call(s32[2,8]{1,0:T(2,128)} %bitcast.13, f32[1,8]{1,0:T(1,128)} %bitcast.8, f32[1,512,512]{2,1,0:T(8,128)} %mask.1), custom_call_target="tpu_custom_call" | custom-call | tf_op jit(solution)/shard_map/edges/pallas_call | solution.py:493
  3.3 0.0 copy-start.16
  3.3 9.0 %collective-permute-start = (bf16[80,512]{1,0:T(8,128)(2,1)}, bf16[80,512]{1,0:T(8,128)(2,1)S(1)}, u32[]{:S(2)}, u32[]{:S(2)}) collective-permute-start(bf16[80,512]{1,0:T(8,128)(2,1)} %get-tuple-element.30), channel_id=1, source_target_pairs={{0,68},{8,76},{16,84},{24,92},{32,100},{40,108},{48,116},{56,124},... | collective-permute-start | bytes 245768 | tf_op jit(solution)/shard_map/ppermute | solution.py:503
  12.3 4.0 %collective-permute-done = bf16[80,512]{1,0:T(8,128)(2,1)S(1)} collective-permute-done((bf16[80,512]{1,0:T(8,128)(2,1)}, bf16[80,512]{1,0:T(8,128)(2,1)S(1)}, u32[]{:S(2)}, u32[]{:S(2)}) %collective-permute-start) | collective-permute-done | bytes 81952 | tf_op jit(solution)/shard_map/ppermute | solution.py:503
  16.3 0.0 copy-done.16
  16.3 0.0 copy-start.10
  16.3 1.7 %collective-permute-start.1 = (bf16[80,512]{1,0:T(8,128)(2,1)S(1)}, bf16[80,512]{1,0:T(8,128)(2,1)S(1)}, u32[]{:S(2)}, u32[]{:S(2)}) collective-permute-start(bf16[80,512]{1,0:T(8,128)(2,1)S(1)} %pad_maximum_fusion.2.mine), channel_id=1, source_target_pairs={{0,2},{1,3},{2,0},{3,1},{4,6},{5,7},{6,4},{7,5},{8,10},{9,11},{10,... | collective-permute-start | bytes 245768 | tf_op jit(solution)/shard_map/ppermute | solution.py:475
  18.0 2.8 %collective-permute-done.1.theirs = bf16[80,512]{1,0:T(8,128)(2,1)S(1)} collective-permute-done((bf16[80,512]{1,0:T(8,128)(2,1)S(1)}, bf16[80,512]{1,0:T(8,128)(2,1)S(1)}, u32[]{:S(2)}, u32[]{:S(2)}) %collective-permute-start.1) | collective-permute-done | bytes 81952 | tf_op jit(solution)/shard_map/ppermute | solution.py:475
  20.9 0.0 copy-done.10
  20.9 0.6 copy-done.12
  21.5 1.7 %corners.1 = (bf16[336,128]{1,0:T(8,128)(2,1)}, bf16[320,128]{1,0:T(8,128)(2,1)}, f32[8,128]{1,0:T(8,128)}) custom-call(bf16[80,512]{1,0:T(8,128)(2,1)} %copy-done.10, bf16[80,512]{1,0:T(8,128)(2,1)} %copy-done.12, bf16[256,128]{1,0:T(8,128)(2,1)} %get-tuple-element.32.side_1, bf16[256,128]{1,0:T(8,128)(2,1)} %get-tuple-element.33.side_2), custom_call_target="tpu_custom_call" | custom-call | tf_op jit(solution)/shard_map/corners/pallas_call | solution.py:506
  23.2 0.0 collective-permute-start.2
  23.2 5.1 %collective-permute-start.3 = (bf16[320,128]{1,0:T(8,128)(2,1)}, bf16[320,128]{1,0:T(8,128)(2,1)S(1)}, u32[]{:S(2)}, u32[]{:S(2)}) collective-permute-start(bf16[320,128]{1,0:T(8,128)(2,1)} %get-tuple-element.36), channel_id=1, source_target_pairs={{8,16},{24,32},{40,48},{72,80},{88,96},{104,112},{136,144},{152,16... | collective-permute-start | bytes 245768 | tf_op jit(solution)/shard_map/ppermute | solution.py:514
  28.3 1.4 %collective-permute-done.2.side_1 = bf16[336,128]{1,0:T(8,128)(2,1)S(1)} collective-permute-done((bf16[336,128]{1,0:T(8,128)(2,1)}, bf16[336,128]{1,0:T(8,128)(2,1)S(1)}, u32[]{:S(2)}, u32[]{:S(2)}) %collective-permute-start.2) | collective-permute-done | bytes 86048 | tf_op jit(solution)/shard_map/ppermute | solution.py:513
  29.7 0.0 copy-done.17
  29.7 0.6 convert_add_fusion.info
  30.3 0.4 collective-permute-done.3.side_2
  30.7 0.0 copy-done.13
  30.7 0.6 copy-done.14
  31.3 19.1 %sources.1 = (bf16[112,512]{1,0:T(8,128)(2,1)}, bf16[64,512]{1,0:T(8,128)(2,1)}) custom-call(f32[8,128]{1,0:T(8,128)} %convert_add_fusion.info, bf16[80,512]{1,0:T(8,128)(2,1)} %copy-done.10, bf16[80,512]{1,0:T(8,128)(2,1)} %copy-done.12, bf16[336,128]{1,0:T(8,128)(2,1)} %copy-done.13, bf16[320,128]{1,0:T(8,128)(2,1)} %copy-done.14, f32[1,512,512]{2,1,0:T(8,128)} %mask.1, ...), custom_call_target="tpu_custom_call" | custom-call | tf_op jit(solution)/shard_map/sources/pallas_call | solution.py:517
  50.4 2.0 %collective-permute-start.6 = (bf16[112,512]{1,0:T(8,128)(2,1)}, bf16[112,512]{1,0:T(8,128)(2,1)S(1)}, u32[]{:S(2)}, u32[]{:S(2)}) collective-permute-start(bf16[112,512]{1,0:T(8,128)(2,1)} %get-tuple-element.37), channel_id=1, source_target_pairs={{0,6},{1,7},{2,4},{3,5},{4,2},{5,3},{6,0},{7,1},{8,14},{9,15},{10,... | collective-permute-start | bytes 344072 | tf_op jit(solution)/shard_map/ppermute | solution.py:475
  52.4 1.5 %collective-permute-start.5 = (bf16[112,512]{1,0:T(8,128)(2,1)}, bf16[112,512]{1,0:T(8,128)(2,1)S(1)}, u32[]{:S(2)}, u32[]{:S(2)}) collective-permute-start(bf16[112,512]{1,0:T(8,128)(2,1)} %get-tuple-element.37), channel_id=1, source_target_pairs={{0,4},{1,5},{2,6},{3,7},{4,0},{5,1},{6,2},{7,3},{8,12},{9,13},{10,... | collective-permute-start | bytes 344072 | tf_op jit(solution)/shard_map/ppermute | solution.py:475
  53.9 0.7 collective-permute-start.4
  54.6 0.0 copy-start.11
  54.6 0.0 copy-start.6
  54.6 1.0 convert_element_type.25
  55.6 0.0 copy-start
  55.6 1.4 %collective-permute-start.9 = (bf16[64,512]{1,0:T(8,128)(2,1)S(1)}, bf16[64,512]{1,0:T(8,128)(2,1)S(1)}, u32[]{:S(2)}, u32[]{:S(2)}) collective-permute-start(bf16[64,512]{1,0:T(8,128)(2,1)S(1)} %copy-done.15), channel_id=1, source_target_pairs={{0,2},{1,3},{2,0},{3,1},{4,6},{5,7},{6,4},{7,5},{8,10},{9,11},{10,... | collective-permute-start | bytes 196616 | tf_op jit(solution)/shard_map/ppermute | solution.py:475
  57.0 4.0 %collective-permute-done.4 = bf16[112,512]{1,0:T(8,128)(2,1)S(1)} collective-permute-done((bf16[112,512]{1,0:T(8,128)(2,1)}, bf16[112,512]{1,0:T(8,128)(2,1)S(1)}, u32[]{:S(2)}, u32[]{:S(2)}) %collective-permute-start.4) | collective-permute-done | bytes 114720 | tf_op jit(solution)/shard_map/ppermute | solution.py:475
  61.0 0.0 collective-permute-done.5
  61.1 0.0 copy-start.1
  61.1 0.0 collective-permute-done.6
  61.2 0.1 select_convert_fusion.part_1
  61.3 2.2 %collective-permute-start.7 = (bf16[112,512]{1,0:T(8,128)(2,1)S(1)}, bf16[112,512]{1,0:T(8,128)(2,1)S(1)}, u32[]{:S(2)}, u32[]{:S(2)}) collective-permute-start(bf16[112,512]{1,0:T(8,128)(2,1)S(1)} %select_convert_fusion.part_1), channel_id=1, source_target_pairs={{0,1},{1,0},{2,3},{3,2},{4,5},{5,4},{6,7},{7,6},{8,9},{9,8},{10,11... | collective-permute-start | bytes 344072 | tf_op jit(solution)/shard_map/ppermute | solution.py:475
  63.4 5.4 %collective-permute-done.7.part_2 = bf16[112,512]{1,0:T(8,128)(2,1)S(1)} collective-permute-done((bf16[112,512]{1,0:T(8,128)(2,1)S(1)}, bf16[112,512]{1,0:T(8,128)(2,1)S(1)}, u32[]{:S(2)}, u32[]{:S(2)}) %collective-permute-start.7) | collective-permute-done | bytes 114720 | tf_op jit(solution)/shard_map/ppermute | solution.py:475
  68.8 0.1 collective-permute-start.8
  68.9 0.0 collective-permute-done.9
  69.0 1.2 %mask_gradient.1 = (f32[512,512]{1,0:T(8,128)S(1)}, f32[128,512]{1,0:T(8,128)S(1)}, bf16[320,128]{1,0:T(8,128)(2,1)S(1)}, bf16[320,128]{1,0:T(8,128)(2,1)S(1)}) custom-call(f32[1,512,512]{2,1,0:T(8,128)S(1)} %copy-done, bf16[112,512]{1,0:T(8,128)(2,1)S(1)} %select_convert_fusion.part_1, bf16[112,512]{1,0:T(8,128)(2,1)S(1)} %collective-permute-done.7.part_2, ...), custom_call_target="tpu_custom_call" | custom-call | tf_op jit(solution)/shard_map/mask_gradient/pallas_call | solution.py:553
  70.2 0.0 copy-start.7
  70.2 0.0 collective-permute-done.8
  70.3 1.5 %collective-permute-start.14 = (bf16[128,512]{1,0:T(8,128)(2,1)S(1)}, bf16[128,512]{1,0:T(8,128)(2,1)S(1)}, u32[]{:S(2)}, u32[]{:S(2)}) collective-permute-start(bf16[128,512]{1,0:T(8,128)(2,1)S(1)} %pad_maximum_fusion.1), channel_id=1, source_target_pairs={{0,4},{1,5},{2,6},{3,7},{4,0},{5,1},{6,2},{7,3},{8,12},{9,13},{10,... | collective-permute-start | bytes 393224 | tf_op jit(solution)/shard_map/ppermute | solution.py:475
  71.7 0.1 collective-permute-start.10
  71.8 2.0 %collective-permute-start.11 = (bf16[320,128]{1,0:T(8,128)(2,1)S(1)}, bf16[320,128]{1,0:T(8,128)(2,1)S(1)}, u32[]{:S(2)}, u32[]{:S(2)}) collective-permute-start(bf16[320,128]{1,0:T(8,128)(2,1)S(1)} %get-tuple-element.43), channel_id=1, source_target_pairs={{8,16},{24,32},{40,48},{72,80},{88,96},{104,112},{136,144},{152,16... | collective-permute-start | bytes 245768 | tf_op jit(solution)/shard_map/ppermute | solution.py:566
  73.8 0.1 collective-permute-start.12
  73.9 3.6 %collective-permute-done.12 = f32[8,128]{1,0:T(8,128)S(1)} collective-permute-done((f32[8,128]{1,0:T(8,128)S(1)}, f32[8,128]{1,0:T(8,128)S(1)}, u32[]{:S(2)}, u32[]{:S(2)}) %collective-permute-start.12) | collective-permute-done | bytes 4128 | tf_op jit(solution)/shard_map/ppermute | solution.py:479
  77.6 3.9 %collective-permute-start.13 = (f32[8,128]{1,0:T(8,128)S(1)}, f32[8,128]{1,0:T(8,128)S(1)}, u32[]{:S(2)}, u32[]{:S(2)}) collective-permute-start(f32[8,128]{1,0:T(8,128)S(1)} %add.96), channel_id=1, source_target_pairs={{0,32},{8,40},{16,48},{24,56},{32,0},{40,8},{48,16},{56,24},{64,96... | collective-permute-start | bytes 12296 | tf_op jit(solution)/shard_map/ppermute | solution.py:479
  81.5 1.6 %collective-permute-done.13 = f32[8,128]{1,0:T(8,128)S(1)} collective-permute-done((f32[8,128]{1,0:T(8,128)S(1)}, f32[8,128]{1,0:T(8,128)S(1)}, u32[]{:S(2)}, u32[]{:S(2)}) %collective-permute-start.13) | collective-permute-done | bytes 4128 | tf_op jit(solution)/shard_map/ppermute | solution.py:479
  83.1 0.6 add.97.weight
  83.7 0.0 collective-permute-done.10.side_1
  83.7 0.0 collective-permute-done.11.side_2
  83.7 0.0 copy-start.4
  83.7 0.0 collective-permute-done.14
  83.7 0.6 copy-done.2
  84.3 0.0 copy-done.4
  84.3 1.8 %row_rims.1 = bf16[80,512]{1,0:T(8,128)(2,1)} custom-call(f32[128,512]{1,0:T(8,128)} %copy-done.7, bf16[320,128]{1,0:T(8,128)(2,1)} %copy-done.2, bf16[320,128]{1,0:T(8,128)(2,1)} %copy-done.4, f32[8,128]{1,0:T(8,128)} %add.97.weight), custom_call_target="tpu_custom_call" | custom-call | tf_op jit(solution)/shard_map/row_rims/pallas_call | solution.py:570
  86.1 1.2 %collective-permute-start.18 = (bf16[256,512]{1,0:T(8,128)(2,1)S(1)}, bf16[256,512]{1,0:T(8,128)(2,1)S(1)}, u32[]{:S(2)}, u32[]{:S(2)}) collective-permute-start(bf16[256,512]{1,0:T(8,128)(2,1)S(1)} %pad_maximum_fusion.near), channel_id=1, source_target_pairs={{0,1},{1,0},{2,3},{3,2},{4,5},{5,4},{6,7},{7,6},{8,9},{9,8},{10,11... | collective-permute-start | bytes 786440 | tf_op jit(solution)/shard_map/ppermute | solution.py:475
  87.3 7.2 %collective-permute-start.15 = (bf16[80,512]{1,0:T(8,128)(2,1)}, bf16[80,512]{1,0:T(8,128)(2,1)S(1)}, u32[]{:S(2)}, u32[]{:S(2)}) collective-permute-start(bf16[80,512]{1,0:T(8,128)(2,1)} %row_rims.1), channel_id=1, source_target_pairs={{0,64},{8,72},{16,80},{24,88},{32,96},{40,104},{48,112},{56,120},{... | collective-permute-start | bytes 245768 | tf_op jit(solution)/shard_map/ppermute | solution.py:580
  94.4 3.2 %collective-permute-done.15.mine = bf16[80,512]{1,0:T(8,128)(2,1)S(1)} collective-permute-done((bf16[80,512]{1,0:T(8,128)(2,1)}, bf16[80,512]{1,0:T(8,128)(2,1)S(1)}, u32[]{:S(2)}, u32[]{:S(2)}) %collective-permute-start.15) | collective-permute-done | bytes 81952 | tf_op jit(solution)/shard_map/ppermute | solution.py:580
  97.6 1.9 %collective-permute-start.16 = (bf16[80,512]{1,0:T(8,128)(2,1)S(1)}, bf16[80,512]{1,0:T(8,128)(2,1)S(1)}, u32[]{:S(2)}, u32[]{:S(2)}) collective-permute-start(bf16[80,512]{1,0:T(8,128)(2,1)S(1)} %collective-permute-done.15.mine), channel_id=1, source_target_pairs={{0,2},{1,3},{2,0},{3,1},{4,6},{5,7},{6,4},{7,5},{8,10},{9,11},{10,... | collective-permute-start | bytes 245768 | tf_op jit(solution)/shard_map/ppermute | solution.py:475
  99.5 0.9 collective-permute-start.17
  100.4 2.7 %collective-permute-done.17.other = f32[8,128]{1,0:T(8,128)S(1)} collective-permute-done((f32[8,128]{1,0:T(8,128)S(1)}, f32[8,128]{1,0:T(8,128)S(1)}, u32[]{:S(2)}, u32[]{:S(2)}) %collective-permute-start.17) | collective-permute-done | bytes 4128 | tf_op jit(solution)/shard_map/ppermute | solution.py:479
  103.1 0.0 collective-permute-done.16.theirs
  103.1 0.0 collective-permute-done.18.far
  103.2 2.1 %new_mask.1 = (f32[1,512,512]{2,1,0:T(8,128)}, f32[1,512,512]{2,1,0:T(8,128)}, f32[1,8]{1,0:T(1,128)}) custom-call(f32[512,512]{1,0:T(8,128)S(1)} %get-tuple-element.38.base_in, bf16[320,128]{1,0:T(8,128)(2,1)S(1)} %copy-done.3, bf16[320,128]{1,0:T(8,128)(2,1)S(1)} %copy-done.5, bf16[80,512]{1,0:T(8,128)(2,1)S(1)} %collective-permute-done.15.mine, ...), custom_call_target="tpu_custom_call" | custom-call | tf_op jit(solution)/shard_map/new_mask/pallas_call | solution.py:584
  (38 shorter events, 0.2 us)
Async XLA Ops:
  3.3 13.0 %copy-start.16 = (bf16[16,512]{1,0:T(8,128)(2,1)S(1)}, bf16[16,512]{1,0:T(8,128)(2,1)}, u32[]{:S(2)}) copy-start(bf16[16,512]{1,0:T(8,128)(2,1)} %get-tuple-element.31) | copy-start | bytes 49156
  3.3 13.0 %collective-permute-start = (bf16[80,512]{1,0:T(8,128)(2,1)}, bf16[80,512]{1,0:T(8,128)(2,1)S(1)}, u32[]{:S(2)}, u32[]{:S(2)}) collective-permute-start(bf16[80,512]{1,0:T(8,128)(2,1)} %get-tuple-element.30), channel_id=1, source_target_pairs={{0,68},{8,76},{16,84},{24,92},{32,100},{40,108},{48,116},{56,124},... | collective-permute-start | bytes 245768 | tf_op jit(solution)/shard_map/ppermute | solution.py:503
  16.3 4.5 %copy-start.10 = (bf16[80,512]{1,0:T(8,128)(2,1)}, bf16[80,512]{1,0:T(8,128)(2,1)S(1)}, u32[]{:S(2)}) copy-start(bf16[80,512]{1,0:T(8,128)(2,1)S(1)} %pad_maximum_fusion.2.mine) | copy-start | bytes 245764
  16.3 4.5 %collective-permute-start.1 = (bf16[80,512]{1,0:T(8,128)(2,1)S(1)}, bf16[80,512]{1,0:T(8,128)(2,1)S(1)}, u32[]{:S(2)}, u32[]{:S(2)}) collective-permute-start(bf16[80,512]{1,0:T(8,128)(2,1)S(1)} %pad_maximum_fusion.2.mine), channel_id=1, source_target_pairs={{0,2},{1,3},{2,0},{3,1},{4,6},{5,7},{6,4},{7,5},{8,10},{9,11},{10,... | collective-permute-start | bytes 245768 | tf_op jit(solution)/shard_map/ppermute | solution.py:475
  20.9 0.6 copy-start.12
  23.2 6.5 %copy-start.17 = (f32[8,128]{1,0:T(8,128)S(1)}, f32[8,128]{1,0:T(8,128)}, u32[]{:S(2)}) copy-start(f32[8,128]{1,0:T(8,128)} %get-tuple-element.34) | copy-start | bytes 12292
  23.2 6.5 %collective-permute-start.2 = (bf16[336,128]{1,0:T(8,128)(2,1)}, bf16[336,128]{1,0:T(8,128)(2,1)S(1)}, u32[]{:S(2)}, u32[]{:S(2)}) collective-permute-start(bf16[336,128]{1,0:T(8,128)(2,1)} %get-tuple-element.35), channel_id=1, source_target_pairs={{0,9},{8,1},{16,25},{24,17},{32,41},{40,33},{48,57},{56,49},{64,73... | collective-permute-start | bytes 258056 | tf_op jit(solution)/shard_map/ppermute | solution.py:513
  23.2 7.5 %collective-permute-start.3 = (bf16[320,128]{1,0:T(8,128)(2,1)}, bf16[320,128]{1,0:T(8,128)(2,1)S(1)}, u32[]{:S(2)}, u32[]{:S(2)}) collective-permute-start(bf16[320,128]{1,0:T(8,128)(2,1)} %get-tuple-element.36), channel_id=1, source_target_pairs={{8,16},{24,32},{40,48},{72,80},{88,96},{104,112},{136,144},{152,16... | collective-permute-start | bytes 245768 | tf_op jit(solution)/shard_map/ppermute | solution.py:514
  29.7 1.0 copy-start.13
  30.7 0.6 copy-start.14
  50.4 10.7 %collective-permute-start.6 = (bf16[112,512]{1,0:T(8,128)(2,1)}, bf16[112,512]{1,0:T(8,128)(2,1)S(1)}, u32[]{:S(2)}, u32[]{:S(2)}) collective-permute-start(bf16[112,512]{1,0:T(8,128)(2,1)} %get-tuple-element.37), channel_id=1, source_target_pairs={{0,6},{1,7},{2,4},{3,5},{4,2},{5,3},{6,0},{7,1},{8,14},{9,15},{10,... | collective-permute-start | bytes 344072 | tf_op jit(solution)/shard_map/ppermute | solution.py:475
  52.4 8.6 %collective-permute-start.5 = (bf16[112,512]{1,0:T(8,128)(2,1)}, bf16[112,512]{1,0:T(8,128)(2,1)S(1)}, u32[]{:S(2)}, u32[]{:S(2)}) collective-permute-start(bf16[112,512]{1,0:T(8,128)(2,1)} %get-tuple-element.37), channel_id=1, source_target_pairs={{0,4},{1,5},{2,6},{3,7},{4,0},{5,1},{6,2},{7,3},{8,12},{9,13},{10,... | collective-permute-start | bytes 344072 | tf_op jit(solution)/shard_map/ppermute | solution.py:475
  53.9 7.1 %collective-permute-start.4 = (bf16[112,512]{1,0:T(8,128)(2,1)}, bf16[112,512]{1,0:T(8,128)(2,1)S(1)}, u32[]{:S(2)}, u32[]{:S(2)}) collective-permute-start(bf16[112,512]{1,0:T(8,128)(2,1)} %get-tuple-element.37), channel_id=1, source_target_pairs={{0,2},{1,3},{2,0},{3,1},{4,6},{5,7},{6,4},{7,5},{8,10},{9,11},{10,... | collective-permute-start | bytes 344072 | tf_op jit(solution)/shard_map/ppermute | solution.py:475
  54.6 1.0 copy-start.15
  54.6 6.6 %copy-start.11 = (bf16[112,512]{1,0:T(8,128)(2,1)S(1)}, bf16[112,512]{1,0:T(8,128)(2,1)}, u32[]{:S(2)}) copy-start(bf16[112,512]{1,0:T(8,128)(2,1)} %get-tuple-element.37) | copy-start | bytes 344068
  54.6 14.4 %copy-start.6 = (bf16[640,224]{1,0:T(8,128)(2,1)S(1)}, bf16[640,224]{1,0:T(8,128)(2,1)}, u32[]{:S(2)}) copy-start(bf16[640,224]{1,0:T(8,128)(2,1)} %constant.25.clone.fold_t) | copy-start | bytes 860164
  55.6 13.4 %copy-start = (f32[1,512,512]{2,1,0:T(8,128)S(1)}, f32[1,512,512]{2,1,0:T(8,128)}, u32[]{:S(2)}) copy-start(f32[1,512,512]{2,1,0:T(8,128)} %mask.1) | copy-start | bytes 3145732
  55.6 13.3 %collective-permute-start.9 = (bf16[64,512]{1,0:T(8,128)(2,1)S(1)}, bf16[64,512]{1,0:T(8,128)(2,1)S(1)}, u32[]{:S(2)}, u32[]{:S(2)}) collective-permute-start(bf16[64,512]{1,0:T(8,128)(2,1)S(1)} %copy-done.15), channel_id=1, source_target_pairs={{0,2},{1,3},{2,0},{3,1},{4,6},{5,7},{6,4},{7,5},{8,10},{9,11},{10,... | collective-permute-start | bytes 196616 | tf_op jit(solution)/shard_map/ppermute | solution.py:475
  61.1 7.9 %copy-start.1 = (bf16[512,640]{1,0:T(8,128)(2,1)S(1)}, bf16[512,640]{1,0:T(8,128)(2,1)}, u32[]{:S(2)}) copy-start(bf16[512,640]{1,0:T(8,128)(2,1)} %constant.21.clone.freq_at.freq) | copy-start | bytes 1966084
  61.3 7.5 %collective-permute-start.7 = (bf16[112,512]{1,0:T(8,128)(2,1)S(1)}, bf16[112,512]{1,0:T(8,128)(2,1)S(1)}, u32[]{:S(2)}, u32[]{:S(2)}) collective-permute-start(bf16[112,512]{1,0:T(8,128)(2,1)S(1)} %select_convert_fusion.part_1), channel_id=1, source_target_pairs={{0,1},{1,0},{2,3},{3,2},{4,5},{5,4},{6,7},{7,6},{8,9},{9,8},{10,11... | collective-permute-start | bytes 344072 | tf_op jit(solution)/shard_map/ppermute | solution.py:475
  68.8 1.4 %collective-permute-start.8 = (f32[8,128]{1,0:T(8,128)S(1)}, f32[8,128]{1,0:T(8,128)S(1)}, u32[]{:S(2)}, u32[]{:S(2)}) collective-permute-start(f32[8,128]{1,0:T(8,128)S(1)} %broadcast_in_dim.43), channel_id=1, source_target_pairs={{0,8},{8,0},{16,24},{24,16},{32,40},{40,32},{48,56},{56,48},{64,72... | collective-permute-start | bytes 12296 | tf_op jit(solution)/shard_map/ppermute | solution.py:479
  70.2 13.5 %copy-start.7 = (f32[128,512]{1,0:T(8,128)}, f32[128,512]{1,0:T(8,128)S(1)}, u32[]{:S(2)}) copy-start(f32[128,512]{1,0:T(8,128)S(1)} %get-tuple-element.48.rims_in) | copy-start | bytes 786436
  70.3 13.4 %collective-permute-start.14 = (bf16[128,512]{1,0:T(8,128)(2,1)S(1)}, bf16[128,512]{1,0:T(8,128)(2,1)S(1)}, u32[]{:S(2)}, u32[]{:S(2)}) collective-permute-start(bf16[128,512]{1,0:T(8,128)(2,1)S(1)} %pad_maximum_fusion.1), channel_id=1, source_target_pairs={{0,4},{1,5},{2,6},{3,7},{4,0},{5,1},{6,2},{7,3},{8,12},{9,13},{10,... | collective-permute-start | bytes 393224 | tf_op jit(solution)/shard_map/ppermute | solution.py:475
  71.7 11.9 %collective-permute-start.10 = (bf16[320,128]{1,0:T(8,128)(2,1)S(1)}, bf16[320,128]{1,0:T(8,128)(2,1)S(1)}, u32[]{:S(2)}, u32[]{:S(2)}) collective-permute-start(bf16[320,128]{1,0:T(8,128)(2,1)S(1)} %get-tuple-element.42), channel_id=1, source_target_pairs={{0,8},{8,0},{16,24},{24,16},{32,40},{40,32},{48,56},{56,48},{64,72... | collective-permute-start | bytes 245768 | tf_op jit(solution)/shard_map/ppermute | solution.py:565
  71.8 11.9 %collective-permute-start.11 = (bf16[320,128]{1,0:T(8,128)(2,1)S(1)}, bf16[320,128]{1,0:T(8,128)(2,1)S(1)}, u32[]{:S(2)}, u32[]{:S(2)}) collective-permute-start(bf16[320,128]{1,0:T(8,128)(2,1)S(1)} %get-tuple-element.43), channel_id=1, source_target_pairs={{8,16},{24,32},{40,48},{72,80},{88,96},{104,112},{136,144},{152,16... | collective-permute-start | bytes 245768 | tf_op jit(solution)/shard_map/ppermute | solution.py:566
  73.8 3.7 %collective-permute-start.12 = (f32[8,128]{1,0:T(8,128)S(1)}, f32[8,128]{1,0:T(8,128)S(1)}, u32[]{:S(2)}, u32[]{:S(2)}) collective-permute-start(f32[8,128]{1,0:T(8,128)S(1)} %broadcast_add_fusion), channel_id=1, source_target_pairs={{0,16},{8,24},{16,0},{24,8},{32,48},{40,56},{48,32},{56,40},{64,80... | collective-permute-start | bytes 12296 | tf_op jit(solution)/shard_map/ppermute | solution.py:479
  77.6 5.5 %collective-permute-start.13 = (f32[8,128]{1,0:T(8,128)S(1)}, f32[8,128]{1,0:T(8,128)S(1)}, u32[]{:S(2)}, u32[]{:S(2)}) collective-permute-start(f32[8,128]{1,0:T(8,128)S(1)} %add.96), channel_id=1, source_target_pairs={{0,32},{8,40},{16,48},{24,56},{32,0},{40,8},{48,16},{56,24},{64,96... | collective-permute-start | bytes 12296 | tf_op jit(solution)/shard_map/ppermute | solution.py:479
  83.7 0.6 copy-start.2
  83.7 0.6 copy-start.4
  84.3 15.2 %copy-start.8 = (f32[8,128]{1,0:T(8,128)S(1)}, f32[8,128]{1,0:T(8,128)}, u32[]{:S(2)}) copy-start(f32[8,128]{1,0:T(8,128)} %add.97.weight) | copy-start | bytes 12292
  84.3 18.8 %copy-start.3 = (bf16[320,128]{1,0:T(8,128)(2,1)S(1)}, bf16[320,128]{1,0:T(8,128)(2,1)}, u32[]{:S(2)}) copy-start(bf16[320,128]{1,0:T(8,128)(2,1)} %copy-done.2) | copy-start | bytes 245764
  84.3 18.8 %copy-start.5 = (bf16[320,128]{1,0:T(8,128)(2,1)S(1)}, bf16[320,128]{1,0:T(8,128)(2,1)}, u32[]{:S(2)}) copy-start(bf16[320,128]{1,0:T(8,128)(2,1)} %copy-done.4) | copy-start | bytes 245764
  86.1 17.1 %copy-start.9 = (f32[8]{0:T(128)S(1)}, f32[8]{0:T(128)}, u32[]{:S(2)}) copy-start(f32[8]{0:T(128)} %param.14) | copy-start | bytes 100
  86.1 17.1 %collective-permute-start.18 = (bf16[256,512]{1,0:T(8,128)(2,1)S(1)}, bf16[256,512]{1,0:T(8,128)(2,1)S(1)}, u32[]{:S(2)}, u32[]{:S(2)}) collective-permute-start(bf16[256,512]{1,0:T(8,128)(2,1)S(1)} %pad_maximum_fusion.near), channel_id=1, source_target_pairs={{0,1},{1,0},{2,3},{3,2},{4,5},{5,4},{6,7},{7,6},{8,9},{9,8},{10,11... | collective-permute-start | bytes 786440 | tf_op jit(solution)/shard_map/ppermute | solution.py:475
  87.3 10.3 %collective-permute-start.15 = (bf16[80,512]{1,0:T(8,128)(2,1)}, bf16[80,512]{1,0:T(8,128)(2,1)S(1)}, u32[]{:S(2)}, u32[]{:S(2)}) collective-permute-start(bf16[80,512]{1,0:T(8,128)(2,1)} %row_rims.1), channel_id=1, source_target_pairs={{0,64},{8,72},{16,80},{24,88},{32,96},{40,104},{48,112},{56,120},{... | collective-permute-start | bytes 245768 | tf_op jit(solution)/shard_map/ppermute | solution.py:580
  97.6 5.5 %collective-permute-start.16 = (bf16[80,512]{1,0:T(8,128)(2,1)S(1)}, bf16[80,512]{1,0:T(8,128)(2,1)S(1)}, u32[]{:S(2)}, u32[]{:S(2)}) collective-permute-start(bf16[80,512]{1,0:T(8,128)(2,1)S(1)} %collective-permute-done.15.mine), channel_id=1, source_target_pairs={{0,2},{1,3},{2,0},{3,1},{4,6},{5,7},{6,4},{7,5},{8,10},{9,11},{10,... | collective-permute-start | bytes 245768 | tf_op jit(solution)/shard_map/ppermute | solution.py:475
  99.5 3.6 %collective-permute-start.17 = (f32[8,128]{1,0:T(8,128)S(1)}, f32[8,128]{1,0:T(8,128)S(1)}, u32[]{:S(2)}, u32[]{:S(2)}) collective-permute-start(f32[8,128]{1,0:T(8,128)S(1)} %copy-done.8), channel_id=1, source_target_pairs={{0,128},{8,136},{16,144},{24,152},{32,160},{40,168},{48,176},{56,1... | collective-permute-start | bytes 12296 | tf_op jit(solution)/shard_map/ppermute | solution.py:479

commit v5 on v4

--- a/solution.py
+++ b/solution.py
@@ -564,8 +564,7 @@
     far = src_swap(near, 4, groups)
     side_1 = lax.ppermute(side_1, "tile", col_swap)
     side_2 = lax.ppermute(side_2, "tile", col_next)
-    for distance in (2, 4):
-        weight = weight + tile_swap(weight, distance, tiles)
+    weight = (weight + tile_swap(weight, 2, tiles)) + (tile_swap(weight, 4, tiles) + tile_swap(weight, 6, tiles))
     side_1, side_2, weight, far = lax.optimization_barrier((side_1, side_2, weight, far))
     rim = pl.pallas_call(
         rim_kernel,

time: 106 us -> 106 us (level)
    ppermute x4 -> x5, waiting for transfers between devices: 7.91 us -> 2.88 us  [tile_swap(): lax.ppermute(block, 'tile', [(i, i ^ distance) for i in range(count)])]
    ppermute x9, waiting for transfers between devices: 12.2 us -> 16.9 us  [src_swap(): return lax.ppermute(block, 'src', [(i, i ^ distance) for i in range(count)])]
    ppermute x9, starting transfers between devices: 14 us -> 15.5 us  [src_swap(): return lax.ppermute(block, 'src', [(i, i ^ distance) for i in range(count)])]
    ppermute x1, starting transfers between devices: 7.16 us -> 5.91 us  [per_device(): lax.ppermute(rim, ('tile', 'src'), route_of(row_swap, row_ring, groups))]
    ppermute x4 -> x5, starting transfers between devices: 5 us -> 4.42 us  [tile_swap(): lax.ppermute(block, 'tile', [(i, i ^ distance) for i in range(count)])]
  transfers between devices with their start and end apart: 19 -> 20, of which waited for: 10 -> 10; matrix products, arithmetic and copies ran while one was open for 2% -> 2% of each run, Pallas kernels for 1% -> 1%
where the time goes in v5:
time: 106 us; the launch traced here: 105 us
  starting transfers between devices  42.6 us (40%)
  waiting for transfers between devices  29.5 us (28%)
  Pallas kernels  28.4 us (27%)
  other arithmetic  2.48 us (2%)
  local copies, waits for them, and re-layouts  1.35 us (1%)
  between operations  1.15 us (1%)
    pallas_call x1, Pallas kernels, per_device(): pl.pallas_call(source_kernel, out_shape=(shaped((ROWS, 2 * HALF), BF), sh...  18.9 us
    ppermute x9, waiting for transfers between devices, src_swap(): return lax.ppermute(block, 'src', [(i, i ^ distance) for i in range(count)])  16.9 us
    ppermute x9, starting transfers between devices, src_swap(): return lax.ppermute(block, 'src', [(i, i ^ distance) for i in range(count)])  15.5 us
    ppermute x1, starting transfers between devices, per_device(): lax.ppermute(vert, ('tile', 'src'), route_of(row_swap, row_ring, groups, 4))  9.01 us
    ppermute x2, starting transfers between devices, per_device(): side_2 = lax.ppermute(side_2, 'tile', col_next)  7.76 us
    ppermute x1, starting transfers between devices, per_device(): lax.ppermute(rim, ('tile', 'src'), route_of(row_swap, row_ring, groups))  5.91 us
    ppermute x5, starting transfers between devices, tile_swap(): lax.ppermute(block, 'tile', [(i, i ^ distance) for i in range(count)])  4.42 us
    ppermute x1, waiting for transfers between devices, per_device(): lax.ppermute(vert, ('tile', 'src'), route_of(row_swap, row_ring, groups, 4))  3.99 us
  transfers between devices with their start and end apart: 20, of which 10 were waited for; matrix products, arithmetic and copies ran while one was open for 2% of the time, Pallas kernels for 1%

profile of v5, /device:TPU:32, one launch (start us, length us, event | category | flops | bytes accessed | tf_op | source)
XLA Modules:
  0.0 105.4 jit_solution(2643501778474671987)
XLA Ops:
  0.6 2.7 %edges.1 = (bf16[80,512]{1,0:T(8,128)(2,1)}, bf16[256,128]{1,0:T(8,128)(2,1)}, bf16[256,128]{1,0:T(8,128)(2,1)}, bf16[16,512]{1,0:T(8,128)(2,1)}) custom-call(s32[2,8]{1,0:T(2,128)} %bitcast.13, f32[1,8]{1,0:T(1,128)} %bitcast.8, f32[1,512,512]{2,1,0:T(8,128)} %mask.1), custom_call_target="tpu_custom_call" | custom-call | tf_op jit(solution)/shard_map/edges/pallas_call | solution.py:493
  3.3 9.0 %collective-permute-start = (bf16[80,512]{1,0:T(8,128)(2,1)}, bf16[80,512]{1,0:T(8,128)(2,1)S(1)}, u32[]{:S(2)}, u32[]{:S(2)}) collective-permute-start(bf16[80,512]{1,0:T(8,128)(2,1)} %get-tuple-element.30), channel_id=1, source_target_pairs={{0,68},{8,76},{16,84},{24,92},{32,100},{40,108},{48,116},{56,124},... | collective-permute-start | bytes 245768 | tf_op jit(solution)/shard_map/ppermute | solution.py:503
  12.3 4.0 %collective-permute-done = bf16[80,512]{1,0:T(8,128)(2,1)S(1)} collective-permute-done((bf16[80,512]{1,0:T(8,128)(2,1)}, bf16[80,512]{1,0:T(8,128)(2,1)S(1)}, u32[]{:S(2)}, u32[]{:S(2)}) %collective-permute-start) | collective-permute-done | bytes 81952 | tf_op jit(solution)/shard_map/ppermute | solution.py:503
  16.3 1.7 %collective-permute-start.1 = (bf16[80,512]{1,0:T(8,128)(2,1)S(1)}, bf16[80,512]{1,0:T(8,128)(2,1)S(1)}, u32[]{:S(2)}, u32[]{:S(2)}) collective-permute-start(bf16[80,512]{1,0:T(8,128)(2,1)S(1)} %pad_maximum_fusion.2.mine), channel_id=1, source_target_pairs={{0,2},{1,3},{2,0},{3,1},{4,6},{5,7},{6,4},{7,5},{8,10},{9,11},{10,... | collective-permute-start | bytes 245768 | tf_op jit(solution)/shard_map/ppermute | solution.py:475
  18.0 2.8 %collective-permute-done.1.theirs = bf16[80,512]{1,0:T(8,128)(2,1)S(1)} collective-permute-done((bf16[80,512]{1,0:T(8,128)(2,1)S(1)}, bf16[80,512]{1,0:T(8,128)(2,1)S(1)}, u32[]{:S(2)}, u32[]{:S(2)}) %collective-permute-start.1) | collective-permute-done | bytes 81952 | tf_op jit(solution)/shard_map/ppermute | solution.py:475
  20.9 0.6 copy-done.12
  21.5 1.7 %corners.1 = (bf16[336,128]{1,0:T(8,128)(2,1)}, bf16[320,128]{1,0:T(8,128)(2,1)}, f32[8,128]{1,0:T(8,128)}) custom-call(bf16[80,512]{1,0:T(8,128)(2,1)} %copy-done.10, bf16[80,512]{1,0:T(8,128)(2,1)} %copy-done.12, bf16[256,128]{1,0:T(8,128)(2,1)} %get-tuple-element.32.side_1, bf16[256,128]{1,0:T(8,128)(2,1)} %get-tuple-element.33.side_2), custom_call_target="tpu_custom_call" | custom-call | tf_op jit(solution)/shard_map/corners/pallas_call | solution.py:506
  23.2 0.0 collective-permute-start.2
  23.2 5.1 %collective-permute-start.3 = (bf16[320,128]{1,0:T(8,128)(2,1)}, bf16[320,128]{1,0:T(8,128)(2,1)S(1)}, u32[]{:S(2)}, u32[]{:S(2)}) collective-permute-start(bf16[320,128]{1,0:T(8,128)(2,1)} %get-tuple-element.36), channel_id=1, source_target_pairs={{8,16},{24,32},{40,48},{72,80},{88,96},{104,112},{136,144},{152,16... | collective-permute-start | bytes 245768 | tf_op jit(solution)/shard_map/ppermute | solution.py:514
  28.3 1.4 %collective-permute-done.2.side_1 = bf16[336,128]{1,0:T(8,128)(2,1)S(1)} collective-permute-done((bf16[336,128]{1,0:T(8,128)(2,1)}, bf16[336,128]{1,0:T(8,128)(2,1)S(1)}, u32[]{:S(2)}, u32[]{:S(2)}) %collective-permute-start.2) | collective-permute-done | bytes 86048 | tf_op jit(solution)/shard_map/ppermute | solution.py:513
  29.7 0.6 convert_add_fusion.info
  30.3 0.4 collective-permute-done.3.side_2
  30.7 0.0 copy-done.13
  30.7 0.6 copy-done.14
  31.3 18.9 %sources.1 = (bf16[112,512]{1,0:T(8,128)(2,1)}, bf16[64,512]{1,0:T(8,128)(2,1)}) custom-call(f32[8,128]{1,0:T(8,128)} %convert_add_fusion.info, bf16[80,512]{1,0:T(8,128)(2,1)} %copy-done.10, bf16[80,512]{1,0:T(8,128)(2,1)} %copy-done.12, bf16[336,128]{1,0:T(8,128)(2,1)} %copy-done.13, bf16[320,128]{1,0:T(8,128)(2,1)} %copy-done.14, f32[1,512,512]{2,1,0:T(8,128)} %mask.1, ...), custom_call_target="tpu_custom_call" | custom-call | tf_op jit(solution)/shard_map/sources/pallas_call | solution.py:517
  50.3 2.0 %collective-permute-start.6 = (bf16[112,512]{1,0:T(8,128)(2,1)}, bf16[112,512]{1,0:T(8,128)(2,1)S(1)}, u32[]{:S(2)}, u32[]{:S(2)}) collective-permute-start(bf16[112,512]{1,0:T(8,128)(2,1)} %get-tuple-element.37), channel_id=1, source_target_pairs={{0,6},{1,7},{2,4},{3,5},{4,2},{5,3},{6,0},{7,1},{8,14},{9,15},{10,... | collective-permute-start | bytes 344072 | tf_op jit(solution)/shard_map/ppermute | solution.py:475
  52.3 1.5 %collective-permute-start.5 = (bf16[112,512]{1,0:T(8,128)(2,1)}, bf16[112,512]{1,0:T(8,128)(2,1)S(1)}, u32[]{:S(2)}, u32[]{:S(2)}) collective-permute-start(bf16[112,512]{1,0:T(8,128)(2,1)} %get-tuple-element.37), channel_id=1, source_target_pairs={{0,4},{1,5},{2,6},{3,7},{4,0},{5,1},{6,2},{7,3},{8,12},{9,13},{10,... | collective-permute-start | bytes 344072 | tf_op jit(solution)/shard_map/ppermute | solution.py:475
  53.7 0.7 collective-permute-start.4
  54.5 0.0 copy-start.11
  54.5 0.0 copy-start.6
  54.5 1.0 convert_element_type.25
  55.5 0.0 copy-start
  55.5 1.4 %collective-permute-start.9 = (bf16[64,512]{1,0:T(8,128)(2,1)S(1)}, bf16[64,512]{1,0:T(8,128)(2,1)S(1)}, u32[]{:S(2)}, u32[]{:S(2)}) collective-permute-start(bf16[64,512]{1,0:T(8,128)(2,1)S(1)} %copy-done.15), channel_id=1, source_target_pairs={{0,2},{1,3},{2,0},{3,1},{4,6},{5,7},{6,4},{7,5},{8,10},{9,11},{10,... | collective-permute-start | bytes 196616 | tf_op jit(solution)/shard_map/ppermute | solution.py:475
  56.9 4.0 %collective-permute-done.4 = bf16[112,512]{1,0:T(8,128)(2,1)S(1)} collective-permute-done((bf16[112,512]{1,0:T(8,128)(2,1)}, bf16[112,512]{1,0:T(8,128)(2,1)S(1)}, u32[]{:S(2)}, u32[]{:S(2)}) %collective-permute-start.4) | collective-permute-done | bytes 114720 | tf_op jit(solution)/shard_map/ppermute | solution.py:475
  60.9 0.0 collective-permute-done.5
  60.9 0.0 copy-start.1
  60.9 0.0 collective-permute-done.6
  61.0 0.1 select_convert_fusion.part_1
  61.1 2.2 %collective-permute-start.7 = (bf16[112,512]{1,0:T(8,128)(2,1)S(1)}, bf16[112,512]{1,0:T(8,128)(2,1)S(1)}, u32[]{:S(2)}, u32[]{:S(2)}) collective-permute-start(bf16[112,512]{1,0:T(8,128)(2,1)S(1)} %select_convert_fusion.part_1), channel_id=1, source_target_pairs={{0,1},{1,0},{2,3},{3,2},{4,5},{5,4},{6,7},{7,6},{8,9},{9,8},{10,11... | collective-permute-start | bytes 344072 | tf_op jit(solution)/shard_map/ppermute | solution.py:475
  63.3 5.4 %collective-permute-done.7.part_2 = bf16[112,512]{1,0:T(8,128)(2,1)S(1)} collective-permute-done((bf16[112,512]{1,0:T(8,128)(2,1)S(1)}, bf16[112,512]{1,0:T(8,128)(2,1)S(1)}, u32[]{:S(2)}, u32[]{:S(2)}) %collective-permute-start.7) | collective-permute-done | bytes 114720 | tf_op jit(solution)/shard_map/ppermute | solution.py:475
  68.7 0.1 collective-permute-start.8
  68.8 0.0 collective-permute-done.9
  68.9 1.2 %mask_gradient.1 = (f32[512,512]{1,0:T(8,128)S(1)}, f32[128,512]{1,0:T(8,128)S(1)}, bf16[320,128]{1,0:T(8,128)(2,1)S(1)}, bf16[320,128]{1,0:T(8,128)(2,1)S(1)}) custom-call(f32[1,512,512]{2,1,0:T(8,128)S(1)} %copy-done, bf16[112,512]{1,0:T(8,128)(2,1)S(1)} %select_convert_fusion.part_1, bf16[112,512]{1,0:T(8,128)(2,1)S(1)} %collective-permute-done.7.part_2, ...), custom_call_target="tpu_custom_call" | custom-call | tf_op jit(solution)/shard_map/mask_gradient/pallas_call | solution.py:553
  70.1 0.0 copy-start.7
  70.1 0.0 collective-permute-done.8
  70.1 1.9 %collective-permute-start.14 = (f32[8,128]{1,0:T(8,128)S(1)}, f32[8,128]{1,0:T(8,128)S(1)}, u32[]{:S(2)}, u32[]{:S(2)}) collective-permute-start(f32[8,128]{1,0:T(8,128)S(1)} %broadcast_add_fusion), channel_id=1, source_target_pairs={{0,48},{8,56},{16,32},{24,40},{32,16},{40,24},{48,0},{56,8},{64,11... | collective-permute-start | bytes 12296 | tf_op jit(solution)/shard_map/ppermute | solution.py:479
  72.0 0.3 collective-permute-start.13
  72.3 1.4 %collective-permute-start.12 = (f32[8,128]{1,0:T(8,128)S(1)}, f32[8,128]{1,0:T(8,128)S(1)}, u32[]{:S(2)}, u32[]{:S(2)}) collective-permute-start(f32[8,128]{1,0:T(8,128)S(1)} %broadcast_add_fusion), channel_id=1, source_target_pairs={{0,16},{8,24},{16,0},{24,8},{32,48},{40,56},{48,32},{56,40},{64,80... | collective-permute-start | bytes 12296 | tf_op jit(solution)/shard_map/ppermute | solution.py:479
  73.7 0.0 collective-permute-start.10
  73.7 2.7 %collective-permute-start.11 = (bf16[320,128]{1,0:T(8,128)(2,1)S(1)}, bf16[320,128]{1,0:T(8,128)(2,1)S(1)}, u32[]{:S(2)}, u32[]{:S(2)}) collective-permute-start(bf16[320,128]{1,0:T(8,128)(2,1)S(1)} %get-tuple-element.43), channel_id=1, source_target_pairs={{8,16},{24,32},{40,48},{72,80},{88,96},{104,112},{136,144},{152,16... | collective-permute-start | bytes 245768 | tf_op jit(solution)/shard_map/ppermute | solution.py:566
  76.4 0.0 collective-permute-done.14
  76.4 2.0 %collective-permute-start.15 = (bf16[128,512]{1,0:T(8,128)(2,1)S(1)}, bf16[128,512]{1,0:T(8,128)(2,1)S(1)}, u32[]{:S(2)}, u32[]{:S(2)}) collective-permute-start(bf16[128,512]{1,0:T(8,128)(2,1)S(1)} %pad_maximum_fusion.1), channel_id=1, source_target_pairs={{0,4},{1,5},{2,6},{3,7},{4,0},{5,1},{6,2},{7,3},{8,12},{9,13},{10,... | collective-permute-start | bytes 393224 | tf_op jit(solution)/shard_map/ppermute | solution.py:475
  78.4 0.0 collective-permute-done.13
  78.4 0.0 collective-permute-done.12
  78.4 0.6 add_add_fusion.weight
  79.0 0.0 collective-permute-done.10.side_1
  79.0 0.5 collective-permute-done.11.side_2
  79.5 4.7 %collective-permute-done.15 = bf16[128,512]{1,0:T(8,128)(2,1)S(1)} collective-permute-done((bf16[128,512]{1,0:T(8,128)(2,1)S(1)}, bf16[128,512]{1,0:T(8,128)(2,1)S(1)}, u32[]{:S(2)}, u32[]{:S(2)}) %collective-permute-start.15) | collective-permute-done | bytes 131104 | tf_op jit(solution)/shard_map/ppermute | solution.py:475
  84.2 0.0 copy-done.7
  84.2 0.0 copy-done.2
  84.2 0.0 copy-done.4
  84.2 0.0 copy-start.8
  84.2 0.0 copy-start.3
  84.3 1.8 %row_rims.1 = bf16[80,512]{1,0:T(8,128)(2,1)} custom-call(f32[128,512]{1,0:T(8,128)} %copy-done.7, bf16[320,128]{1,0:T(8,128)(2,1)} %copy-done.2, bf16[320,128]{1,0:T(8,128)(2,1)} %copy-done.4, f32[8,128]{1,0:T(8,128)} %add_add_fusion.weight), custom_call_target="tpu_custom_call" | custom-call | tf_op jit(solution)/shard_map/row_rims/pallas_call | solution.py:569
  86.0 1.6 %collective-permute-start.19 = (bf16[256,512]{1,0:T(8,128)(2,1)S(1)}, bf16[256,512]{1,0:T(8,128)(2,1)S(1)}, u32[]{:S(2)}, u32[]{:S(2)}) collective-permute-start(bf16[256,512]{1,0:T(8,128)(2,1)S(1)} %pad_maximum_fusion.near), channel_id=1, source_target_pairs={{0,1},{1,0},{2,3},{3,2},{4,5},{5,4},{6,7},{7,6},{8,9},{9,8},{10,11... | collective-permute-start | bytes 786440 | tf_op jit(solution)/shard_map/ppermute | solution.py:475
  87.6 5.9 %collective-permute-start.16 = (bf16[80,512]{1,0:T(8,128)(2,1)}, bf16[80,512]{1,0:T(8,128)(2,1)S(1)}, u32[]{:S(2)}, u32[]{:S(2)}) collective-permute-start(bf16[80,512]{1,0:T(8,128)(2,1)} %row_rims.1), channel_id=1, source_target_pairs={{0,64},{8,72},{16,80},{24,88},{32,96},{40,104},{48,112},{56,120},{... | collective-permute-start | bytes 245768 | tf_op jit(solution)/shard_map/ppermute | solution.py:579
  93.5 3.5 %collective-permute-done.16.mine = bf16[80,512]{1,0:T(8,128)(2,1)S(1)} collective-permute-done((bf16[80,512]{1,0:T(8,128)(2,1)}, bf16[80,512]{1,0:T(8,128)(2,1)S(1)}, u32[]{:S(2)}, u32[]{:S(2)}) %collective-permute-start.16) | collective-permute-done | bytes 81952 | tf_op jit(solution)/shard_map/ppermute | solution.py:579
  97.1 2.5 %collective-permute-start.17 = (bf16[80,512]{1,0:T(8,128)(2,1)S(1)}, bf16[80,512]{1,0:T(8,128)(2,1)S(1)}, u32[]{:S(2)}, u32[]{:S(2)}) collective-permute-start(bf16[80,512]{1,0:T(8,128)(2,1)S(1)} %collective-permute-done.16.mine), channel_id=1, source_target_pairs={{0,2},{1,3},{2,0},{3,1},{4,6},{5,7},{6,4},{7,5},{8,10},{9,11},{10,... | collective-permute-start | bytes 245768 | tf_op jit(solution)/shard_map/ppermute | solution.py:475
  99.5 0.7 collective-permute-start.18
  100.3 2.9 %collective-permute-done.18.other = f32[8,128]{1,0:T(8,128)S(1)} collective-permute-done((f32[8,128]{1,0:T(8,128)S(1)}, f32[8,128]{1,0:T(8,128)S(1)}, u32[]{:S(2)}, u32[]{:S(2)}) %collective-permute-start.18) | collective-permute-done | bytes 4128 | tf_op jit(solution)/shard_map/ppermute | solution.py:479
  103.1 0.0 collective-permute-done.17.theirs
  103.2 0.0 collective-permute-done.19.far
  103.2 0.0 copy-done.5
  103.2 2.1 %new_mask.1 = (f32[1,512,512]{2,1,0:T(8,128)}, f32[1,512,512]{2,1,0:T(8,128)}, f32[1,8]{1,0:T(1,128)}) custom-call(f32[512,512]{1,0:T(8,128)S(1)} %get-tuple-element.38.base_in, bf16[320,128]{1,0:T(8,128)(2,1)S(1)} %copy-done.3, bf16[320,128]{1,0:T(8,128)(2,1)S(1)} %copy-done.5, bf16[80,512]{1,0:T(8,128)(2,1)S(1)} %collective-permute-done.16.mine, ...), custom_call_target="tpu_custom_call" | custom-call | tf_op jit(solution)/shard_map/new_mask/pallas_call | solution.py:583
  (39 shorter events, 0.2 us)
Async XLA Ops:
  3.3 13.0 %copy-start.16 = (bf16[16,512]{1,0:T(8,128)(2,1)S(1)}, bf16[16,512]{1,0:T(8,128)(2,1)}, u32[]{:S(2)}) copy-start(bf16[16,512]{1,0:T(8,128)(2,1)} %get-tuple-element.31) | copy-start | bytes 49156
  3.3 13.0 %collective-permute-start = (bf16[80,512]{1,0:T(8,128)(2,1)}, bf16[80,512]{1,0:T(8,128)(2,1)S(1)}, u32[]{:S(2)}, u32[]{:S(2)}) collective-permute-start(bf16[80,512]{1,0:T(8,128)(2,1)} %get-tuple-element.30), channel_id=1, source_target_pairs={{0,68},{8,76},{16,84},{24,92},{32,100},{40,108},{48,116},{56,124},... | collective-permute-start | bytes 245768 | tf_op jit(solution)/shard_map/ppermute | solution.py:503
  16.3 4.5 %copy-start.10 = (bf16[80,512]{1,0:T(8,128)(2,1)}, bf16[80,512]{1,0:T(8,128)(2,1)S(1)}, u32[]{:S(2)}) copy-start(bf16[80,512]{1,0:T(8,128)(2,1)S(1)} %pad_maximum_fusion.2.mine) | copy-start | bytes 245764
  16.3 4.5 %collective-permute-start.1 = (bf16[80,512]{1,0:T(8,128)(2,1)S(1)}, bf16[80,512]{1,0:T(8,128)(2,1)S(1)}, u32[]{:S(2)}, u32[]{:S(2)}) collective-permute-start(bf16[80,512]{1,0:T(8,128)(2,1)S(1)} %pad_maximum_fusion.2.mine), channel_id=1, source_target_pairs={{0,2},{1,3},{2,0},{3,1},{4,6},{5,7},{6,4},{7,5},{8,10},{9,11},{10,... | collective-permute-start | bytes 245768 | tf_op jit(solution)/shard_map/ppermute | solution.py:475
  20.9 0.6 copy-start.12
  23.2 6.5 %copy-start.17 = (f32[8,128]{1,0:T(8,128)S(1)}, f32[8,128]{1,0:T(8,128)}, u32[]{:S(2)}) copy-start(f32[8,128]{1,0:T(8,128)} %get-tuple-element.34) | copy-start | bytes 12292
  23.2 6.5 %collective-permute-start.2 = (bf16[336,128]{1,0:T(8,128)(2,1)}, bf16[336,128]{1,0:T(8,128)(2,1)S(1)}, u32[]{:S(2)}, u32[]{:S(2)}) collective-permute-start(bf16[336,128]{1,0:T(8,128)(2,1)} %get-tuple-element.35), channel_id=1, source_target_pairs={{0,9},{8,1},{16,25},{24,17},{32,41},{40,33},{48,57},{56,49},{64,73... | collective-permute-start | bytes 258056 | tf_op jit(solution)/shard_map/ppermute | solution.py:513
  23.2 7.5 %collective-permute-start.3 = (bf16[320,128]{1,0:T(8,128)(2,1)}, bf16[320,128]{1,0:T(8,128)(2,1)S(1)}, u32[]{:S(2)}, u32[]{:S(2)}) collective-permute-start(bf16[320,128]{1,0:T(8,128)(2,1)} %get-tuple-element.36), channel_id=1, source_target_pairs={{8,16},{24,32},{40,48},{72,80},{88,96},{104,112},{136,144},{152,16... | collective-permute-start | bytes 245768 | tf_op jit(solution)/shard_map/ppermute | solution.py:514
  29.7 1.0 copy-start.13
  30.7 0.6 copy-start.14
  50.3 10.7 %collective-permute-start.6 = (bf16[112,512]{1,0:T(8,128)(2,1)}, bf16[112,512]{1,0:T(8,128)(2,1)S(1)}, u32[]{:S(2)}, u32[]{:S(2)}) collective-permute-start(bf16[112,512]{1,0:T(8,128)(2,1)} %get-tuple-element.37), channel_id=1, source_target_pairs={{0,6},{1,7},{2,4},{3,5},{4,2},{5,3},{6,0},{7,1},{8,14},{9,15},{10,... | collective-permute-start | bytes 344072 | tf_op jit(solution)/shard_map/ppermute | solution.py:475
  52.3 8.6 %collective-permute-start.5 = (bf16[112,512]{1,0:T(8,128)(2,1)}, bf16[112,512]{1,0:T(8,128)(2,1)S(1)}, u32[]{:S(2)}, u32[]{:S(2)}) collective-permute-start(bf16[112,512]{1,0:T(8,128)(2,1)} %get-tuple-element.37), channel_id=1, source_target_pairs={{0,4},{1,5},{2,6},{3,7},{4,0},{5,1},{6,2},{7,3},{8,12},{9,13},{10,... | collective-permute-start | bytes 344072 | tf_op jit(solution)/shard_map/ppermute | solution.py:475
  53.7 7.1 %collective-permute-start.4 = (bf16[112,512]{1,0:T(8,128)(2,1)}, bf16[112,512]{1,0:T(8,128)(2,1)S(1)}, u32[]{:S(2)}, u32[]{:S(2)}) collective-permute-start(bf16[112,512]{1,0:T(8,128)(2,1)} %get-tuple-element.37), channel_id=1, source_target_pairs={{0,2},{1,3},{2,0},{3,1},{4,6},{5,7},{6,4},{7,5},{8,10},{9,11},{10,... | collective-permute-start | bytes 344072 | tf_op jit(solution)/shard_map/ppermute | solution.py:475
  54.4 1.0 copy-start.15
  54.5 6.6 %copy-start.11 = (bf16[112,512]{1,0:T(8,128)(2,1)S(1)}, bf16[112,512]{1,0:T(8,128)(2,1)}, u32[]{:S(2)}) copy-start(bf16[112,512]{1,0:T(8,128)(2,1)} %get-tuple-element.37) | copy-start | bytes 344068
  54.5 14.4 %copy-start.6 = (bf16[640,224]{1,0:T(8,128)(2,1)S(1)}, bf16[640,224]{1,0:T(8,128)(2,1)}, u32[]{:S(2)}) copy-start(bf16[640,224]{1,0:T(8,128)(2,1)} %constant.25.clone.fold_t) | copy-start | bytes 860164
  55.5 13.4 %copy-start = (f32[1,512,512]{2,1,0:T(8,128)S(1)}, f32[1,512,512]{2,1,0:T(8,128)}, u32[]{:S(2)}) copy-start(f32[1,512,512]{2,1,0:T(8,128)} %mask.1) | copy-start | bytes 3145732
  55.5 13.3 %collective-permute-start.9 = (bf16[64,512]{1,0:T(8,128)(2,1)S(1)}, bf16[64,512]{1,0:T(8,128)(2,1)S(1)}, u32[]{:S(2)}, u32[]{:S(2)}) collective-permute-start(bf16[64,512]{1,0:T(8,128)(2,1)S(1)} %copy-done.15), channel_id=1, source_target_pairs={{0,2},{1,3},{2,0},{3,1},{4,6},{5,7},{6,4},{7,5},{8,10},{9,11},{10,... | collective-permute-start | bytes 196616 | tf_op jit(solution)/shard_map/ppermute | solution.py:475
  60.9 7.9 %copy-start.1 = (bf16[512,640]{1,0:T(8,128)(2,1)S(1)}, bf16[512,640]{1,0:T(8,128)(2,1)}, u32[]{:S(2)}) copy-start(bf16[512,640]{1,0:T(8,128)(2,1)} %constant.21.clone.freq_at.freq) | copy-start | bytes 1966084
  61.1 7.5 %collective-permute-start.7 = (bf16[112,512]{1,0:T(8,128)(2,1)S(1)}, bf16[112,512]{1,0:T(8,128)(2,1)S(1)}, u32[]{:S(2)}, u32[]{:S(2)}) collective-permute-start(bf16[112,512]{1,0:T(8,128)(2,1)S(1)} %select_convert_fusion.part_1), channel_id=1, source_target_pairs={{0,1},{1,0},{2,3},{3,2},{4,5},{5,4},{6,7},{7,6},{8,9},{9,8},{10,11... | collective-permute-start | bytes 344072 | tf_op jit(solution)/shard_map/ppermute | solution.py:475
  68.7 1.4 %collective-permute-start.8 = (f32[8,128]{1,0:T(8,128)S(1)}, f32[8,128]{1,0:T(8,128)S(1)}, u32[]{:S(2)}, u32[]{:S(2)}) collective-permute-start(f32[8,128]{1,0:T(8,128)S(1)} %broadcast_in_dim.43), channel_id=1, source_target_pairs={{0,8},{8,0},{16,24},{24,16},{32,40},{40,32},{48,56},{56,48},{64,72... | collective-permute-start | bytes 12296 | tf_op jit(solution)/shard_map/ppermute | solution.py:479
  70.1 14.1 %copy-start.7 = (f32[128,512]{1,0:T(8,128)}, f32[128,512]{1,0:T(8,128)S(1)}, u32[]{:S(2)}) copy-start(f32[128,512]{1,0:T(8,128)S(1)} %get-tuple-element.48.rims_in) | copy-start | bytes 786436
  70.1 6.3 %collective-permute-start.14 = (f32[8,128]{1,0:T(8,128)S(1)}, f32[8,128]{1,0:T(8,128)S(1)}, u32[]{:S(2)}, u32[]{:S(2)}) collective-permute-start(f32[8,128]{1,0:T(8,128)S(1)} %broadcast_add_fusion), channel_id=1, source_target_pairs={{0,48},{8,56},{16,32},{24,40},{32,16},{40,24},{48,0},{56,8},{64,11... | collective-permute-start | bytes 12296 | tf_op jit(solution)/shard_map/ppermute | solution.py:479
  72.0 6.4 %collective-permute-start.13 = (f32[8,128]{1,0:T(8,128)S(1)}, f32[8,128]{1,0:T(8,128)S(1)}, u32[]{:S(2)}, u32[]{:S(2)}) collective-permute-start(f32[8,128]{1,0:T(8,128)S(1)} %broadcast_add_fusion), channel_id=1, source_target_pairs={{0,32},{8,40},{16,48},{24,56},{32,0},{40,8},{48,16},{56,24},{64,96... | collective-permute-start | bytes 12296 | tf_op jit(solution)/shard_map/ppermute | solution.py:479
  72.3 6.1 %collective-permute-start.12 = (f32[8,128]{1,0:T(8,128)S(1)}, f32[8,128]{1,0:T(8,128)S(1)}, u32[]{:S(2)}, u32[]{:S(2)}) collective-permute-start(f32[8,128]{1,0:T(8,128)S(1)} %broadcast_add_fusion), channel_id=1, source_target_pairs={{0,16},{8,24},{16,0},{24,8},{32,48},{40,56},{48,32},{56,40},{64,80... | collective-permute-start | bytes 12296 | tf_op jit(solution)/shard_map/ppermute | solution.py:479
  73.7 5.3 %collective-permute-start.10 = (bf16[320,128]{1,0:T(8,128)(2,1)S(1)}, bf16[320,128]{1,0:T(8,128)(2,1)S(1)}, u32[]{:S(2)}, u32[]{:S(2)}) collective-permute-start(bf16[320,128]{1,0:T(8,128)(2,1)S(1)} %get-tuple-element.42), channel_id=1, source_target_pairs={{0,8},{8,0},{16,24},{24,16},{32,40},{40,32},{48,56},{56,48},{64,72... | collective-permute-start | bytes 245768 | tf_op jit(solution)/shard_map/ppermute | solution.py:565
  73.7 5.7 %collective-permute-start.11 = (bf16[320,128]{1,0:T(8,128)(2,1)S(1)}, bf16[320,128]{1,0:T(8,128)(2,1)S(1)}, u32[]{:S(2)}, u32[]{:S(2)}) collective-permute-start(bf16[320,128]{1,0:T(8,128)(2,1)S(1)} %get-tuple-element.43), channel_id=1, source_target_pairs={{8,16},{24,32},{40,48},{72,80},{88,96},{104,112},{136,144},{152,16... | collective-permute-start | bytes 245768 | tf_op jit(solution)/shard_map/ppermute | solution.py:566
  76.4 7.8 %collective-permute-start.15 = (bf16[128,512]{1,0:T(8,128)(2,1)S(1)}, bf16[128,512]{1,0:T(8,128)(2,1)S(1)}, u32[]{:S(2)}, u32[]{:S(2)}) collective-permute-start(bf16[128,512]{1,0:T(8,128)(2,1)S(1)} %pad_maximum_fusion.1), channel_id=1, source_target_pairs={{0,4},{1,5},{2,6},{3,7},{4,0},{5,1},{6,2},{7,3},{8,12},{9,13},{10,... | collective-permute-start | bytes 393224 | tf_op jit(solution)/shard_map/ppermute | solution.py:475
  79.0 5.2 %copy-start.2 = (bf16[320,128]{1,0:T(8,128)(2,1)}, bf16[320,128]{1,0:T(8,128)(2,1)S(1)}, u32[]{:S(2)}) copy-start(bf16[320,128]{1,0:T(8,128)(2,1)S(1)} %collective-permute-done.10.side_1) | copy-start | bytes 245764
  79.5 4.8 %copy-start.4 = (bf16[320,128]{1,0:T(8,128)(2,1)}, bf16[320,128]{1,0:T(8,128)(2,1)S(1)}, u32[]{:S(2)}) copy-start(bf16[320,128]{1,0:T(8,128)(2,1)S(1)} %collective-permute-done.11.side_2) | copy-start | bytes 245764
  84.2 15.3 %copy-start.8 = (f32[8,128]{1,0:T(8,128)S(1)}, f32[8,128]{1,0:T(8,128)}, u32[]{:S(2)}) copy-start(f32[8,128]{1,0:T(8,128)} %add_add_fusion.weight) | copy-start | bytes 12292
  84.2 18.9 %copy-start.3 = (bf16[320,128]{1,0:T(8,128)(2,1)S(1)}, bf16[320,128]{1,0:T(8,128)(2,1)}, u32[]{:S(2)}) copy-start(bf16[320,128]{1,0:T(8,128)(2,1)} %copy-done.2) | copy-start | bytes 245764
  84.3 18.9 %copy-start.5 = (bf16[320,128]{1,0:T(8,128)(2,1)S(1)}, bf16[320,128]{1,0:T(8,128)(2,1)}, u32[]{:S(2)}) copy-start(bf16[320,128]{1,0:T(8,128)(2,1)} %copy-done.4) | copy-start | bytes 245764
  86.0 17.1 %copy-start.9 = (f32[8]{0:T(128)S(1)}, f32[8]{0:T(128)}, u32[]{:S(2)}) copy-start(f32[8]{0:T(128)} %param.14) | copy-start | bytes 100
  86.0 17.1 %collective-permute-start.19 = (bf16[256,512]{1,0:T(8,128)(2,1)S(1)}, bf16[256,512]{1,0:T(8,128)(2,1)S(1)}, u32[]{:S(2)}, u32[]{:S(2)}) collective-permute-start(bf16[256,512]{1,0:T(8,128)(2,1)S(1)} %pad_maximum_fusion.near), channel_id=1, source_target_pairs={{0,1},{1,0},{2,3},{3,2},{4,5},{5,4},{6,7},{7,6},{8,9},{9,8},{10,11... | collective-permute-start | bytes 786440 | tf_op jit(solution)/shard_map/ppermute | solution.py:475
  87.6 9.4 %collective-permute-start.16 = (bf16[80,512]{1,0:T(8,128)(2,1)}, bf16[80,512]{1,0:T(8,128)(2,1)S(1)}, u32[]{:S(2)}, u32[]{:S(2)}) collective-permute-start(bf16[80,512]{1,0:T(8,128)(2,1)} %row_rims.1), channel_id=1, source_target_pairs={{0,64},{8,72},{16,80},{24,88},{32,96},{40,104},{48,112},{56,120},{... | collective-permute-start | bytes 245768 | tf_op jit(solution)/shard_map/ppermute | solution.py:579
  97.1 6.1 %collective-permute-start.17 = (bf16[80,512]{1,0:T(8,128)(2,1)S(1)}, bf16[80,512]{1,0:T(8,128)(2,1)S(1)}, u32[]{:S(2)}, u32[]{:S(2)}) collective-permute-start(bf16[80,512]{1,0:T(8,128)(2,1)S(1)} %collective-permute-done.16.mine), channel_id=1, source_target_pairs={{0,2},{1,3},{2,0},{3,1},{4,6},{5,7},{6,4},{7,5},{8,10},{9,11},{10,... | collective-permute-start | bytes 245768 | tf_op jit(solution)/shard_map/ppermute | solution.py:475
  99.5 3.6 %collective-permute-start.18 = (f32[8,128]{1,0:T(8,128)S(1)}, f32[8,128]{1,0:T(8,128)S(1)}, u32[]{:S(2)}, u32[]{:S(2)}) collective-permute-start(f32[8,128]{1,0:T(8,128)S(1)} %copy-done.8), channel_id=1, source_target_pairs={{0,128},{8,136},{16,144},{24,152},{32,160},{40,168},{48,176},{56,1... | collective-permute-start | bytes 12296 | tf_op jit(solution)/shard_map/ppermute | solution.py:479
